TPU v7x, 512 devices: a whole 4x8x8 slice. The times are simulated.
512 devices in a mesh: gx: 16 (over x_lo, z), gy: 32 (over y, x_hi, core).
Axes of the slice: x: 4 (x_hi: 2, x_lo: 2; x = x_hi * 2 + x_lo), y: 8, z: 8, core: 2. Of those that a mesh axis runs over, the one named last changes fastest.
Arguments:
- fields: float32 [5, 16, 256, 4096], P(None, None, 'gx', 'gy'), may hold values from -6 to 6
- diffusivity: float32 [16, 256, 4096], P(None, 'gx', 'gy'), may hold values from 0.03 to 0.3
- heights: int32 [256, 4096], P('gx', 'gy'), may hold values from 0 to 8
- wrap_map: int32 [4096], replicated, may hold values from 0 to 4095, each once
Outputs:
- advanced: float32 [5, 16, 256, 4096], P(None, None, 'gx', 'gy')
Inputs may be any that keep to these rules, and one draw needn't show every extreme that they name: `wrap_map`: each spanwise column appears exactly once.
All inputs are finite; a program needn't handle non-finite values.
Results may differ from a plain program's by a relative error of at most 0.00002.
Values sent between devices are 32-bit elements; how exact they have to be, the bound alone decides.
No kernel may reach another device: no remote copies, remote signals or barrier semaphores. Data moves between devices by JAX's collectives and lax.ppermute only.
A program may use at most 64 MiB of HBM per device.

v0:
```python
import jax
import jax.numpy as jnp
from jax import lax
from jax.sharding import PartitionSpec as P

DRAG_COEF = 1.0
TIME_STEP = 0.3
BUOYANCY = 0.5
SPEED_EPS = 0.01


def with_halo(cells, sides, width):
    for axis, dim in sides:
        count = lax.axis_size(axis)
        head = lax.slice_in_dim(cells, 0, width, axis=dim)
        tail = lax.slice_in_dim(cells, cells.shape[dim] - width, cells.shape[dim], axis=dim)
        cells = jnp.concatenate(
            [
                lax.ppermute(tail, axis, [(i, (i + 1) % count) for i in range(count)]),
                cells,
                lax.ppermute(head, axis, [((i + 1) % count, i) for i in range(count)]),
            ],
            axis=dim,
        )
    return cells


def transport(extended, wind_parts, diff_ext):
    centre = extended[:, 1:-1, 1:-1]
    east_cell = extended[:, 2:, 1:-1]
    west_cell = extended[:, :-2, 1:-1]
    north_cell = extended[:, 1:-1, 2:]
    south_cell = extended[:, 1:-1, :-2]
    padded = jnp.pad(centre, ((1, 1), (0, 0), (0, 0)))
    upper_cell = padded[2:]
    lower_cell = padded[:-2]
    advect = 0.5 * (
        wind_parts[0] * (east_cell - west_cell)
        + wind_parts[1] * (north_cell - south_cell)
        + wind_parts[2] * (upper_cell - lower_cell)
    )
    diff_mid = diff_ext[:, 1:-1, 1:-1]
    diff_pad = jnp.pad(diff_mid, ((1, 1), (0, 0), (0, 0)), mode="edge")
    diffuse = 0.5 * (
        (diff_mid + diff_ext[:, 2:, 1:-1]) * (east_cell - centre)
        + (diff_mid + diff_ext[:, :-2, 1:-1]) * (west_cell - centre)
        + (diff_mid + diff_ext[:, 1:-1, 2:]) * (north_cell - centre)
        + (diff_mid + diff_ext[:, 1:-1, :-2]) * (south_cell - centre)
        + (diff_mid + diff_pad[2:]) * (upper_cell - centre)
        + (diff_mid + diff_pad[:-2]) * (lower_cell - centre)
    )
    return diffuse - advect


def tendency(extended, diff_ext, drag_ext):
    centre = extended[:, :, 1:-1, 1:-1]
    wind_parts = centre[:3]
    rates = jax.vmap(lambda column: transport(column, wind_parts, diff_ext))(extended)
    wind_speed = jnp.sqrt(
        centre[0] * centre[0] + centre[1] * centre[1] + centre[2] * centre[2] + SPEED_EPS
    )
    resist = drag_ext[:, 1:-1, 1:-1] * wind_speed
    vertical = rates[2] - resist * centre[2] + BUOYANCY * centre[3]
    return jnp.concatenate([rates[:2] - resist * centre[:2], vertical[None], rates[3:]], 0)


def pick_columns(whole, sources):
    lower_part = jnp.take(whole[0], sources[0], axis=3)
    upper_part = jnp.take(whole[1], sources[1], axis=3)
    return jnp.stack([lower_part, upper_part])


def fetch_gather(rim_pair, sources):
    gathered = lax.all_gather(rim_pair, "gy", axis=4, tiled=True)
    return pick_columns(gathered, sources)


def extend(values, rim_width, sources):
    extended = with_halo(values, (("gx", 2),), rim_width)
    lower_rim = extended[:, :, :rim_width, :]
    upper_rim = extended[:, :, -rim_width:, :]
    rim_pair = jnp.stack([lower_rim, upper_rim])
    fetched = fetch_gather(rim_pair, sources)
    tile_x = lax.axis_index("gx")
    new_lower = jnp.where(tile_x == 0, fetched[0], lower_rim)
    new_upper = jnp.where(tile_x == lax.axis_size("gx") - 1, fetched[1], upper_rim)
    extended = jnp.concatenate([new_lower, extended[:, :, rim_width:-rim_width, :], new_upper], 2)
    return with_halo(extended, (("gy", 3),), rim_width)


def shards(fields, diffusivity, heights, wrap_map):
    all_columns = jnp.arange(wrap_map.shape[0], dtype=jnp.int32)
    backward = jnp.zeros_like(wrap_map).at[wrap_map].set(all_columns)
    cells_y = fields.shape[3]
    own_columns = lax.axis_index("gy") * cells_y + jnp.arange(cells_y, dtype=jnp.int32)
    sources = jnp.stack([jnp.take(backward, own_columns), jnp.take(wrap_map, own_columns)])
    levels = lax.broadcasted_iota(jnp.int32, diffusivity.shape, 0)
    drag_coef = jnp.where(levels < heights[None], DRAG_COEF, 0.0).astype(diffusivity.dtype)
    joined = jnp.concatenate([fields, diffusivity[None]], 0)
    extended = extend(joined, 1, sources)
    drag_pad = jnp.pad(drag_coef, ((0, 0), (1, 1), (1, 1)))
    rates_one = tendency(extended[:5], extended[5], drag_pad)
    section_one = fields + TIME_STEP / 3.0 * rates_one
    again = extend(section_one, 1, sources)
    rates_two = tendency(again, extended[5], drag_pad)
    return fields + TIME_STEP / 2.0 * rates_two


def solution(mesh):
    in_specs = (P(None, None, "gx", "gy"), P(None, "gx", "gy"), P("gx", "gy"), P())
    out_specs = P(None, None, "gx", "gy")
    return jax.shard_map(shards, mesh=mesh, in_specs=in_specs, out_specs=out_specs, check_vma=False)
```

profile of v0, /device:TPU:1, one launch (start us, length us, event | category | flops | bytes accessed | tf_op | source)
XLA Modules:
  0.0 322.4 jit_solution(2679072502645191621)
XLA Ops:
  6.5 1.2 pad_maximum_fusion.28
  7.8 4.8 %collective-permute-start = (f32[6,16,1,128]{3,1,0,2:T(8,128)S(1)}, f32[6,16,1,128]{3,1,0,2:T(8,128)S(1)}, u32[]{:S(2)}, u32[]{:S(2)}) collective-permute-start(f32[6,16,1,128]{3,1,0,2:T(8,128)S(1)} %bitcast.74), channel_id=1, source_target_pairs={{0,32},{32,64},{64,96},{96,128},{128,160},{160,192},{192,224},{224... | collective-permute-start | bytes 147464 | tf_op jit(solution)/shard_map/ppermute | solution.py:19
  12.6 9.5 %collective-permute-start.1 = (f32[6,16,1,128]{3,2,1,0:T(1,128)S(1)}, f32[6,16,1,128]{3,2,1,0:T(1,128)S(1)}, u32[]{:S(2)}, u32[]{:S(2)}) collective-permute-start(f32[6,16,1,128]{3,2,1,0:T(1,128)S(1)} %get-tuple-element.24), channel_id=1, source_target_pairs={{32,0},{64,32},{96,64},{128,96},{160,128},{192,160},{224,192},{256... | collective-permute-start | bytes 147464 | tf_op jit(solution)/shard_map/ppermute | solution.py:21
  22.1 1.1 collective-permute-done.1
  23.3 0.6 pad_maximum_fusion.26
  24.1 1.1 gather_fusion.2
  25.2 15.5 %scatter_custom_fusion = s32[4096]{0:T(1024)S(1)} fusion(s32[4096]{0:T(1024)S(1)} %compare_select_fusion, s32[4096]{0:T(1024)S(1)} %iota.15, s32[]{:T(128)} %constant.39.clone.1), kind=kCustom, calls=%fused_computation.114 | custom fusion | bytes 16388 | tf_op jit(solution)/shard_map/scatter | solution.py:93
  40.8 1.1 gather_fusion
  42.0 69.7 %all-gather.3.cloned.1.call-done = f32[2,6,16,1,4096]{4,2,1,3,0:T(8,128)} async-done(((f32[2,6,16,1,128]{4,2,1,3,0:T(8,128)}), f32[2,6,16,1,4096]{4,2,1,3,0:T(8,128)}) %all-gather.3.cloned.1.call-update) | async-done | bytes 3145744 | tf_op jit(solution)/shard_map/all_gather | solution.py:74
  111.7 2.1 slice_bitcast_fusion
  113.8 8.8 %copy.351 = f32[6,16,4096]{1,0,2:T(8,128)} copy(f32[6,16,4096]{2,1,0:T(8,128)S(1)} %get-tuple-element.16) | data formatting | bytes 3145728 | tf_op jit(solution)/shard_map/jit(_take)/Arg_0.7 | solution.py:69
  122.6 6.4 %gather_fusion.3 = f32[128,6,16]{2,1,0:T(8,128)S(1)} fusion(f32[6,16,4096]{1,0,2:T(8,128)} %copy.351, s32[1024]{0:T(1024)S(1)} %pad_clamp_fusion), kind=kCustom, calls=%fused_computation.4.clone | custom fusion | bytes 98816 | tf_op jit(solution)/shard_map/jit(_take)/gather | solution.py:69
  129.0 0.2 copy.352
  129.2 8.8 %copy.349 = f32[6,16,4096]{1,0,2:T(8,128)} copy(f32[6,16,4096]{2,1,0:T(8,128)S(1)} %get-tuple-element.17) | data formatting | bytes 3145728 | tf_op jit(solution)/shard_map/jit(_take)/Arg_0.7 | solution.py:68
  138.0 6.5 %gather_fusion.1 = f32[128,6,16]{2,1,0:T(8,128)S(1)} fusion(f32[6,16,4096]{1,0,2:T(8,128)} %copy.349, s32[1024]{0:T(1024)S(1)} %pad_clamp_fusion.1), kind=kCustom, calls=%fused_computation.1.clone | custom fusion | bytes 98816 | tf_op jit(solution)/shard_map/jit(_take)/gather | solution.py:68
  144.5 0.2 copy.350
  144.7 0.2 pad_maximum_fusion
  144.9 1.4 fusion.44
  146.4 2.5 copy.354
  148.9 2.3 collective-permute-start.2
  151.2 1.3 copy.355
  152.5 2.0 collective-permute-start.3
  154.5 0.7 slice_bitcast_fusion.7
  155.2 0.2 copy.357
  155.4 1.5 copy.356
  156.9 2.8 collective-permute-done.3
  159.7 1.5 copy.358
  161.2 0.2 fusion.34
  161.4 0.2 slice_add_fusion.3
  161.6 0.1 fusion.47
  161.9 0.7 copy.359
  162.6 0.7 copy.360
  163.3 0.7 copy.362
  163.9 0.7 copy.364
  164.6 1.5 copy.363
  166.1 1.5 copy.365
  167.6 2.4 fusion.22
  170.0 0.1 fusion.37
  170.2 0.1 fusion.32
  170.4 3.3 %collective-permute-start.4 = (f32[5,16,1,128]{3,1,0,2:T(8,128)S(1)}, f32[5,16,1,128]{3,1,0,2:T(8,128)S(1)}, u32[]{:S(2)}, u32[]{:S(2)}) collective-permute-start(f32[5,16,1,128]{3,1,0,2:T(8,128)S(1)} %bitcast.75), channel_id=1, source_target_pairs={{0,32},{32,64},{64,96},{96,128},{128,160},{160,192},{192,224},{224... | collective-permute-start | bytes 122888 | tf_op jit(solution)/shard_map/ppermute | solution.py:19
  173.7 5.3 %collective-permute-start.5 = (f32[5,16,1,128]{3,2,1,0:T(1,128)S(1)}, f32[5,16,1,128]{3,2,1,0:T(1,128)S(1)}, u32[]{:S(2)}, u32[]{:S(2)}) collective-permute-start(f32[5,16,1,128]{3,2,1,0:T(1,128)S(1)} %get-tuple-element.31), channel_id=1, source_target_pairs={{32,0},{64,32},{96,64},{128,96},{160,128},{192,160},{224,192},{256... | collective-permute-start | bytes 122888 | tf_op jit(solution)/shard_map/ppermute | solution.py:21
  179.0 0.9 collective-permute-done.5
  179.9 0.6 pad_maximum_fusion.27
  180.5 84.2 %all-gather.5.cloned.1.call-done = f32[2,5,16,1,4096]{4,2,1,3,0:T(8,128)} async-done(((f32[2,5,16,1,128]{4,2,1,3,0:T(8,128)}), f32[2,5,16,1,4096]{4,2,1,3,0:T(8,128)}) %all-gather.5.cloned.1.call-update) | async-done | bytes 2621456 | tf_op jit(solution)/shard_map/all_gather | solution.py:74
  264.7 3.0 slice_bitcast_fusion.3
  267.7 9.5 %copy.369 = f32[5,16,4096]{1,0,2:T(8,128)} copy(f32[5,16,4096]{2,1,0:T(8,128)} %get-tuple-element.18) | data formatting | bytes 2621440 | tf_op jit(solution)/shard_map/jit(_take)/Arg_0.17 | solution.py:69
  277.2 6.4 %gather_fusion.4 = f32[128,5,16]{2,1,0:T(8,128)S(1)} fusion(f32[5,16,4096]{1,0,2:T(8,128)} %copy.369, s32[1024]{0:T(1024)S(1)} %pad_clamp_fusion), kind=kCustom, calls=%fused_computation.2.clone | custom fusion | bytes 82432 | tf_op jit(solution)/shard_map/jit(_take)/gather | solution.py:69
  283.6 0.1 copy.370
  283.8 8.8 %copy.371 = f32[5,16,4096]{1,0,2:T(8,128)} copy(f32[5,16,4096]{2,1,0:T(8,128)S(1)} %get-tuple-element.19) | data formatting | bytes 2621440 | tf_op jit(solution)/shard_map/jit(_take)/Arg_0.17 | solution.py:68
  292.6 6.4 %gather_fusion.5 = f32[128,5,16]{2,1,0:T(8,128)S(1)} fusion(f32[5,16,4096]{1,0,2:T(8,128)} %copy.371, s32[1024]{0:T(1024)S(1)} %pad_clamp_fusion.1), kind=kCustom, calls=%fused_computation.5.clone | custom fusion | bytes 82432 | tf_op jit(solution)/shard_map/jit(_take)/gather | solution.py:68
  299.0 0.1 copy.372
  299.3 0.6 copy-done.7
  299.9 0.2 pad_maximum_fusion.1
  300.0 0.3 fusion.45
  300.3 1.2 copy.375
  301.5 2.1 collective-permute-start.6
  303.7 0.6 copy.377
  304.3 5.0 %collective-permute-start.7 = (f32[5,16,18,1]{2,1,3,0:T(8,128)S(1)}, f32[5,16,18,1]{2,1,3,0:T(8,128)}, u32[]{:S(2)}, u32[]{:S(2)}) collective-permute-start(f32[5,16,18,1]{2,1,3,0:T(8,128)S(1)} %copy.377), channel_id=1, source_target_pairs={{0,1},{1,2},{2,3},{3,4},{4,5},{5,6},{6,7},{7,8},{8,9},{9,10},{10,1... | collective-permute-start | bytes 17288 | tf_op jit(solution)/shard_map/ppermute | solution.py:19
  309.3 0.7 slice_bitcast_fusion.5
  310.0 0.6 copy.376
  310.6 1.4 copy.378
  312.0 2.5 fusion.6
  314.5 0.1 fusion.36
  314.7 0.9 fusion.33
  (54 shorter events, 0.7 us)
Async XLA Ops:
  6.5 17.5 %copy-start.1 = (s32[4096]{0:T(1024)S(1)}, s32[4096]{0:T(1024)}, u32[]{:S(2)}) copy-start(s32[4096]{0:T(1024)} %param.13) | copy-start | bytes 49156
  6.5 105.2 %all-gather.3.cloned.1.call-start = ((), (), s32[]{:S(2)}) async-start(), calls=%async_computation | async-start | bytes 3244032 | tf_op jit(solution)/shard_map/all_gather | solution.py:74
  7.8 14.4 %collective-permute-start = (f32[6,16,1,128]{3,1,0,2:T(8,128)S(1)}, f32[6,16,1,128]{3,1,0,2:T(8,128)S(1)}, u32[]{:S(2)}, u32[]{:S(2)}) collective-permute-start(f32[6,16,1,128]{3,1,0,2:T(8,128)S(1)} %bitcast.74), channel_id=1, source_target_pairs={{0,32},{32,64},{64,96},{96,128},{128,160},{160,192},{192,224},{224... | collective-permute-start | bytes 147464 | tf_op jit(solution)/shard_map/ppermute | solution.py:19
  12.6 10.7 %collective-permute-start.1 = (f32[6,16,1,128]{3,2,1,0:T(1,128)S(1)}, f32[6,16,1,128]{3,2,1,0:T(1,128)S(1)}, u32[]{:S(2)}, u32[]{:S(2)}) collective-permute-start(f32[6,16,1,128]{3,2,1,0:T(1,128)S(1)} %get-tuple-element.24), channel_id=1, source_target_pairs={{32,0},{64,32},{96,64},{128,96},{160,128},{192,160},{224,192},{256... | collective-permute-start | bytes 147464 | tf_op jit(solution)/shard_map/ppermute | solution.py:21
  24.0 240.7 %all-gather.5.cloned.1.call-start = ((), (), s32[]{:S(2)}) async-start(), calls=%async_computation.1 | async-start | bytes 2703360 | tf_op jit(solution)/shard_map/all_gather | solution.py:74
  41.9 102.7 %copy-start.10 = (pred[128]{0:T(512)(128)(4,1)}, pred[128]{0:T(512)(128)(4,1)S(1)}, u32[]{:S(2)}) copy-start(pred[128]{0:T(512)(128)(4,1)S(1)} %get-tuple-element.12) | copy-start | bytes 388
  42.0 102.7 %copy-start.12 = (pred[128]{0:T(512)(128)(4,1)}, pred[128]{0:T(512)(128)(4,1)S(1)}, u32[]{:S(2)}) copy-start(pred[128]{0:T(512)(128)(4,1)S(1)} %get-tuple-element.14) | copy-start | bytes 388
  129.2 15.5 %copy-start.2 = (f32[16,16,128]{2,1,0:T(8,128)S(1)}, f32[16,16,128]{2,1,0:T(8,128)}, u32[]{:S(2)}) copy-start(f32[16,16,128]{2,1,0:T(8,128)} %param.11) | copy-start | bytes 393220
  138.0 6.8 %copy-start = (f32[5,16,16,128]{3,2,1,0:T(8,128)S(1)}, f32[5,16,16,128]{3,2,1,0:T(8,128)}, u32[]{:S(2)}) copy-start(f32[5,16,16,128]{3,2,1,0:T(8,128)} %param.10) | copy-start | bytes 1966084
  148.9 6.5 %collective-permute-start.2 = (f32[6,16,18,1]{2,1,3,0:T(8,128)}, f32[6,16,18,1]{2,1,3,0:T(8,128)}, u32[]{:S(2)}, u32[]{:S(2)}) collective-permute-start(f32[6,16,18,1]{2,1,3,0:T(8,128)} %copy.354), channel_id=1, source_target_pairs={{0,1},{1,2},{2,3},{3,4},{4,5},{5,6},{6,7},{7,8},{8,9},{9,10},{10,1... | collective-permute-start | bytes 20744 | tf_op jit(solution)/shard_map/ppermute | solution.py:19
  152.5 7.2 %collective-permute-start.3 = (f32[6,16,18,1]{2,1,3,0:T(8,128)}, f32[6,16,18,1]{2,1,3,0:T(8,128)}, u32[]{:S(2)}, u32[]{:S(2)}) collective-permute-start(f32[6,16,18,1]{2,1,3,0:T(8,128)} %copy.355), channel_id=1, source_target_pairs={{1,0},{2,1},{3,2},{4,3},{5,4},{6,5},{7,6},{8,7},{9,8},{10,9},{11,1... | collective-permute-start | bytes 20744 | tf_op jit(solution)/shard_map/ppermute | solution.py:21
  161.8 5.8 %copy-start.3 = (f32[16,16,128]{2,1,0:T(8,128)}, f32[16,16,128]{2,1,0:T(8,128)S(1)}, u32[]{:S(2)}) copy-start(f32[16,16,128]{2,1,0:T(8,128)S(1)} %copy.366) | copy-start | bytes 393220
  161.9 5.8 %copy-start.5 = (f32[16,16,128]{2,1,0:T(8,128)}, f32[16,16,128]{2,1,0:T(8,128)S(1)}, u32[]{:S(2)}) copy-start(f32[16,16,128]{2,1,0:T(8,128)S(1)} %copy.367) | copy-start | bytes 393220
  167.6 2.4 copy-start.9
  170.4 8.6 %collective-permute-start.4 = (f32[5,16,1,128]{3,1,0,2:T(8,128)S(1)}, f32[5,16,1,128]{3,1,0,2:T(8,128)S(1)}, u32[]{:S(2)}, u32[]{:S(2)}) collective-permute-start(f32[5,16,1,128]{3,1,0,2:T(8,128)S(1)} %bitcast.75), channel_id=1, source_target_pairs={{0,32},{32,64},{64,96},{96,128},{128,160},{160,192},{192,224},{224... | collective-permute-start | bytes 122888 | tf_op jit(solution)/shard_map/ppermute | solution.py:19
  173.7 6.2 %collective-permute-start.5 = (f32[5,16,1,128]{3,2,1,0:T(1,128)S(1)}, f32[5,16,1,128]{3,2,1,0:T(1,128)S(1)}, u32[]{:S(2)}, u32[]{:S(2)}) collective-permute-start(f32[5,16,1,128]{3,2,1,0:T(1,128)S(1)} %get-tuple-element.31), channel_id=1, source_target_pairs={{32,0},{64,32},{96,64},{128,96},{160,128},{192,160},{224,192},{256... | collective-permute-start | bytes 122888 | tf_op jit(solution)/shard_map/ppermute | solution.py:21
  283.8 15.3 %copy-start.11 = (pred[128]{0:T(512)(128)(4,1)S(1)}, pred[128]{0:T(512)(128)(4,1)}, u32[]{:S(2)}) copy-start(pred[128]{0:T(512)(128)(4,1)} %copy-done.10) | copy-start | bytes 388
  283.8 15.4 %copy-start.13 = (pred[128]{0:T(512)(128)(4,1)S(1)}, pred[128]{0:T(512)(128)(4,1)}, u32[]{:S(2)}) copy-start(pred[128]{0:T(512)(128)(4,1)} %copy-done.12) | copy-start | bytes 388
  299.2 0.6 copy-start.7
  299.2 0.6 copy-start.8
  301.5 8.5 %collective-permute-start.6 = (f32[5,16,18,1]{2,1,3,0:T(8,128)}, f32[5,16,18,1]{2,1,3,0:T(8,128)S(1)}, u32[]{:S(2)}, u32[]{:S(2)}) collective-permute-start(f32[5,16,18,1]{2,1,3,0:T(8,128)} %copy.375), channel_id=1, source_target_pairs={{1,0},{2,1},{3,2},{4,3},{5,4},{6,5},{7,6},{8,7},{9,8},{10,9},{11,1... | collective-permute-start | bytes 17288 | tf_op jit(solution)/shard_map/ppermute | solution.py:21
  304.3 7.8 %copy-start.4 = (f32[16,16,128]{2,1,0:T(8,128)S(1)}, f32[16,16,128]{2,1,0:T(8,128)}, u32[]{:S(2)}) copy-start(f32[16,16,128]{2,1,0:T(8,128)} %copy-done.3) | copy-start | bytes 393220
  304.3 7.8 %copy-start.6 = (f32[16,16,128]{2,1,0:T(8,128)S(1)}, f32[16,16,128]{2,1,0:T(8,128)}, u32[]{:S(2)}) copy-start(f32[16,16,128]{2,1,0:T(8,128)} %copy-done.5) | copy-start | bytes 393220
  304.3 6.4 %collective-permute-start.7 = (f32[5,16,18,1]{2,1,3,0:T(8,128)S(1)}, f32[5,16,18,1]{2,1,3,0:T(8,128)}, u32[]{:S(2)}, u32[]{:S(2)}) collective-permute-start(f32[5,16,18,1]{2,1,3,0:T(8,128)S(1)} %copy.377), channel_id=1, source_target_pairs={{0,1},{1,2},{2,3},{3,4},{4,5},{5,6},{6,7},{7,8},{8,9},{9,10},{10,1... | collective-permute-start | bytes 17288 | tf_op jit(solution)/shard_map/ppermute | solution.py:19
Sparse Core Ops, SparseCore 0:
  24.1 87.6 all-gather.2
  180.7 83.9 all-gather.4
where the time goes:
time: 327 us; the launch traced here: 322 us
  waiting for transfers between devices  159 us (49%)
  local copies, waits for them, and re-layouts  106 us (32%)
  starting transfers between devices  34.5 us (11%)
  between operations  13.9 us (4%)
  other arithmetic  9.68 us (3%)
    all_gather x2, waiting for transfers between devices, fetch_gather(): gathered = lax.all_gather(rim_pair, 'gy', axis=4, tiled=True)  154 us
    another operation x4, local copies, waits for them, and re-layouts, pick_columns(): upper_part = jnp.take(whole[1], sources[1], axis=3)  23.4 us
    ppermute x4, starting transfers between devices, with_halo(): lax.ppermute(head, axis, [((i + 1) % count, i) for i in range(count)])  19 us
    another operation x2, local copies, waits for them, and re-layouts, pick_columns(): lower_part = jnp.take(whole[0], sources[0], axis=3)  17.6 us
    scatter x1, local copies, waits for them, and re-layouts, shards(): backward = jnp.zeros_like(wrap_map).at[wrap_map].set(all_columns)  15.5 us
    ppermute x4, starting transfers between devices, with_halo(): lax.ppermute(tail, axis, [(i, (i + 1) % count) for i in range(count)])  15.4 us
    gather x4, local copies, waits for them, and re-layouts, pick_columns(): lower_part = jnp.take(whole[0], sources[0], axis=3)  13.2 us
    gather x4, local copies, waits for them, and re-layouts, pick_columns(): upper_part = jnp.take(whole[1], sources[1], axis=3)  13.1 us
  transfers between devices with their start and end apart: 10, of which 5 were waited for; matrix products, arithmetic and copies ran while one was open for 7% of the time, Pallas kernels for 0%

commit v1 on v0

v1 whole, which is shorter than its diff:
```python
import functools

import jax
import jax.numpy as jnp
from jax import lax
from jax.experimental import pallas as pl
from jax.experimental.pallas import tpu as pltpu
from jax.sharding import PartitionSpec as P

DRAG_COEF = 1.0
TIME_STEP = 0.3
BUOYANCY = 0.5
SPEED_EPS = 0.01

NF = 5
NA = 6
NZ = 16
NI = 16
NJ = 128
RIM = NA * NZ
EDGE_ROWS = 2 * RIM + 8
BLOCK = NA * NZ * NI
PACK = BLOCK + 2 * RIM + 64
HEIGHT_AT = BLOCK + 2 * RIM

VMEM = pl.BlockSpec(memory_space=pltpu.VMEM)
EXACT = lax.Precision.HIGHEST


def iota(shape, dim):
    return lax.broadcasted_iota(jnp.int32, shape, dim)


def call(kernel, outs, *args, scratch=(), name=None):
    return pl.pallas_call(
        kernel,
        out_shape=outs,
        in_specs=[VMEM] * len(args),
        out_specs=jax.tree.map(lambda _: VMEM, outs),
        scratch_shapes=list(scratch),
        compiler_params=pltpu.CompilerParams(vmem_limit_bytes=40 * 1024 * 1024),
        name=name,
    )(*args)


def f32(*shape):
    return jax.ShapeDtypeStruct(shape, jnp.float32)


def edges_kernel(fields, diff, heights, east, west):
    for out, near, far in ((east, NI - 1, NI - 2), (west, 0, 1)):
        for a in range(NA):
            src = diff if a == NF else fields.at[a]
            out[a * NZ:(a + 1) * NZ, :] = src[:, near, :]
            out[RIM + a * NZ:RIM + (a + 1) * NZ, :] = src[:, far, :]
        row = heights[near:near + 1, :].astype(jnp.float32)
        out[2 * RIM:EDGE_ROWS, :] = jnp.broadcast_to(row, (8, NJ))


def picks():
    row, lane = iota((8, NJ), 0), iota((8, NJ), 1)
    want = jnp.where(row < 2, row, jnp.where(row < 4, NJ - 4 + row, -1))
    return jnp.where(lane == want, 1.0, 0.0).astype(jnp.float32)


def pack_kernel(fields, diff, heights, west, east, to_a, to_b):
    even = lax.rem(lax.axis_index("gy"), 2) == 0
    rows = jnp.concatenate(
        [
            fields[...].reshape(NF * NZ * NI, NJ),
            diff[...].reshape(NZ * NI, NJ),
            west[0:RIM, :],
            east[0:RIM, :],
            heights[...].astype(jnp.float32),
            jnp.zeros((PACK - HEIGHT_AT - NI, NJ), jnp.float32),
        ],
        0,
    )
    cols = lax.dot_general(
        picks(), rows, (((1,), (1,)), ((), ())), precision=EXACT, preferred_element_type=jnp.float32
    )
    low, high = cols[0:2, :], cols[2:4, :]
    to_a[...] = jnp.where(even, high, low)
    to_b[...] = jnp.where(even, low, high)


def levels(x, edge):
    k = iota(x.shape, 0)
    above = jnp.where(k == NZ - 1, x if edge else 0.0, pltpu.roll(x, NZ - 1, 0))
    below = jnp.where(k == 0, x if edge else 0.0, pltpu.roll(x, 1, 0))
    return above, below


def row_rates(near, far, height, sign):
    u, v, w = near[0], near[1], near[2]
    k_cell = near[NF]
    k_above, k_below = levels(k_cell, True)
    drag = jnp.where(iota(u.shape, 0).astype(jnp.float32) < height, DRAG_COEF, 0.0)
    resist = drag * jnp.sqrt(u * u + v * v + w * w + SPEED_EPS)
    rates = []
    for m in range(NF):
        f = near[m]
        above, below = levels(f, False)
        rate = 0.5 * (
            (k_cell + far[NF]) * (far[m] - f)
            + (k_cell + k_above) * (above - f)
            + (k_cell + k_below) * (below - f)
            + sign * u * far[m]
            - w * (above - below)
        )
        if m < 3:
            rate = rate - resist * f
        if m == 2:
            rate = rate + BUOYANCY * near[3]
        rates.append(rate)
    return rates


def split_rim(rim):
    near = [rim[a * NZ:(a + 1) * NZ, :] for a in range(NA)]
    far = [rim[RIM + a * NZ:RIM + (a + 1) * NZ, :] for a in range(NA)]
    return near, far, rim[2 * RIM:2 * RIM + 1, :]


def packet_kernel(west, east, out):
    first = lax.axis_index("gx") == 0
    rim = jnp.where(first, west[...], east[...])
    sign = jnp.where(first, 1.0, -1.0).astype(jnp.float32)
    near, far, height = split_rim(rim)
    rates = row_rates(near, far, height, sign)
    zero = jnp.zeros((NZ, NJ), jnp.float32)
    lower = [near[0], near[1], near[2], near[NF], rates[0], rates[1], rates[2], zero]
    upper = [near[3], near[4], near[1], near[NF], rates[3], rates[4], zero, zero]
    for row in range(8):
        out[0:NZ, row, :] = lower[row]
        out[NZ:2 * NZ, row, :] = upper[row]


def inverse_kernel(wrap, out):
    total = jnp.zeros((64, NJ), jnp.float32)
    lane = iota((32, NJ), 1).astype(jnp.float32)
    for s in range(32):
        p = wrap[s:s + 1, :]
        hit = jnp.where(iota((32, NJ), 0) == p // NJ, 1.0, 0.0)
        low = jnp.where(iota((NJ, NJ), 0) == lax.rem(p, NJ), 1.0, 0.0).astype(jnp.bfloat16)
        left = jnp.concatenate([hit * lane, hit * float(s)], 0).astype(jnp.bfloat16)
        total = total + lax.dot_general(
            left, low, (((1,), (1,)), ((), ())), preferred_element_type=jnp.float32
        )
    out[...] = (total[0:32, :] + NJ * total[32:64, :]).astype(jnp.int32)


def permute_kernel(rows, wrap, inverse, out, index, held):
    first = lax.axis_index("gx") == 0
    index[...] = jnp.where(first, inverse[...], wrap[...])
    upper = lax.axis_index("gy") >= NZ
    x = rows[...]
    lane, sub = iota(x.shape, 2), iota(x.shape, 1)

    def after(y):
        return jnp.concatenate([y[1:], y[:1]], 0)

    def before(y):
        return jnp.concatenate([y[-1:], y[:-1]], 0)

    left, right = pltpu.roll(x, NJ - 1, 2), pltpu.roll(x, 1, 2)
    north = jnp.where(lane == NJ - 1, after(left), left)
    south = jnp.where(lane == 0, before(right), right)
    v = jnp.where(upper, x[:, 2:3, :], x[:, 1:2, :])
    k_cell, k_north, k_south = x[:, 3:4, :], north[:, 3:4, :], south[:, 3:4, :]
    term = 0.5 * (
        (k_cell + k_north) * (north - x) + (k_cell + k_south) * (south - x) - v * (north - south)
    )
    held[...] = x + jnp.where((sub >= 4) & (sub < 7), pltpu.roll(term, 4, 1), 0.0)

    def target(t, _):
        idx = jnp.broadcast_to(index[pl.ds(t, 1), :], (8, NJ))
        hi, lo = lax.shift_right_logical(idx, 7), lax.bitwise_and(idx, NJ - 1)
        acc = jnp.zeros((8, NJ), jnp.float32)
        for s in range(32):
            got = jnp.take_along_axis(held[s], lo, axis=1, mode="promise_in_bounds")
            acc = jnp.where(hi == s, got, acc)
        out[t] = acc
        return 0

    lax.fori_loop(0, 32, target, 0)
    y = out[...]
    prior, later = before(y), after(y)
    last = jnp.zeros_like(y)
    for r in range(4):
        corner = jnp.where(lane < 64, pltpu.roll(later, r, 2), pltpu.roll(prior, (NJ - r) % NJ, 2))
        corner = pltpu.roll(corner, 7 - r, 1)
        last = jnp.where((lane == r) | (lane == NJ - 1 - r), corner, last)
    out[...] = jnp.where(sub == 7, last, y)


def final_kernel(
    fields, diff, heights, west, east, from_a, from_b, wrapped, out,
    halo, one, one_halo, rim_w, rim_e, corner_w, corner_e, one_w, one_e,
):
    gx = lax.axis_index("gx")
    first, final = gx == 0, gx == lax.axis_size("gx") - 1
    even = lax.rem(lax.axis_index("gy"), 2) == 0
    a, b = from_a[...], from_b[...]
    north, south = jnp.where(even, a, b), jnp.where(even, b, a)
    cols = jnp.concatenate([north, south, jnp.zeros((4, PACK), jnp.float32)], 0)
    halo[...] = lax.dot_general(
        cols, picks(), (((0,), (0,)), ((), ())), precision=EXACT, preferred_element_type=jnp.float32
    )

    lane, sub = iota((NI, NJ), 1), iota((NI, NJ), 0)
    place = {0: (0, 0), 1: (0, 1), 2: (0, 2), NF: (0, 3), 3: (NZ, 0), 4: (NZ, 1)}

    def beside(m, h):
        m_left, h_left = pltpu.roll(m, NJ - 1, 1), pltpu.roll(h, NJ - 1, 1)
        m_right, h_right = pltpu.roll(m, 1, 1), pltpu.roll(h, 1, 1)
        at_end, at_start = lane == NJ - 1, lane == 0
        return (
            jnp.where(at_end, h_left, m_left),
            jnp.where(at_start, h_right, m_right),
            jnp.where(at_end, m_left, h_left),
            jnp.where(at_start, m_right, h_right),
        )

    for rim, mine, sign, own_row, rim_out, corner_at, corner_out, one_out in (
        (west, first, 1.0, 0, rim_w, BLOCK, corner_w, one_w),
        (east, final, -1.0, NI - 1, rim_e, BLOCK + RIM, corner_e, one_e),
    ):
        near, far, height = split_rim(rim[...])
        rates = row_rates(near, far, height, sign)
        corners = [halo[corner_at + i * NZ:corner_at + (i + 1) * NZ, :] for i in range(NA)]
        sides = [beside(near[i], corners[i]) for i in range(NA)]
        k_cell, k_n, k_s = near[NF], sides[NF][0], sides[NF][1]
        for m in range(NF):
            f, n, s = near[m], sides[m][0], sides[m][1]
            rates[m] = rates[m] + 0.5 * (
                (k_cell + k_n) * (n - f) + (k_cell + k_s) * (s - f) - near[1] * (n - s)
            )
            half, row = (0, 4 + m) if m < 3 else (NZ, 1 + m)
            rates[m] = jnp.where(mine, wrapped[half:half + NZ, row, :], rates[m])
        for i in range(NA):
            half, row = place[i]
            near[i] = jnp.where(mine, wrapped[half:half + NZ, row, :], near[i])
            spare = wrapped[half:half + NZ, 7, :]
            spare = jnp.where(lane < 64, pltpu.roll(spare, (NJ - row) % NJ, 1), pltpu.roll(spare, row, 1))
            rim_out[i * NZ:(i + 1) * NZ, :] = near[i]
            corner_out[i * NZ:(i + 1) * NZ, :] = jnp.where(mine, spare, corners[i])
        k_own = diff[:, own_row, :]
        for m in range(NF):
            own = fields[m, :, own_row, :]
            rate = rates[m] + 0.5 * ((near[NF] + k_own) * (own - near[m]) - sign * near[0] * own)
            one_out[m * NZ:(m + 1) * NZ, :] = near[m] + TIME_STEP / 3.0 * rate

    def row_of(ref, i, k):
        return ref[pl.ds(i * NZ + k, 1), :]

    def along(x, low, high):
        return (
            jnp.where(sub == NI - 1, high, pltpu.roll(x, NI - 1, 0)),
            jnp.where(sub == 0, low, pltpu.roll(x, 1, 0)),
        )

    def halo_tile(i, k):
        at = pl.multiple_of((i * NZ + k) * NI, NI)
        return halo[pl.ds(at, NI), :]

    def rates_of(cells, k_cell, k_sides, drag):
        u, v, w = cells[0][0], cells[1][0], cells[2][0]
        resist = drag * jnp.sqrt(u * u + v * v + w * w + SPEED_EPS)
        sums = [k_cell + side for side in k_sides]
        total = sums[0] + sums[1] + sums[2] + sums[3] + sums[4] + sums[5]
        rates = []
        for m in range(NF):
            f, e, ws, n, s, up, dn = cells[m]
            rate = 0.5 * (
                (sums[0] - u) * e + (sums[1] + u) * ws
                + (sums[2] - v) * n + (sums[3] + v) * s
                + (sums[4] - w) * up + (sums[5] + w) * dn
                - total * f
            )
            if m < 3:
                rate = rate - resist * f
            if m == 2:
                rate = rate + BUOYANCY * cells[3][0]
            rates.append(rate)
        return rates

    high_main = heights[...].astype(jnp.float32)
    high_halo = halo[HEIGHT_AT:HEIGHT_AT + NI, :]

    def section_one(k, _):
        up, dn = jnp.minimum(k + 1, NZ - 1), jnp.maximum(k - 1, 0)
        has_up = jnp.where(k < NZ - 1, 1.0, 0.0).astype(jnp.float32)
        has_dn = jnp.where(k > 0, 1.0, 0.0).astype(jnp.float32)
        level = k.astype(jnp.float32)
        k_main, k_halo = diff[k], halo_tile(NF, k)
        n, s, hn, hs = beside(k_main, k_halo)
        e, ws = along(k_main, row_of(rim_w, NF, k), row_of(rim_e, NF, k))
        he, hw = along(k_halo, row_of(corner_w, NF, k), row_of(corner_e, NF, k))
        k_sides = (e, ws, n, s, diff[up], diff[dn])
        kh_sides = (he, hw, hn, hs, halo_tile(NF, up), halo_tile(NF, dn))
        cells, halos = [], []
        for m in range(NF):
            f, h = fields[m, k], halo_tile(m, k)
            n, s, hn, hs = beside(f, h)
            e, ws = along(f, row_of(rim_w, m, k), row_of(rim_e, m, k))
            he, hw = along(h, row_of(corner_w, m, k), row_of(corner_e, m, k))
            cells.append((f, e, ws, n, s, has_up * fields[m, up], has_dn * fields[m, dn]))
            halos.append((h, he, hw, hn, hs, has_up * halo_tile(m, up), has_dn * halo_tile(m, dn)))
        drag = jnp.where(level < high_main, DRAG_COEF, 0.0)
        drag_h = jnp.where(level < high_halo, DRAG_COEF, 0.0)
        rates = rates_of(cells, k_main, k_sides, drag)
        rates_h = rates_of(halos, k_halo, kh_sides, drag_h)
        for m in range(NF):
            one[m, k] = cells[m][0] + TIME_STEP / 3.0 * rates[m]
            one_halo[m, k] = halos[m][0] + TIME_STEP / 3.0 * rates_h[m]
        return 0

    lax.fori_loop(0, NZ, section_one, 0)

    def section_two(k, _):
        up, dn = jnp.minimum(k + 1, NZ - 1), jnp.maximum(k - 1, 0)
        has_up = jnp.where(k < NZ - 1, 1.0, 0.0).astype(jnp.float32)
        has_dn = jnp.where(k > 0, 1.0, 0.0).astype(jnp.float32)
        k_main = diff[k]
        n, s, _, _ = beside(k_main, halo_tile(NF, k))
        e, ws = along(k_main, row_of(rim_w, NF, k), row_of(rim_e, NF, k))
        k_sides = (e, ws, n, s, diff[up], diff[dn])
        cells = []
        for m in range(NF):
            f = one[m, k]
            n, s, _, _ = beside(f, one_halo[m, k])
            e, ws = along(f, row_of(one_w, m, k), row_of(one_e, m, k))
            cells.append((f, e, ws, n, s, has_up * one[m, up], has_dn * one[m, dn]))
        drag = jnp.where(k.astype(jnp.float32) < high_main, DRAG_COEF, 0.0)
        rates = rates_of(cells, k_main, k_sides, drag)
        for m in range(NF):
            out[m, k] = fields[m, k] + TIME_STEP / 2.0 * rates[m]
        return 0

    lax.fori_loop(0, NZ, section_two, 0)


def shards(fields, diffusivity, heights, wrap_map):
    count_x, count_y = lax.axis_size("gx"), lax.axis_size("gy")
    edge = f32(EDGE_ROWS, NJ)
    to_east, to_west = call(edges_kernel, (edge, edge), fields, diffusivity, heights, name="edges")
    east_pairs = [(i, (i + 1) % count_x) for i in range(count_x)]
    west = lax.ppermute(to_east, "gx", east_pairs)
    east = lax.ppermute(to_west, "gx", [(j, i) for i, j in east_pairs])

    wrap = wrap_map.reshape(count_y, NJ)
    inverse = call(
        inverse_kernel, jax.ShapeDtypeStruct((count_y, NJ), jnp.int32), wrap, name="inverse"
    )

    packets = call(packet_kernel, f32(count_y, 8, NJ), west, east, name="packets")
    pack = f32(2, PACK)
    to_a, to_b = call(pack_kernel, (pack, pack), fields, diffusivity, heights, west, east, name="pack")
    low_pairs = [(i, i + 1) for i in range(0, count_y, 2)]
    high_pairs = [(i, (i + 1) % count_y) for i in range(1, count_y, 2)]
    from_a = lax.ppermute(to_a, "gy", low_pairs + [(j, i) for i, j in low_pairs])
    from_b = lax.ppermute(to_b, "gy", high_pairs + [(j, i) for i, j in high_pairs])

    rows = lax.all_to_all(packets, "gy", 0, 0)
    moved = call(
        permute_kernel, f32(count_y, 8, NJ), rows, wrap, inverse, name="permute",
        scratch=[pltpu.VMEM((32, NJ), jnp.int32), pltpu.VMEM((32, 8, NJ), jnp.float32)],
    )
    wrapped = lax.all_to_all(moved, "gy", 0, 0)

    state = pltpu.VMEM((NF, NZ, NI, NJ), jnp.float32)
    rim = pltpu.VMEM((RIM, NJ), jnp.float32)
    return call(
        final_kernel, f32(NF, NZ, NI, NJ),
        fields, diffusivity, heights, west, east, from_a, from_b, wrapped, name="sections",
        scratch=[pltpu.VMEM((PACK, NJ), jnp.float32), state, state, rim, rim, rim, rim, rim, rim],
    )


def solution(mesh):
    in_specs = (P(None, None, "gx", "gy"), P(None, "gx", "gy"), P("gx", "gy"), P())
    out_specs = P(None, None, "gx", "gy")
    return jax.shard_map(shards, mesh=mesh, in_specs=in_specs, out_specs=out_specs, check_vma=False)
```

time: 327 us -> 67.5 us (0.21); the launches traced: 322 us -> 67.1 us
  waiting for transfers between devices: 159 us -> 14.5 us
  local copies, waits for them, and re-layouts: 106 us -> 2.7 us
  between operations: 13.9 us -> 0.12 us
  Pallas kernels: 0 us -> 13.3 us
  other arithmetic: 9.68 us -> 0 us
    all_gather x2 -> x0, waiting for transfers between devices: 154 us -> none  [fetch_gather(): gathered = lax.all_gather(rim_pair, 'gy', axis=4, tiled=True)]
    another operation x6 -> x0, local copies, waits for them, and re-layouts: 41 us -> none  [the longest x4 23.4 us: pick_columns(): upper_part = jnp.take(whole[1], sources[1], axis=3)]
    gather x10 -> x0, local copies, waits for them, and re-layouts: 28.6 us -> none  [the longest x4 13.2 us: pick_columns(): lower_part = jnp.take(whole[0], sources[0], axis=3)]
    scatter x1 -> x0, local copies, waits for them, and re-layouts: 15.5 us -> none  [shards(): backward = jnp.zeros_like(wrap_map).at[wrap_map].set(all_columns)]
    all_to_all x0 -> x2, starting transfers between devices: none -> 14.8 us  [the longest x1 11 us: shards(): rows = lax.all_to_all(packets, 'gy', 0, 0)]
    pallas_call x0 -> x6, Pallas kernels: none -> 13.3 us  [call(): pl.pallas_call(kernel, out_shape=outs, in_specs=[VMEM] * len(args), out_s...]
    ppermute x8 -> x4, starting transfers between devices: 34.4 us -> 21.6 us  [the longest x1 9.52 us: shards(): east = lax.ppermute(to_west, 'gx', [(j, i) for i, j in east_pairs])]
    all_to_all x0 -> x2, waiting for transfers between devices: none -> 10.8 us  [the longest x1 9.95 us: shards(): rows = lax.all_to_all(packets, 'gy', 0, 0)]
  transfers between devices with their start and end apart: 10 -> 6, of which waited for: 5 -> 5; matrix products, arithmetic and copies ran while one was open for 7% -> 0% of each run, Pallas kernels for 0% -> 3%
where the time goes in v1:
time: 67.5 us; the launch traced here: 67.1 us
  starting transfers between devices  36.4 us (54%)
  waiting for transfers between devices  14.5 us (21%)
  Pallas kernels  13.3 us (20%)
  local copies, waits for them, and re-layouts  2.7 us (4%)
    pallas_call x6, Pallas kernels, call(): pl.pallas_call(kernel, out_shape=outs, in_specs=[VMEM] * len(args), out_s...  13.3 us
    all_to_all x1, starting transfers between devices, shards(): rows = lax.all_to_all(packets, 'gy', 0, 0)  11 us
    all_to_all x1, waiting for transfers between devices, shards(): rows = lax.all_to_all(packets, 'gy', 0, 0)  9.95 us
    ppermute x1, starting transfers between devices, shards(): east = lax.ppermute(to_west, 'gx', [(j, i) for i, j in east_pairs])  9.52 us
    ppermute x1, starting transfers between devices, shards(): west = lax.ppermute(to_east, 'gx', east_pairs)  4.96 us
    ppermute x1, starting transfers between devices, shards(): lax.ppermute(to_b, 'gy', high_pairs + [(j, i) for i, j in high_pairs])  4.85 us
    all_to_all x1, starting transfers between devices, shards(): wrapped = lax.all_to_all(moved, 'gy', 0, 0)  3.87 us
    unnamed x14, local copies, waits for them, and re-layouts  2.7 us
  transfers between devices with their start and end apart: 6, of which 5 were waited for; matrix products, arithmetic and copies ran while one was open for 0% of the time, Pallas kernels for 3%

profile of v1, /device:TPU:1, one launch (start us, length us, event | category | flops | bytes accessed | tf_op | source)
XLA Modules:
  0.0 67.1 jit_solution(11237214746176969296)
XLA Ops:
  0.0 0.0 copy-start
  0.0 1.1 %copy-done = f32[5,16,16,128]{3,2,1,0:T(8,128)S(1)} copy-done((f32[5,16,16,128]{3,2,1,0:T(8,128)S(1)}, f32[5,16,16,128]{3,2,1,0:T(8,128)}, u32[]{:S(2)}) %copy-start) | copy-done | bytes 655384
  1.1 0.0 copy-start.2
  1.1 0.9 %copy-done.2 = f32[16,16,128]{2,1,0:T(8,128)S(1)} copy-done((f32[16,16,128]{2,1,0:T(8,128)S(1)}, f32[16,16,128]{2,1,0:T(8,128)}, u32[]{:S(2)}) %copy-start.2) | copy-done | bytes 131096
  2.0 0.0 copy-start.4
  2.0 0.7 %copy-done.4 = s32[16,128]{1,0:T(8,128)S(1)} copy-done((s32[16,128]{1,0:T(8,128)S(1)}, s32[16,128]{1,0:T(8,128)}, u32[]{:S(2)}) %copy-start.4) | copy-done | bytes 8216
  2.7 0.0 copy-start.6
  2.7 0.1 edges.1
  2.8 0.0 copy-start.1
  2.8 5.0 %collective-permute-start = (f32[200,128]{1,0:T(8,128)S(1)}, f32[200,128]{1,0:T(8,128)S(1)}, u32[]{:S(2)}, u32[]{:S(2)}) collective-permute-start(f32[200,128]{1,0:T(8,128)S(1)} %get-tuple-element.9), channel_id=1, source_target_pairs={{0,32},{32,64},{64,96},{96,128},{128,160},{160,192},{192,224},{224... | collective-permute-start | bytes 307208 | tf_op jit(solution)/shard_map/ppermute | solution.py:349
  7.8 9.5 %collective-permute-start.1 = (f32[200,128]{1,0:T(8,128)S(1)}, f32[200,128]{1,0:T(8,128)S(1)}, u32[]{:S(2)}, u32[]{:S(2)}) collective-permute-start(f32[200,128]{1,0:T(8,128)S(1)} %get-tuple-element.10), channel_id=1, source_target_pairs={{32,0},{64,32},{96,64},{128,96},{160,128},{192,160},{224,192},{256... | collective-permute-start | bytes 307208 | tf_op jit(solution)/shard_map/ppermute | solution.py:350
  17.3 0.7 collective-permute-done.west
  18.0 1.0 %collective-permute-done.1.east = f32[200,128]{1,0:T(8,128)S(1)} collective-permute-done((f32[200,128]{1,0:T(8,128)S(1)}, f32[200,128]{1,0:T(8,128)S(1)}, u32[]{:S(2)}, u32[]{:S(2)}) %collective-permute-start.1) | collective-permute-done | bytes 102432 | tf_op jit(solution)/shard_map/ppermute | solution.py:350
  19.0 0.8 %packets.1 = f32[32,8,128]{2,1,0:T(8,128)} custom-call(f32[200,128]{1,0:T(8,128)S(1)} %collective-permute-done.west, f32[200,128]{1,0:T(8,128)S(1)} %collective-permute-done.1.east), custom_call_target="tpu_custom_call" | custom-call | tf_op jit(solution)/shard_map/packets/pallas_call | solution.py:35
  19.7 11.0 %all-to-all-start = ((f32[32,8,128]{2,1,0:T(8,128)}), f32[32,8,128]{2,1,0:T(8,128)S(1)}, u32[]{:S(2)}, u32[]{:S(2)}) async-start(f32[32,8,128]{2,1,0:T(8,128)} %packets.1), calls=%async_computation | async-start | bytes 262144 | tf_op jit(solution)/shard_map/all_to_all | solution.py:365
  30.7 0.0 copy-done.6
  30.7 0.8 %inverse.1 = s32[32,128]{1,0:T(8,128)S(1)} custom-call(s32[32,128]{1,0:T(8,128)S(1)} %bitcast.1), custom_call_target="tpu_custom_call" | custom-call | tf_op jit(solution)/shard_map/inverse/pallas_call | solution.py:35
  31.5 9.9 %all-to-all-done.rows = f32[32,8,128]{2,1,0:T(8,128)S(1)} async-done(((f32[32,8,128]{2,1,0:T(8,128)}), f32[32,8,128]{2,1,0:T(8,128)S(1)}, u32[]{:S(2)}, u32[]{:S(2)}) %all-to-all-start) | async-done | bytes 131104 | tf_op jit(solution)/shard_map/all_to_all | solution.py:365
  41.5 4.5 %permute.1 = f32[32,8,128]{2,1,0:T(8,128)} custom-call(f32[32,8,128]{2,1,0:T(8,128)S(1)} %all-to-all-done.rows, s32[32,128]{1,0:T(8,128)S(1)} %bitcast.2, s32[32,128]{1,0:T(8,128)S(1)} %inverse.1), custom_call_target="tpu_custom_call" | custom-call | tf_op jit(solution)/shard_map/permute/pallas_call | solution.py:35
  46.0 0.0 copy-start.3
  46.0 0.0 copy-start.5
  46.0 3.9 %all-to-all-start.1 = ((f32[32,8,128]{2,1,0:T(8,128)}), f32[32,8,128]{2,1,0:T(8,128)S(1)}, u32[]{:S(2)}, u32[]{:S(2)}) async-start(f32[32,8,128]{2,1,0:T(8,128)} %permute.1), calls=%async_computation.1 | async-start | bytes 262144 | tf_op jit(solution)/shard_map/all_to_all | solution.py:370
  49.9 0.0 copy-done.1
  49.9 0.0 copy-done.3
  49.9 0.0 copy-done.5
  49.9 0.9 %pack.1 = (f32[2,1792]{1,0:T(2,128)S(1)}, f32[2,1792]{1,0:T(2,128)S(1)}) custom-call(f32[5,16,16,128]{3,2,1,0:T(8,128)S(1)} %copy-done.1, f32[16,16,128]{2,1,0:T(8,128)S(1)} %copy-done.3, s32[16,128]{1,0:T(8,128)S(1)} %copy-done.5, f32[200,128]{1,0:T(8,128)S(1)} %collective-permute-done.west, f32[200,128]{1,0:T(8,128)S(1)} %collective-permute-done.1.east), custom_call_target="tpu_custom_call" | custom-call | tf_op jit(solution)/shard_map/pack/pallas_call | solution.py:35
  50.8 2.3 %collective-permute-start.2 = (f32[2,1792]{1,0:T(2,128)S(1)}, f32[2,1792]{1,0:T(2,128)S(1)}, u32[]{:S(2)}, u32[]{:S(2)}) collective-permute-start(f32[2,1792]{1,0:T(2,128)S(1)} %get-tuple-element.11), channel_id=1, source_target_pairs={{0,1},{2,3},{4,5},{6,7},{8,9},{10,11},{12,13},{14,15},{16,17},{18,... | collective-permute-start | bytes 43016 | tf_op jit(solution)/shard_map/ppermute | solution.py:362
  53.1 4.9 %collective-permute-start.3 = (f32[2,1792]{1,0:T(2,128)S(1)}, f32[2,1792]{1,0:T(2,128)S(1)}, u32[]{:S(2)}, u32[]{:S(2)}) collective-permute-start(f32[2,1792]{1,0:T(2,128)S(1)} %get-tuple-element.12), channel_id=1, source_target_pairs={{1,2},{3,4},{5,6},{7,8},{9,10},{11,12},{13,14},{15,16},{17,18},{19... | collective-permute-start | bytes 43016 | tf_op jit(solution)/shard_map/ppermute | solution.py:363
  57.9 0.0 collective-permute-done.2.from_a
  57.9 2.0 %collective-permute-done.3.from_b = f32[2,1792]{1,0:T(2,128)S(1)} collective-permute-done((f32[2,1792]{1,0:T(2,128)S(1)}, f32[2,1792]{1,0:T(2,128)S(1)}, u32[]{:S(2)}, u32[]{:S(2)}) %collective-permute-start.3) | collective-permute-done | bytes 14368 | tf_op jit(solution)/shard_map/ppermute | solution.py:363
  59.9 0.9 %all-to-all-done.1.wrapped = f32[32,8,128]{2,1,0:T(8,128)S(1)} async-done(((f32[32,8,128]{2,1,0:T(8,128)}), f32[32,8,128]{2,1,0:T(8,128)S(1)}, u32[]{:S(2)}, u32[]{:S(2)}) %all-to-all-start.1) | async-done | bytes 131104 | tf_op jit(solution)/shard_map/all_to_all | solution.py:370
  60.8 6.3 %sections.1 = f32[5,16,16,128]{3,2,1,0:T(8,128)} custom-call(f32[5,16,16,128]{3,2,1,0:T(8,128)S(1)} %copy-done.1, f32[16,16,128]{2,1,0:T(8,128)S(1)} %copy-done.3, s32[16,128]{1,0:T(8,128)S(1)} %copy-done.5, f32[200,128]{1,0:T(8,128)S(1)} %collective-permute-done.west, f32[200,128]{1,0:T(8,128)S(1)} %collective-permute-done.1.east, ...), custom_call_target="tpu_custom_call" | custom-call | tf_op jit(solution)/shard_map/sections/pallas_call | solution.py:35
Async XLA Ops:
  0.0 1.1 %copy-start = (f32[5,16,16,128]{3,2,1,0:T(8,128)S(1)}, f32[5,16,16,128]{3,2,1,0:T(8,128)}, u32[]{:S(2)}) copy-start(f32[5,16,16,128]{3,2,1,0:T(8,128)} %fields.5) | copy-start | bytes 1966084
  1.1 0.9 %copy-start.2 = (f32[16,16,128]{2,1,0:T(8,128)S(1)}, f32[16,16,128]{2,1,0:T(8,128)}, u32[]{:S(2)}) copy-start(f32[16,16,128]{2,1,0:T(8,128)} %diff.5) | copy-start | bytes 393220
  2.0 0.7 %copy-start.4 = (s32[16,128]{1,0:T(8,128)S(1)}, s32[16,128]{1,0:T(8,128)}, u32[]{:S(2)}) copy-start(s32[16,128]{1,0:T(8,128)} %heights.5) | copy-start | bytes 24580
  2.7 28.0 %copy-start.6 = (s32[4096]{0:T(1024)S(1)}, s32[4096]{0:T(1024)}, u32[]{:S(2)}) copy-start(s32[4096]{0:T(1024)} %param.7) | copy-start | bytes 49156
  2.8 47.1 %copy-start.1 = (f32[5,16,16,128]{3,2,1,0:T(8,128)S(1)}, f32[5,16,16,128]{3,2,1,0:T(8,128)}, u32[]{:S(2)}) copy-start(f32[5,16,16,128]{3,2,1,0:T(8,128)} %fields.5) | copy-start | bytes 1966084
  2.8 15.2 %collective-permute-start = (f32[200,128]{1,0:T(8,128)S(1)}, f32[200,128]{1,0:T(8,128)S(1)}, u32[]{:S(2)}, u32[]{:S(2)}) collective-permute-start(f32[200,128]{1,0:T(8,128)S(1)} %get-tuple-element.9), channel_id=1, source_target_pairs={{0,32},{32,64},{64,96},{96,128},{128,160},{160,192},{192,224},{224... | collective-permute-start | bytes 307208 | tf_op jit(solution)/shard_map/ppermute | solution.py:349
  7.8 11.2 %collective-permute-start.1 = (f32[200,128]{1,0:T(8,128)S(1)}, f32[200,128]{1,0:T(8,128)S(1)}, u32[]{:S(2)}, u32[]{:S(2)}) collective-permute-start(f32[200,128]{1,0:T(8,128)S(1)} %get-tuple-element.10), channel_id=1, source_target_pairs={{32,0},{64,32},{96,64},{128,96},{160,128},{192,160},{224,192},{256... | collective-permute-start | bytes 307208 | tf_op jit(solution)/shard_map/ppermute | solution.py:350
  19.7 21.7 %all-to-all-start = ((f32[32,8,128]{2,1,0:T(8,128)}), f32[32,8,128]{2,1,0:T(8,128)S(1)}, u32[]{:S(2)}, u32[]{:S(2)}) async-start(f32[32,8,128]{2,1,0:T(8,128)} %packets.1), calls=%async_computation | async-start | bytes 262144 | tf_op jit(solution)/shard_map/all_to_all | solution.py:365
  46.0 3.9 %copy-start.3 = (f32[16,16,128]{2,1,0:T(8,128)S(1)}, f32[16,16,128]{2,1,0:T(8,128)}, u32[]{:S(2)}) copy-start(f32[16,16,128]{2,1,0:T(8,128)} %diff.5) | copy-start | bytes 393220
  46.0 3.9 %copy-start.5 = (s32[16,128]{1,0:T(8,128)S(1)}, s32[16,128]{1,0:T(8,128)}, u32[]{:S(2)}) copy-start(s32[16,128]{1,0:T(8,128)} %heights.5) | copy-start | bytes 24580
  46.0 14.9 %all-to-all-start.1 = ((f32[32,8,128]{2,1,0:T(8,128)}), f32[32,8,128]{2,1,0:T(8,128)S(1)}, u32[]{:S(2)}, u32[]{:S(2)}) async-start(f32[32,8,128]{2,1,0:T(8,128)} %permute.1), calls=%async_computation.1 | async-start | bytes 262144 | tf_op jit(solution)/shard_map/all_to_all | solution.py:370
  50.8 7.1 %collective-permute-start.2 = (f32[2,1792]{1,0:T(2,128)S(1)}, f32[2,1792]{1,0:T(2,128)S(1)}, u32[]{:S(2)}, u32[]{:S(2)}) collective-permute-start(f32[2,1792]{1,0:T(2,128)S(1)} %get-tuple-element.11), channel_id=1, source_target_pairs={{0,1},{2,3},{4,5},{6,7},{8,9},{10,11},{12,13},{14,15},{16,17},{18,... | collective-permute-start | bytes 43016 | tf_op jit(solution)/shard_map/ppermute | solution.py:362
  53.1 6.9 %collective-permute-start.3 = (f32[2,1792]{1,0:T(2,128)S(1)}, f32[2,1792]{1,0:T(2,128)S(1)}, u32[]{:S(2)}, u32[]{:S(2)}) collective-permute-start(f32[2,1792]{1,0:T(2,128)S(1)} %get-tuple-element.12), channel_id=1, source_target_pairs={{1,2},{3,4},{5,6},{7,8},{9,10},{11,12},{13,14},{15,16},{17,18},{19... | collective-permute-start | bytes 43016 | tf_op jit(solution)/shard_map/ppermute | solution.py:363

commit v2 on v1

v2 whole, which is shorter than its diff:
```python
import functools

import jax
import jax.numpy as jnp
from jax import lax
from jax.experimental import pallas as pl
from jax.experimental.pallas import tpu as pltpu
from jax.sharding import PartitionSpec as P

DRAG_COEF = 1.0
TIME_STEP = 0.3
BUOYANCY = 0.5
SPEED_EPS = 0.01

NF = 5
NA = 6
NZ = 16
NI = 16
NJ = 128
RIM = NA * NZ
EDGE_ROWS = 2 * RIM + 8
MESSAGE = EDGE_ROWS + 8
BLOCK = NA * NZ * NI
PACK = BLOCK + 128
HEIGHT_AT = BLOCK

VMEM = pl.BlockSpec(memory_space=pltpu.VMEM)
EXACT = lax.Precision.HIGHEST


def iota(shape, dim):
    return lax.broadcasted_iota(jnp.int32, shape, dim)


def call(kernel, outs, *args, scratch=(), name=None):
    return pl.pallas_call(
        kernel,
        out_shape=outs,
        in_specs=[VMEM] * len(args),
        out_specs=jax.tree.map(lambda _: VMEM, outs),
        scratch_shapes=list(scratch),
        compiler_params=pltpu.CompilerParams(vmem_limit_bytes=40 * 1024 * 1024),
        name=name,
    )(*args)


def f32(*shape):
    return jax.ShapeDtypeStruct(shape, jnp.float32)


def picks():
    row, lane = iota((8, NJ), 0), iota((8, NJ), 1)
    want = jnp.where(row < 2, row, jnp.where(row < 4, NJ - 4 + row, -1))
    return jnp.where(lane == want, 1.0, 0.0).astype(jnp.float32)


def is_first():
    return lax.rem(lax.axis_index("gx"), lax.axis_size("gx") // 2) == 0


def is_last():
    half = lax.axis_size("gx") // 2
    return lax.rem(lax.axis_index("gx"), half) == half - 1


def pack_kernel(early, fields, diff, heights, to_a, to_b):
    @pl.when(is_first() == early)
    def _():
        even = lax.rem(lax.axis_index("gy"), 2) == 0
        rows = jnp.concatenate(
            [
                fields[...].reshape(NF * NZ * NI, NJ),
                diff[...].reshape(NZ * NI, NJ),
                heights[...].astype(jnp.float32),
                jnp.zeros((PACK - HEIGHT_AT - NI, NJ), jnp.float32),
            ],
            0,
        )
        cols = lax.dot_general(
            picks(), rows, (((1,), (1,)), ((), ())), precision=EXACT, preferred_element_type=jnp.float32
        )
        low, high = cols[0:2, :], cols[2:4, :]
        to_a[...] = jnp.where(even, high, low)
        to_b[...] = jnp.where(even, low, high)


def unpack_kernel(
    early_a, early_b, late_a, late_b, fields, diff, heights, halo, to_east, to_west, view
):
    even, early = lax.rem(lax.axis_index("gy"), 2) == 0, is_first()
    a = jnp.where(early, early_a[...], late_a[...])
    b = jnp.where(early, early_b[...], late_b[...])
    north, south = jnp.where(even, a, b), jnp.where(even, b, a)
    cols = jnp.concatenate([north, south, jnp.zeros((4, PACK), jnp.float32)], 0)
    spread = lax.dot_general(
        cols, picks(), (((0,), (0,)), ((), ())), precision=EXACT, preferred_element_type=jnp.float32
    )
    halo[...] = spread
    view[...] = spread[0:BLOCK, :].reshape(RIM, NI, NJ)
    spare = jnp.zeros((NJ - RIM, NJ), jnp.float32)
    for to, near, far in ((to_east, NI - 1, NI - 2), (to_west, 0, 1)):
        for i in range(NA):
            src = diff if i == NF else fields.at[i]
            to[i * NZ:(i + 1) * NZ, :] = src[:, near, :]
            to[RIM + i * NZ:RIM + (i + 1) * NZ, :] = src[:, far, :]
        row = heights[near:near + 1, :].astype(jnp.float32)
        to[2 * RIM:EDGE_ROWS, :] = jnp.broadcast_to(row, (8, NJ))
        corners = jnp.concatenate([view[:, near, :], spare], 0)
        to[EDGE_ROWS:MESSAGE, :] = lax.dot_general(
            picks(), corners, (((1,), (1,)), ((), ())), precision=EXACT, preferred_element_type=jnp.float32
        )


def levels(x, edge):
    k = iota(x.shape, 0)
    above = jnp.where(k == NZ - 1, x if edge else 0.0, pltpu.roll(x, NZ - 1, 0))
    below = jnp.where(k == 0, x if edge else 0.0, pltpu.roll(x, 1, 0))
    return above, below


def row_rates(near, far, height, sign):
    u, v, w = near[0], near[1], near[2]
    k_cell = near[NF]
    k_above, k_below = levels(k_cell, True)
    drag = jnp.where(iota(u.shape, 0).astype(jnp.float32) < height, DRAG_COEF, 0.0)
    resist = drag * jnp.sqrt(u * u + v * v + w * w + SPEED_EPS)
    rates = []
    for m in range(NF):
        f = near[m]
        above, below = levels(f, False)
        rate = 0.5 * (
            (k_cell + far[NF]) * (far[m] - f)
            + (k_cell + k_above) * (above - f)
            + (k_cell + k_below) * (below - f)
            + sign * u * far[m]
            - w * (above - below)
        )
        if m < 3:
            rate = rate - resist * f
        if m == 2:
            rate = rate + BUOYANCY * near[3]
        rates.append(rate)
    return rates


def split_rim(rim):
    near = [rim[a * NZ:(a + 1) * NZ, :] for a in range(NA)]
    far = [rim[RIM + a * NZ:RIM + (a + 1) * NZ, :] for a in range(NA)]
    return near, far, rim[2 * RIM:2 * RIM + 1, :]


def packet_kernel(fields_hbm, diff_hbm, heights_hbm, out, fields, diff, heights, sems):
    late = is_last()
    half = pl.ds(pl.multiple_of(jnp.where(late, NI - 8, 0), 8), 8)
    copies = [
        pltpu.make_async_copy(fields_hbm.at[:, :, half, :], fields, sems.at[0]),
        pltpu.make_async_copy(diff_hbm.at[:, half, :], diff, sems.at[1]),
        pltpu.make_async_copy(heights_hbm.at[half, :], heights, sems.at[2]),
    ]
    for copy in copies:
        copy.start()
    out[...] = jnp.zeros_like(out)
    for copy in copies:
        copy.wait()

    def row(r):
        both = [fields[m, :, r, :] for m in range(NF)], [fields[m, :, 7 - r, :] for m in range(NF)]
        parts = [jnp.where(late, b, a) for a, b in zip(*both)]
        return parts + [jnp.where(late, diff[:, 7 - r, :], diff[:, r, :])]

    near, far = row(0), row(1)
    height = jnp.where(late, heights[7:8, :], heights[0:1, :]).astype(jnp.float32)
    sign = jnp.where(late, 1.0, -1.0).astype(jnp.float32)
    rates = row_rates(near, far, height, sign)
    zero = jnp.zeros((NZ, NJ), jnp.float32)
    lower = [near[0], near[1], near[2], near[NF], rates[0], rates[1], rates[2], zero]
    upper = [near[3], near[4], near[1], near[NF], rates[3], rates[4], zero, zero]
    at = jnp.where(late, 0, 2 * NZ)
    for row in range(8):
        out[pl.ds(at, NZ), row, :] = lower[row]
        out[pl.ds(at + NZ, NZ), row, :] = upper[row]


def inverse_kernel(wrap, out):
    total = jnp.zeros((64, NJ), jnp.float32)
    lane = iota((32, NJ), 1).astype(jnp.float32)
    for s in range(32):
        p = wrap[s:s + 1, :]
        hit = jnp.where(iota((32, NJ), 0) == p // NJ, 1.0, 0.0)
        low = jnp.where(iota((NJ, NJ), 0) == lax.rem(p, NJ), 1.0, 0.0).astype(jnp.bfloat16)
        left = jnp.concatenate([hit * lane, hit * float(s)], 0).astype(jnp.bfloat16)
        total = total + lax.dot_general(
            left, low, (((1,), (1,)), ((), ())), preferred_element_type=jnp.float32
        )
    out[...] = (total[0:32, :] + NJ * total[32:64, :]).astype(jnp.int32)


def permute_kernel(rows, wrap, inverse, out, left_side, right_side):
    first, gx, half = is_first(), lax.axis_index("gx"), lax.axis_size("gx") // 2
    target = jnp.where(first, wrap[...], inverse[...])
    column = iota(target.shape, 0) * NJ + iota(target.shape, 1)
    target = jnp.where((gx == half) | (gx == half - 1), column, target)
    upper = lax.axis_index("gy") >= NZ
    x = jnp.where(first, rows[32:64], rows[0:32])
    lane, sub = iota(x.shape, 2), iota(x.shape, 1)

    def after(y):
        return jnp.concatenate([y[1:], y[:1]], 0)

    def before(y):
        return jnp.concatenate([y[-1:], y[:-1]], 0)

    left, right = pltpu.roll(x, NJ - 1, 2), pltpu.roll(x, 1, 2)
    north = jnp.where(lane == NJ - 1, after(left), left)
    south = jnp.where(lane == 0, before(right), right)
    v = jnp.where(upper, x[:, 2:3, :], x[:, 1:2, :])
    k_cell, k_north, k_south = x[:, 3:4, :], north[:, 3:4, :], south[:, 3:4, :]
    term = 0.5 * (
        (k_cell + k_north) * (north - x) + (k_cell + k_south) * (south - x) - v * (north - south)
    )
    x = x + jnp.where((sub >= 4) & (sub < 7), pltpu.roll(term, 4, 1), 0.0)

    part_a = x.astype(jnp.bfloat16).astype(jnp.float32)
    rest = x - part_a
    part_b = rest.astype(jnp.bfloat16).astype(jnp.float32)
    part_c = rest - part_b
    for s in range(32):
        t = target[s:s + 1, :]
        hi, lo = lax.shift_right_logical(t, 8), lax.bitwise_and(t, 255)
        stack = jnp.concatenate([part_a[s], part_b[s], part_c[s]], 0)
        masked = jnp.concatenate([jnp.where(hi == h, stack, 0.0) for h in range(16)], 0)
        at = slice(s * NJ, (s + 1) * NJ)
        left_side[:, at] = masked.astype(jnp.bfloat16)
        right_side[:, at] = jnp.where(iota((256, NJ), 0) == lo, 1.0, 0.0).astype(jnp.bfloat16)
    moved = lax.dot_general(
        left_side[...], right_side[...], (((1,), (1,)), ((), ())), preferred_element_type=jnp.float32
    )
    for h in range(16):
        at = h * 24
        tile = moved[at:at + 8, :] + moved[at + 8:at + 16, :] + moved[at + 16:at + 24, :]
        out[2 * h] = tile[:, 0:NJ]
        out[2 * h + 1] = tile[:, NJ:2 * NJ]
    y = out[...]
    prior, later = before(y), after(y)
    last = jnp.zeros_like(y)
    for r in range(4):
        corner = jnp.where(lane < 64, pltpu.roll(later, r, 2), pltpu.roll(prior, (NJ - r) % NJ, 2))
        corner = pltpu.roll(corner, 7 - r, 1)
        last = jnp.where((lane == r) | (lane == NJ - 1 - r), corner, last)
    out[...] = jnp.where(sub == 7, last, y)


def beside(m, h):
    lane = iota(m.shape, 1)
    m_left, h_left = pltpu.roll(m, NJ - 1, 1), pltpu.roll(h, NJ - 1, 1)
    m_right, h_right = pltpu.roll(m, 1, 1), pltpu.roll(h, 1, 1)
    at_end, at_start = lane == NJ - 1, lane == 0
    return (
        jnp.where(at_end, h_left, m_left),
        jnp.where(at_start, h_right, m_right),
        jnp.where(at_end, m_left, h_left),
        jnp.where(at_start, m_right, h_right),
    )


def rates_of(cells, k_cell, k_sides, drag, sign=None):
    u, v, w = cells[0][0], cells[1][0], cells[2][0]
    resist = drag * jnp.sqrt(u * u + v * v + w * w + SPEED_EPS)
    if sign is not None:
        u = sign * u
    sums = [k_cell + side for side in k_sides]
    total = sums[0] + sums[1] + sums[2] + sums[3] + sums[4] + sums[5]
    rates = []
    for m in range(NF):
        f, e, ws, n, s, up, dn = cells[m]
        rate = 0.5 * (
            (sums[0] - u) * e + (sums[1] + u) * ws
            + (sums[2] - v) * n + (sums[3] + v) * s
            + (sums[4] - w) * up + (sums[5] + w) * dn
            - total * f
        )
        if m < 3:
            rate = rate - resist * f
        if m == 2:
            rate = rate + BUOYANCY * cells[3][0]
        rates.append(rate)
    return rates


def sections_kernel(
    fields, diff, heights, west, east, halo, out, kept, one, one_halo, one_w, one_e, corner_w, corner_e
):
    first = is_first()
    sub = iota((NI, NJ), 0)

    for rim, sign, own_row, one_out, corners in (
        (west, 1.0, 0, one_w, corner_w), (east, -1.0, NI - 1, one_e, corner_e)
    ):
        corners[...] = lax.dot_general(
            rim[EDGE_ROWS:MESSAGE, :], picks(), (((0,), (0,)), ((), ())),
            precision=EXACT, preferred_element_type=jnp.float32,
        )
        near, far, height = split_rim(rim)
        rates = row_rates(near, far, height, sign)
        sides = [beside(near[i], corners[i * NZ:(i + 1) * NZ, :]) for i in range(NA)]
        k_cell, k_n, k_s = near[NF], sides[NF][0], sides[NF][1]
        k_own = diff[:, own_row, :]
        for m in range(NF):
            f, n, s = near[m], sides[m][0], sides[m][1]
            own = fields[m, :, own_row, :]
            rate = rates[m] + 0.5 * (
                (k_cell + k_n) * (n - f) + (k_cell + k_s) * (s - f) - near[1] * (n - s)
                + (k_cell + k_own) * (own - f) - sign * near[0] * own
            )
            one_out[m * NZ:(m + 1) * NZ, :] = f + TIME_STEP / 3.0 * rate

    def row_of(ref, i, k):
        return ref[pl.ds(i * NZ + k, 1), :]

    def along(x, low, high):
        return (
            jnp.where(sub == NI - 1, high, pltpu.roll(x, NI - 1, 0)),
            jnp.where(sub == 0, low, pltpu.roll(x, 1, 0)),
        )

    def halo_tile(i, k):
        at = pl.multiple_of((i * NZ + k) * NI, NI)
        return halo[pl.ds(at, NI), :]

    high_main = heights[...].astype(jnp.float32)
    high_halo = halo[HEIGHT_AT:HEIGHT_AT + NI, :]

    def section_one(k, _):
        up, dn = jnp.minimum(k + 1, NZ - 1), jnp.maximum(k - 1, 0)
        has_up = jnp.where(k < NZ - 1, 1.0, 0.0).astype(jnp.float32)
        has_dn = jnp.where(k > 0, 1.0, 0.0).astype(jnp.float32)
        level = k.astype(jnp.float32)
        k_main, k_halo = diff[k], halo_tile(NF, k)
        n, s, hn, hs = beside(k_main, k_halo)
        e, ws = along(k_main, row_of(west, NF, k), row_of(east, NF, k))
        he, hw = along(k_halo, row_of(corner_w, NF, k), row_of(corner_e, NF, k))
        k_sides = (e, ws, n, s, diff[up], diff[dn])
        kh_sides = (he, hw, hn, hs, halo_tile(NF, up), halo_tile(NF, dn))
        cells, halos = [], []
        for m in range(NF):
            f, h = fields[m, k], halo_tile(m, k)
            n, s, hn, hs = beside(f, h)
            e, ws = along(f, row_of(west, m, k), row_of(east, m, k))
            he, hw = along(h, row_of(corner_w, m, k), row_of(corner_e, m, k))
            cells.append((f, e, ws, n, s, has_up * fields[m, up], has_dn * fields[m, dn]))
            halos.append((h, he, hw, hn, hs, has_up * halo_tile(m, up), has_dn * halo_tile(m, dn)))
        drag = jnp.where(level < high_main, DRAG_COEF, 0.0)
        drag_h = jnp.where(level < high_halo, DRAG_COEF, 0.0)
        rates = rates_of(cells, k_main, k_sides, drag)
        rates_h = rates_of(halos, k_halo, kh_sides, drag_h)
        for m in range(NF):
            one[m, k] = cells[m][0] + TIME_STEP / 3.0 * rates[m]
            one_halo[m, k] = halos[m][0] + TIME_STEP / 3.0 * rates_h[m]
        return 0

    lax.fori_loop(0, NZ, section_one, 0)

    def section_two(k, _):
        up, dn = jnp.minimum(k + 1, NZ - 1), jnp.maximum(k - 1, 0)
        has_up = jnp.where(k < NZ - 1, 1.0, 0.0).astype(jnp.float32)
        has_dn = jnp.where(k > 0, 1.0, 0.0).astype(jnp.float32)
        k_main = diff[k]
        n, s, _, _ = beside(k_main, halo_tile(NF, k))
        e, ws = along(k_main, row_of(west, NF, k), row_of(east, NF, k))
        k_sides = (e, ws, n, s, diff[up], diff[dn])
        cells = []
        for m in range(NF):
            f = one[m, k]
            n, s, _, _ = beside(f, one_halo[m, k])
            e, ws = along(f, row_of(one_w, m, k), row_of(one_e, m, k))
            cells.append((f, e, ws, n, s, has_up * one[m, up], has_dn * one[m, dn]))
        drag = jnp.where(k.astype(jnp.float32) < high_main, DRAG_COEF, 0.0)
        rates = rates_of(cells, k_main, k_sides, drag)
        for m in range(NF):
            out[m, k] = fields[m, k] + TIME_STEP / 2.0 * rates[m]
        return 0

    lax.fori_loop(0, NZ, section_two, 0)
    for m in range(NF):
        for r in range(3):
            kept[m, r] = jnp.where(first, one[m, :, r, :], one[m, :, NI - 1 - r, :])
        for r in range(2):
            kept[m, 3 + r] = jnp.where(first, one_halo[m, :, r, :], one_halo[m, :, NI - 1 - r, :])


def wrap_kernel(fields, diff, heights, halo, kept, wrapped, done, out, view):
    first, final = is_first(), is_last()
    out[...] = done[...]

    @pl.when(first | final)
    def _():
        view[...] = halo[0:BLOCK, :].reshape(RIM, NI, NJ)
        sign = jnp.where(first, 1.0, -1.0).astype(jnp.float32)
        lane = iota((NZ, NJ), 1)

        def block_row(i, r):
            src = diff if i == NF else fields.at[i]
            return jnp.where(first, src[:, r, :], src[:, NI - 1 - r, :])

        def halo_row(i, r):
            at = slice(i * NZ, (i + 1) * NZ)
            return jnp.where(first, view[at, r, :], view[at, NI - 1 - r, :])

        place = {0: (0, 0), 1: (0, 1), 2: (0, 2), NF: (0, 3), 3: (NZ, 0), 4: (NZ, 1)}
        outer, corner = [], []
        for i in range(NA):
            half, row = place[i]
            outer.append(wrapped[half:half + NZ, row, :])
            spare = wrapped[half:half + NZ, 7, :]
            corner.append(
                jnp.where(lane < 64, pltpu.roll(spare, (NJ - row) % NJ, 1), pltpu.roll(spare, row, 1))
            )
        own = [block_row(i, 0) for i in range(NA)]
        side = [halo_row(i, 0) for i in range(NA)]
        one_out, one_own, one_side = [], [], []
        for m in range(NF):
            half, row = (0, 4 + m) if m < 3 else (NZ, 1 + m)
            rate = wrapped[half:half + NZ, row, :] + 0.5 * (
                (outer[NF] + own[NF]) * (own[m] - outer[m]) - sign * outer[0] * own[m]
            )
            one_out.append(outer[m] + TIME_STEP / 3.0 * rate)
            rate = (own[NF] + outer[NF] + sign * own[0]) * outer[m] - outer[NF] * own[m]
            one_own.append(kept[m, 0] + TIME_STEP / 6.0 * rate)
            rate = (side[NF] + corner[NF] + sign * side[0]) * corner[m] - corner[NF] * side[m]
            one_side.append(kept[m, 3] + TIME_STEP / 6.0 * rate)
        k_rows = [outer[NF], own[NF], block_row(NF, 1), block_row(NF, 2)]
        k_halos = [side[NF], halo_row(NF, 1)]
        ones = [[one_out[m], one_own[m], kept[m, 1], kept[m, 2]] for m in range(NF)]
        one_halos = [[one_side[m], kept[m, 4]] for m in range(NF)]
        for r in range(2):
            k_cell = k_rows[r + 1]
            k_n, k_s, _, _ = beside(k_cell, k_halos[r])
            k_up, k_dn = levels(k_cell, True)
            k_sides = (k_rows[r + 2], k_rows[r], k_n, k_s, k_up, k_dn)
            cells = []
            for m in range(NF):
                f = ones[m][r + 1]
                n, s, _, _ = beside(f, one_halos[m][r])
                up, dn = levels(f, False)
                cells.append((f, ones[m][r + 2], ones[m][r], n, s, up, dn))
            height = jnp.where(first, heights[r:r + 1, :], heights[NI - 1 - r:NI - r, :])
            drag = jnp.where(iota((NZ, NJ), 0) < height, DRAG_COEF, 0.0)
            rates = rates_of(cells, k_cell, k_sides, drag, sign)
            for m in range(NF):
                value = block_row(m, r) + TIME_STEP / 2.0 * rates[m]

                @pl.when(first)
                def _(value=value, m=m):
                    out[m, :, r, :] = value

                @pl.when(final)
                def _(value=value, m=m):
                    out[m, :, NI - 1 - r, :] = value


def shards(fields, diffusivity, heights, wrap_map):
    count_x, count_y = lax.axis_size("gx"), lax.axis_size("gy")
    last = count_x - 1
    pack = f32(2, PACK)
    block = (fields, diffusivity, heights)
    half = pltpu.VMEM((NF, NZ, 8, NJ), jnp.float32), pltpu.VMEM((NZ, 8, NJ), jnp.float32)
    packets = pl.pallas_call(
        packet_kernel,
        out_shape=f32(2 * count_y, 8, NJ),
        in_specs=[pl.BlockSpec(memory_space=pl.ANY)] * 3,
        out_specs=VMEM,
        scratch_shapes=[*half, pltpu.VMEM((8, NJ), jnp.int32), pltpu.SemaphoreType.DMA((3,))],
        compiler_params=pltpu.CompilerParams(vmem_limit_bytes=56 * 1024 * 1024),
        name="packets",
    )(*block)

    half_x = count_x // 2
    early_rows = [0, half_x]
    rest = [r for r in range(count_x) if r not in early_rows]
    low = [(i, i + 1) for i in range(0, count_y, 2)]
    high = [(i, (i + 1) % count_y) for i in range(1, count_y, 2)]

    def spanwise(early, rows, *after):
        tied = lax.optimization_barrier((*block, *after))[:3]
        to_a, to_b = call(functools.partial(pack_kernel, early), (pack, pack), *tied, name="pack")

        def swap(x, pairs):
            pairs = [(r * count_y + i, r * count_y + j) for r in rows for i, j in pairs]
            return lax.ppermute(x, ("gx", "gy"), pairs + [(j, i) for i, j in pairs])

        from_b = swap(to_b, high)
        return swap(to_a, low), from_b

    early_a, early_b = spanwise(True, early_rows, packets)
    packets, early_a, early_b = lax.optimization_barrier((packets, early_a, early_b))

    row_pairs = [(0, last), (half_x, half_x - 1)] + [(i, i + half_x) for i in range(1, half_x - 1)]
    groups = [[r * count_y + i for r in rows for i in range(count_y)] for rows in row_pairs]
    rows = lax.all_to_all(packets, ("gx", "gy"), 0, 0, axis_index_groups=groups)

    late_a, late_b = spanwise(False, rest, packets)
    message = f32(MESSAGE, NJ)
    halo, to_east, to_west = call(
        unpack_kernel, (f32(PACK, NJ), message, message),
        early_a, early_b, late_a, late_b, *block, name="unpack",
        scratch=[pltpu.VMEM((RIM, NI, NJ), jnp.float32)],
    )
    east_pairs = [(i, i + 1) for i in range(last) if i + 1 != half_x]
    west = lax.ppermute(to_east, "gx", east_pairs)
    east = lax.ppermute(to_west, "gx", [(j, i) for i, j in east_pairs])

    wrap = wrap_map.reshape(count_y, NJ)
    inverse = call(
        inverse_kernel, jax.ShapeDtypeStruct((count_y, NJ), jnp.int32), wrap, name="inverse"
    )
    rows, inverse, *_ = lax.optimization_barrier((rows, inverse, to_east, to_west))
    moved = call(
        permute_kernel, f32(count_y, 8, NJ), rows, wrap, inverse, name="permute",
        scratch=[pltpu.VMEM((384, 32 * NJ), jnp.bfloat16), pltpu.VMEM((256, 32 * NJ), jnp.bfloat16)],
    )
    moved, west, east = lax.optimization_barrier((moved, west, east))
    wrapped = lax.all_to_all(moved, "gy", 0, 0)

    state = pltpu.VMEM((NF, NZ, NI, NJ), jnp.float32)
    line = pltpu.VMEM((RIM, NJ), jnp.float32)
    corner = pltpu.VMEM((NJ, NJ), jnp.float32)
    done, kept = call(
        sections_kernel, (f32(NF, NZ, NI, NJ), f32(NF, 5, NZ, NJ)),
        *block, west, east, halo, name="sections", scratch=[state, state, line, line, corner, corner],
    )
    return call(
        wrap_kernel, f32(NF, NZ, NI, NJ), *block, halo, kept, wrapped, done, name="wrapped_rows",
        scratch=[pltpu.VMEM((RIM, NI, NJ), jnp.float32)],
    )


def solution(mesh):
    in_specs = (P(None, None, "gx", "gy"), P(None, "gx", "gy"), P("gx", "gy"), P())
    out_specs = P(None, None, "gx", "gy")
    return jax.shard_map(shards, mesh=mesh, in_specs=in_specs, out_specs=out_specs, check_vma=False)
```

time: 67.5 us -> 61.4 us (0.910); the launches traced: 67.1 us -> 60.2 us
  starting transfers between devices: 36.4 us -> 28.7 us
  local copies, waits for them, and re-layouts: 2.7 us -> 0.02 us
  waiting for transfers between devices: 14.5 us -> 16.7 us
  Pallas kernels: 13.3 us -> 14.6 us
    ppermute x1, starting transfers between devices: 9.52 us -> 1.29 us  [shards(): east = lax.ppermute(to_west, 'gx', [(j, i) for i, j in east_pairs])]
    all_to_all x1, waiting for transfers between devices: 0.9 us -> 5.89 us  [shards(): wrapped = lax.all_to_all(moved, 'gy', 0, 0)]
    ppermute x2 -> x4, starting transfers between devices: 7.11 us -> 12 us  [swap(): return lax.ppermute(x, ('gx', 'gy'), pairs + [(j, i) for i, j in pairs])]
    all_to_all x1, starting transfers between devices: 11 us -> 6.18 us  [shards(): rows = lax.all_to_all(packets, ('gx', 'gy'), 0, 0, axis_index_groups=groups)]
    all_to_all x1, waiting for transfers between devices: 9.95 us -> 6.24 us  [shards(): rows = lax.all_to_all(packets, ('gx', 'gy'), 0, 0, axis_index_groups=groups)]
    unnamed x14 -> x8, local copies, waits for them, and re-layouts: 2.7 us -> 0.02 us
    ppermute x2 -> x4, waiting for transfers between devices: 2.01 us -> 4.6 us  [swap(): return lax.ppermute(x, ('gx', 'gy'), pairs + [(j, i) for i, j in pairs])]
    pallas_call x0 -> x1, Pallas kernels: none -> 2.06 us  [shards(): pl.pallas_call(packet_kernel, out_shape=f32(2 * count_y, 8, NJ), in_specs...]
  transfers between devices with their start and end apart: 6 -> 8, of which waited for: 5 -> 3; matrix products, arithmetic and copies ran while one was open for 0% -> 0% of each run, Pallas kernels for 3% -> 17%
where the time goes in v2:
time: 61.4 us; the launch traced here: 60.2 us
  starting transfers between devices  28.7 us (47%)
  waiting for transfers between devices  16.7 us (27%)
  Pallas kernels  14.6 us (24%)
    pallas_call x7, Pallas kernels, call(): pl.pallas_call(kernel, out_shape=outs, in_specs=[VMEM] * len(args), out_s...  12.5 us
    ppermute x4, starting transfers between devices, swap(): return lax.ppermute(x, ('gx', 'gy'), pairs + [(j, i) for i, j in pairs])  12 us
    all_to_all x1, waiting for transfers between devices, shards(): rows = lax.all_to_all(packets, ('gx', 'gy'), 0, 0, axis_index_groups=groups)  6.24 us
    all_to_all x1, starting transfers between devices, shards(): rows = lax.all_to_all(packets, ('gx', 'gy'), 0, 0, axis_index_groups=groups)  6.18 us
    all_to_all x1, waiting for transfers between devices, shards(): wrapped = lax.all_to_all(moved, 'gy', 0, 0)  5.89 us
    all_to_all x1, starting transfers between devices, shards(): wrapped = lax.all_to_all(moved, 'gy', 0, 0)  5.63 us
    ppermute x4, waiting for transfers between devices, swap(): return lax.ppermute(x, ('gx', 'gy'), pairs + [(j, i) for i, j in pairs])  4.6 us
    ppermute x1, starting transfers between devices, shards(): west = lax.ppermute(to_east, 'gx', east_pairs)  3.58 us
  transfers between devices with their start and end apart: 8, of which 3 were waited for; matrix products, arithmetic and copies ran while one was open for 0% of the time, Pallas kernels for 17%

profile of v2, /device:TPU:1, one launch (start us, length us, event | category | flops | bytes accessed | tf_op | source)
XLA Modules:
  0.0 60.2 jit_solution(16387894552836091730)
XLA Ops:
  0.0 0.0 copy-start.2
  0.0 0.0 copy-start.1
  0.0 0.0 copy-start
  0.0 2.1 %packets.1 = f32[64,8,128]{2,1,0:T(8,128)} custom-call(f32[5,16,16,128]{3,2,1,0:T(8,128)} %fields.7, f32[16,16,128]{2,1,0:T(8,128)} %diff.7, s32[16,128]{1,0:T(8,128)} %heights.7), custom_call_target="tpu_custom_call" | custom-call | tf_op jit(solution)/shard_map/packets/pallas_call | solution.py:467
  2.1 0.0 copy-done.2
  2.1 0.0 copy-done.1
  2.1 0.0 copy-done
  2.1 0.8 %pack.2 = (f32[2,1664]{1,0:T(2,128)S(1)}, f32[2,1664]{1,0:T(2,128)S(1)}) custom-call(f32[5,16,16,128]{3,2,1,0:T(8,128)S(1)} %copy-done, f32[16,16,128]{2,1,0:T(8,128)S(1)} %copy-done.1, s32[16,128]{1,0:T(8,128)S(1)} %copy-done.2), custom_call_target="tpu_custom_call" | custom-call | tf_op jit(solution)/shard_map/pack/pallas_call | solution.py:36
  2.9 8.8 %collective-permute-start = (f32[2,1664]{1,0:T(2,128)S(1)}, f32[2,1664]{1,0:T(2,128)S(1)}, u32[]{:S(2)}, u32[]{:S(2)}) collective-permute-start(f32[2,1664]{1,0:T(2,128)S(1)} %get-tuple-element.31), channel_id=1, source_target_pairs={{0,1},{2,3},{4,5},{6,7},{8,9},{10,11},{12,13},{14,15},{16,17},{18,... | collective-permute-start | bytes 39944 | tf_op jit(solution)/shard_map/ppermute | solution.py:489
  11.7 1.9 %collective-permute-start.1 = (f32[2,1664]{1,0:T(2,128)S(1)}, f32[2,1664]{1,0:T(2,128)S(1)}, u32[]{:S(2)}, u32[]{:S(2)}) collective-permute-start(f32[2,1664]{1,0:T(2,128)S(1)} %get-tuple-element.32), channel_id=1, source_target_pairs={{1,2},{3,4},{5,6},{7,8},{9,10},{11,12},{13,14},{15,16},{17,18},{19... | collective-permute-start | bytes 39944 | tf_op jit(solution)/shard_map/ppermute | solution.py:489
  13.6 0.0 collective-permute-done.early_a
  13.6 4.6 %collective-permute-done.1.early_b = f32[2,1664]{1,0:T(2,128)S(1)} collective-permute-done((f32[2,1664]{1,0:T(2,128)S(1)}, f32[2,1664]{1,0:T(2,128)S(1)}, u32[]{:S(2)}, u32[]{:S(2)}) %collective-permute-start.1) | collective-permute-done | bytes 13344 | tf_op jit(solution)/shard_map/ppermute | solution.py:489
  18.2 6.2 %all-to-all-start = ((f32[64,8,128]{2,1,0:T(8,128)}), f32[64,8,128]{2,1,0:T(8,128)S(1)}, u32[]{:S(2)}, u32[]{:S(2)}) async-start(f32[64,8,128]{2,1,0:T(8,128)} %packets.1), calls=%async_computation | async-start | bytes 524288 | tf_op jit(solution)/shard_map/all_to_all | solution.py:499
  24.4 0.7 %collective-permute-start.2 = (f32[2,1664]{1,0:T(2,128)S(1)}, f32[2,1664]{1,0:T(2,128)S(1)}, u32[]{:S(2)}, u32[]{:S(2)}) collective-permute-start(f32[2,1664]{1,0:T(2,128)S(1)} %get-tuple-element.39), channel_id=1, source_target_pairs={{32,33},{34,35},{36,37},{38,39},{40,41},{42,43},{44,45},{46,47},{4... | collective-permute-start | bytes 39944 | tf_op jit(solution)/shard_map/ppermute | solution.py:489
  25.1 0.7 %collective-permute-start.3 = (f32[2,1664]{1,0:T(2,128)S(1)}, f32[2,1664]{1,0:T(2,128)S(1)}, u32[]{:S(2)}, u32[]{:S(2)}) collective-permute-start(f32[2,1664]{1,0:T(2,128)S(1)} %get-tuple-element.40), channel_id=1, source_target_pairs={{33,34},{35,36},{37,38},{39,40},{41,42},{43,44},{45,46},{47,48},{4... | collective-permute-start | bytes 39944 | tf_op jit(solution)/shard_map/ppermute | solution.py:489
  25.8 0.0 collective-permute-done.2.late_a
  25.8 0.0 collective-permute-done.3.late_b
  25.8 0.0 copy-start.3
  25.8 1.5 %unpack.1 = (f32[1664,128]{1,0:T(8,128)S(1)}, f32[208,128]{1,0:T(8,128)S(1)}, f32[208,128]{1,0:T(8,128)S(1)}) custom-call(f32[2,1664]{1,0:T(2,128)S(1)} %collective-permute-done.early_a, f32[2,1664]{1,0:T(2,128)S(1)} %collective-permute-done.1.early_b, f32[2,1664]{1,0:T(2,128)S(1)} %collective-permute-done.2.late_a, ...), custom_call_target="tpu_custom_call" | custom-call | tf_op jit(solution)/shard_map/unpack/pallas_call | solution.py:36
  27.3 3.6 %collective-permute-start.4 = (f32[208,128]{1,0:T(8,128)S(1)}, f32[208,128]{1,0:T(8,128)S(1)}, u32[]{:S(2)}, u32[]{:S(2)}) collective-permute-start(f32[208,128]{1,0:T(8,128)S(1)} %get-tuple-element.42), channel_id=1, source_target_pairs={{0,32},{32,64},{64,96},{96,128},{128,160},{160,192},{192,224},{256... | collective-permute-start | bytes 319496 | tf_op jit(solution)/shard_map/ppermute | solution.py:509
  30.9 1.3 %collective-permute-start.5 = (f32[208,128]{1,0:T(8,128)S(1)}, f32[208,128]{1,0:T(8,128)S(1)}, u32[]{:S(2)}, u32[]{:S(2)}) collective-permute-start(f32[208,128]{1,0:T(8,128)S(1)} %get-tuple-element.43), channel_id=1, source_target_pairs={{32,0},{64,32},{96,64},{128,96},{160,128},{192,160},{224,192},{288... | collective-permute-start | bytes 319496 | tf_op jit(solution)/shard_map/ppermute | solution.py:510
  32.2 0.0 copy-done.3
  32.2 0.8 %inverse.1 = s32[32,128]{1,0:T(8,128)S(1)} custom-call(s32[32,128]{1,0:T(8,128)S(1)} %bitcast.1), custom_call_target="tpu_custom_call" | custom-call | tf_op jit(solution)/shard_map/inverse/pallas_call | solution.py:36
  33.0 6.2 %all-to-all-done.rows = f32[64,8,128]{2,1,0:T(8,128)S(1)} async-done(((f32[64,8,128]{2,1,0:T(8,128)}), f32[64,8,128]{2,1,0:T(8,128)S(1)}, u32[]{:S(2)}, u32[]{:S(2)}) %all-to-all-start) | async-done | bytes 262176 | tf_op jit(solution)/shard_map/all_to_all | solution.py:499
  39.2 3.0 %permute.1 = f32[32,8,128]{2,1,0:T(8,128)} custom-call(f32[64,8,128]{2,1,0:T(8,128)S(1)} %all-to-all-done.rows, s32[32,128]{1,0:T(8,128)S(1)} %bitcast.2, s32[32,128]{1,0:T(8,128)S(1)} %inverse.1), custom_call_target="tpu_custom_call" | custom-call | tf_op jit(solution)/shard_map/permute/pallas_call | solution.py:36
  42.2 0.0 collective-permute-done.4.west
  42.2 0.0 collective-permute-done.5.east
  42.2 5.6 %all-to-all-start.1 = ((f32[32,8,128]{2,1,0:T(8,128)}), f32[32,8,128]{2,1,0:T(8,128)S(1)}, u32[]{:S(2)}, u32[]{:S(2)}) async-start(f32[32,8,128]{2,1,0:T(8,128)} %permute.1), calls=%async_computation.1 | async-start | bytes 262144 | tf_op jit(solution)/shard_map/all_to_all | solution.py:522
  47.9 4.9 %sections.1 = (f32[5,16,16,128]{3,2,1,0:T(8,128)S(1)}, f32[5,5,16,128]{3,2,1,0:T(8,128)S(1)}) custom-call(f32[5,16,16,128]{3,2,1,0:T(8,128)S(1)} %copy-done, f32[16,16,128]{2,1,0:T(8,128)S(1)} %copy-done.1, s32[16,128]{1,0:T(8,128)S(1)} %copy-done.2, f32[208,128]{1,0:T(8,128)S(1)} %collective-permute-done.4.west, ...), custom_call_target="tpu_custom_call" | custom-call | tf_op jit(solution)/shard_map/sections/pallas_call | solution.py:36
  52.7 5.9 %all-to-all-done.1.wrapped = f32[32,8,128]{2,1,0:T(8,128)S(1)} async-done(((f32[32,8,128]{2,1,0:T(8,128)}), f32[32,8,128]{2,1,0:T(8,128)S(1)}, u32[]{:S(2)}, u32[]{:S(2)}) %all-to-all-start.1) | async-done | bytes 131104 | tf_op jit(solution)/shard_map/all_to_all | solution.py:522
  58.6 1.6 %wrapped_rows.1 = f32[5,16,16,128]{3,2,1,0:T(8,128)} custom-call(f32[5,16,16,128]{3,2,1,0:T(8,128)S(1)} %copy-done, f32[16,16,128]{2,1,0:T(8,128)S(1)} %copy-done.1, s32[16,128]{1,0:T(8,128)S(1)} %copy-done.2, f32[1664,128]{1,0:T(8,128)S(1)} %get-tuple-element.41.halo, f32[5,5,16,128]{3,2,1,0:T(8,128)S(1)} %get-tuple-element.48.kept, ...), custom_call_target="tpu_custom_call" | custom-call | tf_op jit(solution)/shard_map/wrapped_rows/pallas_call | solution.py:36
  (1 shorter events, 0.0 us)
Async XLA Ops:
  0.0 2.1 %copy-start.2 = (s32[16,128]{1,0:T(8,128)S(1)}, s32[16,128]{1,0:T(8,128)}, u32[]{:S(2)}) copy-start(s32[16,128]{1,0:T(8,128)} %heights.7) | copy-start | bytes 24580
  0.0 2.1 %copy-start.1 = (f32[16,16,128]{2,1,0:T(8,128)S(1)}, f32[16,16,128]{2,1,0:T(8,128)}, u32[]{:S(2)}) copy-start(f32[16,16,128]{2,1,0:T(8,128)} %diff.7) | copy-start | bytes 393220
  0.0 2.1 %copy-start = (f32[5,16,16,128]{3,2,1,0:T(8,128)S(1)}, f32[5,16,16,128]{3,2,1,0:T(8,128)}, u32[]{:S(2)}) copy-start(f32[5,16,16,128]{3,2,1,0:T(8,128)} %fields.7) | copy-start | bytes 1966084
  2.9 10.7 %collective-permute-start = (f32[2,1664]{1,0:T(2,128)S(1)}, f32[2,1664]{1,0:T(2,128)S(1)}, u32[]{:S(2)}, u32[]{:S(2)}) collective-permute-start(f32[2,1664]{1,0:T(2,128)S(1)} %get-tuple-element.31), channel_id=1, source_target_pairs={{0,1},{2,3},{4,5},{6,7},{8,9},{10,11},{12,13},{14,15},{16,17},{18,... | collective-permute-start | bytes 39944 | tf_op jit(solution)/shard_map/ppermute | solution.py:489
  11.7 6.5 %collective-permute-start.1 = (f32[2,1664]{1,0:T(2,128)S(1)}, f32[2,1664]{1,0:T(2,128)S(1)}, u32[]{:S(2)}, u32[]{:S(2)}) collective-permute-start(f32[2,1664]{1,0:T(2,128)S(1)} %get-tuple-element.32), channel_id=1, source_target_pairs={{1,2},{3,4},{5,6},{7,8},{9,10},{11,12},{13,14},{15,16},{17,18},{19... | collective-permute-start | bytes 39944 | tf_op jit(solution)/shard_map/ppermute | solution.py:489
  18.2 21.0 %all-to-all-start = ((f32[64,8,128]{2,1,0:T(8,128)}), f32[64,8,128]{2,1,0:T(8,128)S(1)}, u32[]{:S(2)}, u32[]{:S(2)}) async-start(f32[64,8,128]{2,1,0:T(8,128)} %packets.1), calls=%async_computation | async-start | bytes 524288 | tf_op jit(solution)/shard_map/all_to_all | solution.py:499
  24.4 1.3 %collective-permute-start.2 = (f32[2,1664]{1,0:T(2,128)S(1)}, f32[2,1664]{1,0:T(2,128)S(1)}, u32[]{:S(2)}, u32[]{:S(2)}) collective-permute-start(f32[2,1664]{1,0:T(2,128)S(1)} %get-tuple-element.39), channel_id=1, source_target_pairs={{32,33},{34,35},{36,37},{38,39},{40,41},{42,43},{44,45},{46,47},{4... | collective-permute-start | bytes 39944 | tf_op jit(solution)/shard_map/ppermute | solution.py:489
  25.1 0.7 %collective-permute-start.3 = (f32[2,1664]{1,0:T(2,128)S(1)}, f32[2,1664]{1,0:T(2,128)S(1)}, u32[]{:S(2)}, u32[]{:S(2)}) collective-permute-start(f32[2,1664]{1,0:T(2,128)S(1)} %get-tuple-element.40), channel_id=1, source_target_pairs={{33,34},{35,36},{37,38},{39,40},{41,42},{43,44},{45,46},{47,48},{4... | collective-permute-start | bytes 39944 | tf_op jit(solution)/shard_map/ppermute | solution.py:489
  25.8 6.4 %copy-start.3 = (s32[4096]{0:T(1024)S(1)}, s32[4096]{0:T(1024)}, u32[]{:S(2)}) copy-start(s32[4096]{0:T(1024)} %param.7) | copy-start | bytes 49156
  27.3 14.9 %collective-permute-start.4 = (f32[208,128]{1,0:T(8,128)S(1)}, f32[208,128]{1,0:T(8,128)S(1)}, u32[]{:S(2)}, u32[]{:S(2)}) collective-permute-start(f32[208,128]{1,0:T(8,128)S(1)} %get-tuple-element.42), channel_id=1, source_target_pairs={{0,32},{32,64},{64,96},{96,128},{128,160},{160,192},{192,224},{256... | collective-permute-start | bytes 319496 | tf_op jit(solution)/shard_map/ppermute | solution.py:509
  30.9 11.4 %collective-permute-start.5 = (f32[208,128]{1,0:T(8,128)S(1)}, f32[208,128]{1,0:T(8,128)S(1)}, u32[]{:S(2)}, u32[]{:S(2)}) collective-permute-start(f32[208,128]{1,0:T(8,128)S(1)} %get-tuple-element.43), channel_id=1, source_target_pairs={{32,0},{64,32},{96,64},{128,96},{160,128},{192,160},{224,192},{288... | collective-permute-start | bytes 319496 | tf_op jit(solution)/shard_map/ppermute | solution.py:510
  42.2 16.4 %all-to-all-start.1 = ((f32[32,8,128]{2,1,0:T(8,128)}), f32[32,8,128]{2,1,0:T(8,128)S(1)}, u32[]{:S(2)}, u32[]{:S(2)}) async-start(f32[32,8,128]{2,1,0:T(8,128)} %permute.1), calls=%async_computation.1 | async-start | bytes 262144 | tf_op jit(solution)/shard_map/all_to_all | solution.py:522

commit v3 on v2

--- a/solution.py
+++ b/solution.py
@@ -1,5 +1,3 @@
-import functools
-
 import jax
 import jax.numpy as jnp
 from jax import lax
@@ -23,6 +21,7 @@
 BLOCK = NA * NZ * NI
 PACK = BLOCK + 128
 HEIGHT_AT = BLOCK
+HALO = RIM + 1
 
 VMEM = pl.BlockSpec(memory_space=pltpu.VMEM)
 EXACT = lax.Precision.HIGHEST
@@ -63,40 +62,34 @@
     return lax.rem(lax.axis_index("gx"), half) == half - 1
 
 
-def pack_kernel(early, fields, diff, heights, to_a, to_b):
-    @pl.when(is_first() == early)
-    def _():
-        even = lax.rem(lax.axis_index("gy"), 2) == 0
-        rows = jnp.concatenate(
-            [
-                fields[...].reshape(NF * NZ * NI, NJ),
-                diff[...].reshape(NZ * NI, NJ),
-                heights[...].astype(jnp.float32),
-                jnp.zeros((PACK - HEIGHT_AT - NI, NJ), jnp.float32),
-            ],
-            0,
-        )
-        cols = lax.dot_general(
-            picks(), rows, (((1,), (1,)), ((), ())), precision=EXACT, preferred_element_type=jnp.float32
-        )
-        low, high = cols[0:2, :], cols[2:4, :]
-        to_a[...] = jnp.where(even, high, low)
-        to_b[...] = jnp.where(even, low, high)
-
-
-def unpack_kernel(
-    early_a, early_b, late_a, late_b, fields, diff, heights, halo, to_east, to_west, view
-):
-    even, early = lax.rem(lax.axis_index("gy"), 2) == 0, is_first()
-    a = jnp.where(early, early_a[...], late_a[...])
-    b = jnp.where(early, early_b[...], late_b[...])
+def pack_kernel(fields, diff, heights, to_a, to_b):
+    even = lax.rem(lax.axis_index("gy"), 2) == 0
+    rows = jnp.concatenate(
+        [
+            fields[...].reshape(NF * NZ * NI, NJ),
+            diff[...].reshape(NZ * NI, NJ),
+            heights[...].astype(jnp.float32),
+            jnp.zeros((PACK - HEIGHT_AT - NI, NJ), jnp.float32),
+        ],
+        0,
+    )
+    cols = lax.dot_general(
+        picks(), rows, (((1,), (1,)), ((), ())), precision=EXACT, preferred_element_type=jnp.float32
+    )
+    low, high = cols[0:2, :], cols[2:4, :]
+    to_a[...] = jnp.where(even, high, low)
+    to_b[...] = jnp.where(even, low, high)
+
+
+def unpack_kernel(from_a, from_b, fields, diff, heights, halo, to_east, to_west):
+    even = lax.rem(lax.axis_index("gy"), 2) == 0
+    a, b = from_a[...], from_b[...]
     north, south = jnp.where(even, a, b), jnp.where(even, b, a)
     cols = jnp.concatenate([north, south, jnp.zeros((4, PACK), jnp.float32)], 0)
     spread = lax.dot_general(
         cols, picks(), (((0,), (0,)), ((), ())), precision=EXACT, preferred_element_type=jnp.float32
     )
-    halo[...] = spread
-    view[...] = spread[0:BLOCK, :].reshape(RIM, NI, NJ)
+    halo[...] = spread[0:HALO * NI, :].reshape(HALO, NI, NJ)
     spare = jnp.zeros((NJ - RIM, NJ), jnp.float32)
     for to, near, far in ((to_east, NI - 1, NI - 2), (to_west, 0, 1)):
         for i in range(NA):
@@ -105,7 +98,7 @@
             to[RIM + i * NZ:RIM + (i + 1) * NZ, :] = src[:, far, :]
         row = heights[near:near + 1, :].astype(jnp.float32)
         to[2 * RIM:EDGE_ROWS, :] = jnp.broadcast_to(row, (8, NJ))
-        corners = jnp.concatenate([view[:, near, :], spare], 0)
+        corners = jnp.concatenate([halo[0:RIM, near, :], spare], 0)
         to[EDGE_ROWS:MESSAGE, :] = lax.dot_general(
             picks(), corners, (((1,), (1,)), ((), ())), precision=EXACT, preferred_element_type=jnp.float32
         )
@@ -287,68 +280,33 @@
     return rates
 
 
-def sections_kernel(
-    fields, diff, heights, west, east, halo, out, kept, one, one_halo, one_w, one_e, corner_w, corner_e
-):
-    first = is_first()
+def sections_kernel(fields, diff, heights, halo, out, kept, one, one_halo):
     sub = iota((NI, NJ), 0)
 
-    for rim, sign, own_row, one_out, corners in (
-        (west, 1.0, 0, one_w, corner_w), (east, -1.0, NI - 1, one_e, corner_e)
-    ):
-        corners[...] = lax.dot_general(
-            rim[EDGE_ROWS:MESSAGE, :], picks(), (((0,), (0,)), ((), ())),
-            precision=EXACT, preferred_element_type=jnp.float32,
-        )
-        near, far, height = split_rim(rim)
-        rates = row_rates(near, far, height, sign)
-        sides = [beside(near[i], corners[i * NZ:(i + 1) * NZ, :]) for i in range(NA)]
-        k_cell, k_n, k_s = near[NF], sides[NF][0], sides[NF][1]
-        k_own = diff[:, own_row, :]
-        for m in range(NF):
-            f, n, s = near[m], sides[m][0], sides[m][1]
-            own = fields[m, :, own_row, :]
-            rate = rates[m] + 0.5 * (
-                (k_cell + k_n) * (n - f) + (k_cell + k_s) * (s - f) - near[1] * (n - s)
-                + (k_cell + k_own) * (own - f) - sign * near[0] * own
-            )
-            one_out[m * NZ:(m + 1) * NZ, :] = f + TIME_STEP / 3.0 * rate
-
-    def row_of(ref, i, k):
-        return ref[pl.ds(i * NZ + k, 1), :]
-
-    def along(x, low, high):
+    def along(x):
         return (
-            jnp.where(sub == NI - 1, high, pltpu.roll(x, NI - 1, 0)),
-            jnp.where(sub == 0, low, pltpu.roll(x, 1, 0)),
-        )
-
-    def halo_tile(i, k):
-        at = pl.multiple_of((i * NZ + k) * NI, NI)
-        return halo[pl.ds(at, NI), :]
+            jnp.where(sub == NI - 1, 0.0, pltpu.roll(x, NI - 1, 0)),
+            jnp.where(sub == 0, 0.0, pltpu.roll(x, 1, 0)),
+        )
 
     high_main = heights[...].astype(jnp.float32)
-    high_halo = halo[HEIGHT_AT:HEIGHT_AT + NI, :]
+    high_halo = halo[HALO - 1]
 
     def section_one(k, _):
         up, dn = jnp.minimum(k + 1, NZ - 1), jnp.maximum(k - 1, 0)
         has_up = jnp.where(k < NZ - 1, 1.0, 0.0).astype(jnp.float32)
         has_dn = jnp.where(k > 0, 1.0, 0.0).astype(jnp.float32)
         level = k.astype(jnp.float32)
-        k_main, k_halo = diff[k], halo_tile(NF, k)
+        k_main, k_halo = diff[k], halo[NF * NZ + k]
         n, s, hn, hs = beside(k_main, k_halo)
-        e, ws = along(k_main, row_of(west, NF, k), row_of(east, NF, k))
-        he, hw = along(k_halo, row_of(corner_w, NF, k), row_of(corner_e, NF, k))
-        k_sides = (e, ws, n, s, diff[up], diff[dn])
-        kh_sides = (he, hw, hn, hs, halo_tile(NF, up), halo_tile(NF, dn))
+        k_sides = (*along(k_main), n, s, diff[up], diff[dn])
+        kh_sides = (*along(k_halo), hn, hs, halo[NF * NZ + up], halo[NF * NZ + dn])
         cells, halos = [], []
         for m in range(NF):
-            f, h = fields[m, k], halo_tile(m, k)
+            f, h = fields[m, k], halo[m * NZ + k]
             n, s, hn, hs = beside(f, h)
-            e, ws = along(f, row_of(west, m, k), row_of(east, m, k))
-            he, hw = along(h, row_of(corner_w, m, k), row_of(corner_e, m, k))
-            cells.append((f, e, ws, n, s, has_up * fields[m, up], has_dn * fields[m, dn]))
-            halos.append((h, he, hw, hn, hs, has_up * halo_tile(m, up), has_dn * halo_tile(m, dn)))
+            cells.append((f, *along(f), n, s, has_up * fields[m, up], has_dn * fields[m, dn]))
+            halos.append((h, *along(h), hn, hs, has_up * halo[m * NZ + up], has_dn * halo[m * NZ + dn]))
         drag = jnp.where(level < high_main, DRAG_COEF, 0.0)
         drag_h = jnp.where(level < high_halo, DRAG_COEF, 0.0)
         rates = rates_of(cells, k_main, k_sides, drag)
@@ -365,15 +323,13 @@
         has_up = jnp.where(k < NZ - 1, 1.0, 0.0).astype(jnp.float32)
         has_dn = jnp.where(k > 0, 1.0, 0.0).astype(jnp.float32)
         k_main = diff[k]
-        n, s, _, _ = beside(k_main, halo_tile(NF, k))
-        e, ws = along(k_main, row_of(west, NF, k), row_of(east, NF, k))
-        k_sides = (e, ws, n, s, diff[up], diff[dn])
+        n, s, _, _ = beside(k_main, halo[NF * NZ + k])
+        k_sides = (*along(k_main), n, s, diff[up], diff[dn])
         cells = []
         for m in range(NF):
             f = one[m, k]
             n, s, _, _ = beside(f, one_halo[m, k])
-            e, ws = along(f, row_of(one_w, m, k), row_of(one_e, m, k))
-            cells.append((f, e, ws, n, s, has_up * one[m, up], has_dn * one[m, dn]))
+            cells.append((f, *along(f), n, s, has_up * one[m, up], has_dn * one[m, dn]))
         drag = jnp.where(k.astype(jnp.float32) < high_main, DRAG_COEF, 0.0)
         rates = rates_of(cells, k_main, k_sides, drag)
         for m in range(NF):
@@ -383,79 +339,75 @@
     lax.fori_loop(0, NZ, section_two, 0)
     for m in range(NF):
         for r in range(3):
-            kept[m, r] = jnp.where(first, one[m, :, r, :], one[m, :, NI - 1 - r, :])
+            kept[0, m, r] = one[m, :, r, :]
+            kept[1, m, r] = one[m, :, NI - 1 - r, :]
         for r in range(2):
-            kept[m, 3 + r] = jnp.where(first, one_halo[m, :, r, :], one_halo[m, :, NI - 1 - r, :])
-
-
-def wrap_kernel(fields, diff, heights, halo, kept, wrapped, done, out, view):
-    first, final = is_first(), is_last()
+            kept[0, m, 3 + r] = one_halo[m, :, r, :]
+            kept[1, m, 3 + r] = one_halo[m, :, NI - 1 - r, :]
+
+
+def edges_kernel(fields, diff, heights, halo, kept, west, east, wrapped, done, out):
     out[...] = done[...]
-
-    @pl.when(first | final)
-    def _():
-        view[...] = halo[0:BLOCK, :].reshape(RIM, NI, NJ)
-        sign = jnp.where(first, 1.0, -1.0).astype(jnp.float32)
-        lane = iota((NZ, NJ), 1)
+    lane = iota((NZ, NJ), 1)
+    place = {0: (0, 0), 1: (0, 1), 2: (0, 2), NF: (0, 3), 3: (NZ, 0), 4: (NZ, 1)}
+
+    for side, rim, mine, sign in ((0, west, is_first(), 1.0), (1, east, is_last(), -1.0)):
+        rows = [r if side == 0 else NI - 1 - r for r in range(3)]
 
         def block_row(i, r):
-            src = diff if i == NF else fields.at[i]
-            return jnp.where(first, src[:, r, :], src[:, NI - 1 - r, :])
+            return (diff if i == NF else fields.at[i])[:, rows[r], :]
 
         def halo_row(i, r):
-            at = slice(i * NZ, (i + 1) * NZ)
-            return jnp.where(first, view[at, r, :], view[at, NI - 1 - r, :])
-
-        place = {0: (0, 0), 1: (0, 1), 2: (0, 2), NF: (0, 3), 3: (NZ, 0), 4: (NZ, 1)}
-        outer, corner = [], []
+            return halo[i * NZ:(i + 1) * NZ, rows[r], :]
+
+        outer, far, height = split_rim(rim)
+        rates = row_rates(outer, far, height, sign)
+        corner = lax.dot_general(
+            rim[EDGE_ROWS:MESSAGE, :], picks(), (((0,), (0,)), ((), ())),
+            precision=EXACT, preferred_element_type=jnp.float32,
+        )
+        corner = [corner[i * NZ:(i + 1) * NZ, :] for i in range(NA)]
+        sides = [beside(outer[i], corner[i]) for i in range(NA)]
+        k_cell, k_n, k_s = outer[NF], sides[NF][0], sides[NF][1]
+        for m in range(NF):
+            f, n, s = outer[m], sides[m][0], sides[m][1]
+            rate = rates[m] + 0.5 * ((k_cell + k_n) * (n - f) + (k_cell + k_s) * (s - f) - outer[1] * (n - s))
+            half, row = (0, 4 + m) if m < 3 else (NZ, 1 + m)
+            rates[m] = jnp.where(mine, wrapped[half:half + NZ, row, :], rate)
         for i in range(NA):
             half, row = place[i]
-            outer.append(wrapped[half:half + NZ, row, :])
+            outer[i] = jnp.where(mine, wrapped[half:half + NZ, row, :], outer[i])
             spare = wrapped[half:half + NZ, 7, :]
-            corner.append(
-                jnp.where(lane < 64, pltpu.roll(spare, (NJ - row) % NJ, 1), pltpu.roll(spare, row, 1))
-            )
+            spare = jnp.where(lane < 64, pltpu.roll(spare, (NJ - row) % NJ, 1), pltpu.roll(spare, row, 1))
+            corner[i] = jnp.where(mine, spare, corner[i])
         own = [block_row(i, 0) for i in range(NA)]
-        side = [halo_row(i, 0) for i in range(NA)]
-        one_out, one_own, one_side = [], [], []
-        for m in range(NF):
-            half, row = (0, 4 + m) if m < 3 else (NZ, 1 + m)
-            rate = wrapped[half:half + NZ, row, :] + 0.5 * (
+        beyond = [halo_row(i, 0) for i in range(NA)]
+        ones, one_halos = [], []
+        for m in range(NF):
+            rate = rates[m] + 0.5 * (
                 (outer[NF] + own[NF]) * (own[m] - outer[m]) - sign * outer[0] * own[m]
             )
-            one_out.append(outer[m] + TIME_STEP / 3.0 * rate)
+            one_out = outer[m] + TIME_STEP / 3.0 * rate
             rate = (own[NF] + outer[NF] + sign * own[0]) * outer[m] - outer[NF] * own[m]
-            one_own.append(kept[m, 0] + TIME_STEP / 6.0 * rate)
-            rate = (side[NF] + corner[NF] + sign * side[0]) * corner[m] - corner[NF] * side[m]
-            one_side.append(kept[m, 3] + TIME_STEP / 6.0 * rate)
+            one_own = kept[side, m, 0] + TIME_STEP / 6.0 * rate
+            rate = (beyond[NF] + corner[NF] + sign * beyond[0]) * corner[m] - corner[NF] * beyond[m]
+            ones.append([one_out, one_own, kept[side, m, 1], kept[side, m, 2]])
+            one_halos.append([kept[side, m, 3] + TIME_STEP / 6.0 * rate, kept[side, m, 4]])
         k_rows = [outer[NF], own[NF], block_row(NF, 1), block_row(NF, 2)]
-        k_halos = [side[NF], halo_row(NF, 1)]
-        ones = [[one_out[m], one_own[m], kept[m, 1], kept[m, 2]] for m in range(NF)]
-        one_halos = [[one_side[m], kept[m, 4]] for m in range(NF)]
+        k_halos = [beyond[NF], halo_row(NF, 1)]
         for r in range(2):
             k_cell = k_rows[r + 1]
             k_n, k_s, _, _ = beside(k_cell, k_halos[r])
-            k_up, k_dn = levels(k_cell, True)
-            k_sides = (k_rows[r + 2], k_rows[r], k_n, k_s, k_up, k_dn)
+            k_sides = (k_rows[r + 2], k_rows[r], k_n, k_s, *levels(k_cell, True))
             cells = []
             for m in range(NF):
                 f = ones[m][r + 1]
                 n, s, _, _ = beside(f, one_halos[m][r])
-                up, dn = levels(f, False)
-                cells.append((f, ones[m][r + 2], ones[m][r], n, s, up, dn))
-            height = jnp.where(first, heights[r:r + 1, :], heights[NI - 1 - r:NI - r, :])
-            drag = jnp.where(iota((NZ, NJ), 0) < height, DRAG_COEF, 0.0)
+                cells.append((f, ones[m][r + 2], ones[m][r], n, s, *levels(f, False)))
+            drag = jnp.where(iota((NZ, NJ), 0) < heights[rows[r]:rows[r] + 1, :], DRAG_COEF, 0.0)
             rates = rates_of(cells, k_cell, k_sides, drag, sign)
             for m in range(NF):
-                value = block_row(m, r) + TIME_STEP / 2.0 * rates[m]
-
-                @pl.when(first)
-                def _(value=value, m=m):
-                    out[m, :, r, :] = value
-
-                @pl.when(final)
-                def _(value=value, m=m):
-                    out[m, :, NI - 1 - r, :] = value
+                out[m, :, rows[r], :] = block_row(m, r) + TIME_STEP / 2.0 * rates[m]
 
 
 def shards(fields, diffusivity, heights, wrap_map):
@@ -475,62 +427,44 @@
     )(*block)
 
     half_x = count_x // 2
-    early_rows = [0, half_x]
-    rest = [r for r in range(count_x) if r not in early_rows]
-    low = [(i, i + 1) for i in range(0, count_y, 2)]
-    high = [(i, (i + 1) % count_y) for i in range(1, count_y, 2)]
-
-    def spanwise(early, rows, *after):
-        tied = lax.optimization_barrier((*block, *after))[:3]
-        to_a, to_b = call(functools.partial(pack_kernel, early), (pack, pack), *tied, name="pack")
-
-        def swap(x, pairs):
-            pairs = [(r * count_y + i, r * count_y + j) for r in rows for i, j in pairs]
-            return lax.ppermute(x, ("gx", "gy"), pairs + [(j, i) for i, j in pairs])
-
-        from_b = swap(to_b, high)
-        return swap(to_a, low), from_b
-
-    early_a, early_b = spanwise(True, early_rows, packets)
-    packets, early_a, early_b = lax.optimization_barrier((packets, early_a, early_b))
-
     row_pairs = [(0, last), (half_x, half_x - 1)] + [(i, i + half_x) for i in range(1, half_x - 1)]
     groups = [[r * count_y + i for r in rows for i in range(count_y)] for rows in row_pairs]
     rows = lax.all_to_all(packets, ("gx", "gy"), 0, 0, axis_index_groups=groups)
 
-    late_a, late_b = spanwise(False, rest, packets)
+    low = [(i, i + 1) for i in range(0, count_y, 2)]
+    high = [(i, (i + 1) % count_y) for i in range(1, count_y, 2)]
+    tied = lax.optimization_barrier((*block, packets))[:3]
+    to_a, to_b = call(pack_kernel, (pack, pack), *tied, name="pack")
+    from_b = lax.ppermute(to_b, "gy", high + [(j, i) for i, j in high])
+    from_a = lax.ppermute(to_a, "gy", low + [(j, i) for i, j in low])
+
+    wrap = wrap_map.reshape(count_y, NJ)
+    inverse = call(
+        inverse_kernel, jax.ShapeDtypeStruct((count_y, NJ), jnp.int32), wrap, name="inverse"
+    )
+    rows, inverse, from_a, from_b = lax.optimization_barrier((rows, inverse, from_a, from_b))
+    moved = call(
+        permute_kernel, f32(count_y, 8, NJ), rows, wrap, inverse, name="permute",
+        scratch=[pltpu.VMEM((384, 32 * NJ), jnp.bfloat16), pltpu.VMEM((256, 32 * NJ), jnp.bfloat16)],
+    )
+    wrapped = lax.all_to_all(moved, "gy", 0, 0)
+
     message = f32(MESSAGE, NJ)
     halo, to_east, to_west = call(
-        unpack_kernel, (f32(PACK, NJ), message, message),
-        early_a, early_b, late_a, late_b, *block, name="unpack",
-        scratch=[pltpu.VMEM((RIM, NI, NJ), jnp.float32)],
-    )
+        unpack_kernel, (f32(HALO, NI, NJ), message, message),
+        from_a, from_b, *block, name="unpack",
+            )
     east_pairs = [(i, i + 1) for i in range(last) if i + 1 != half_x]
     west = lax.ppermute(to_east, "gx", east_pairs)
     east = lax.ppermute(to_west, "gx", [(j, i) for i, j in east_pairs])
 
-    wrap = wrap_map.reshape(count_y, NJ)
-    inverse = call(
-        inverse_kernel, jax.ShapeDtypeStruct((count_y, NJ), jnp.int32), wrap, name="inverse"
-    )
-    rows, inverse, *_ = lax.optimization_barrier((rows, inverse, to_east, to_west))
-    moved = call(
-        permute_kernel, f32(count_y, 8, NJ), rows, wrap, inverse, name="permute",
-        scratch=[pltpu.VMEM((384, 32 * NJ), jnp.bfloat16), pltpu.VMEM((256, 32 * NJ), jnp.bfloat16)],
-    )
-    moved, west, east = lax.optimization_barrier((moved, west, east))
-    wrapped = lax.all_to_all(moved, "gy", 0, 0)
-
     state = pltpu.VMEM((NF, NZ, NI, NJ), jnp.float32)
-    line = pltpu.VMEM((RIM, NJ), jnp.float32)
-    corner = pltpu.VMEM((NJ, NJ), jnp.float32)
     done, kept = call(
-        sections_kernel, (f32(NF, NZ, NI, NJ), f32(NF, 5, NZ, NJ)),
-        *block, west, east, halo, name="sections", scratch=[state, state, line, line, corner, corner],
+        sections_kernel, (f32(NF, NZ, NI, NJ), f32(2, NF, 5, NZ, NJ)),
+        *block, halo, name="sections", scratch=[state, state],
     )
     return call(
-        wrap_kernel, f32(NF, NZ, NI, NJ), *block, halo, kept, wrapped, done, name="wrapped_rows",
-        scratch=[pltpu.VMEM((RIM, NI, NJ), jnp.float32)],
+        edges_kernel, f32(NF, NZ, NI, NJ), *block, halo, kept, west, east, wrapped, done, name="edges"
     )
 
 

time: 61.4 us -> 58 us (0.945); the launches traced: 60.2 us -> 57.7 us
  waiting for transfers between devices: 16.7 us -> 8.31 us
  starting transfers between devices: 28.7 us -> 34.9 us
    all_to_all x1, starting transfers between devices: 6.18 us -> 20 us  [shards(): rows = lax.all_to_all(packets, ('gx', 'gy'), 0, 0, axis_index_groups=groups)]
    ppermute x4 -> x2, starting transfers between devices: 12 us -> 7.1 us  [the longest x1 4.74 us: shards(): from_b = lax.ppermute(to_b, 'gy', high + [(j, i) for i, j in high])]
    all_to_all x1, waiting for transfers between devices: 5.89 us -> 1.75 us  [shards(): wrapped = lax.all_to_all(moved, 'gy', 0, 0)]
    ppermute x4 -> x2, waiting for transfers between devices: 4.6 us -> 1.45 us  [the longest x1 1.45 us: shards(): from_b = lax.ppermute(to_b, 'gy', high + [(j, i) for i, j in high])]
    ppermute x1, starting transfers between devices: 3.58 us -> 1.29 us  [shards(): west = lax.ppermute(to_east, 'gx', east_pairs)]
    all_to_all x1, waiting for transfers between devices: 6.24 us -> 4.55 us  [shards(): rows = lax.all_to_all(packets, ('gx', 'gy'), 0, 0, axis_index_groups=groups)]
    pallas_call x7 -> x6, Pallas kernels: 12.5 us -> 12.2 us  [call(): pl.pallas_call(kernel, out_shape=outs, in_specs=[VMEM] * len(args), out_s...]
  transfers between devices with their start and end apart: 8 -> 6, of which waited for: 3 -> 4; matrix products, arithmetic and copies ran while one was open for 0% -> 0% of each run, Pallas kernels for 17% -> 13%
where the time goes in v3:
time: 58 us; the launch traced here: 57.7 us
  starting transfers between devices  34.9 us (60%)
  Pallas kernels  14.2 us (24%)
  waiting for transfers between devices  8.31 us (14%)
    all_to_all x1, starting transfers between devices, shards(): rows = lax.all_to_all(packets, ('gx', 'gy'), 0, 0, axis_index_groups=groups)  20 us
    pallas_call x6, Pallas kernels, call(): pl.pallas_call(kernel, out_shape=outs, in_specs=[VMEM] * len(args), out_s...  12.2 us
    all_to_all x1, starting transfers between devices, shards(): wrapped = lax.all_to_all(moved, 'gy', 0, 0)  5.29 us
    ppermute x1, starting transfers between devices, shards(): from_b = lax.ppermute(to_b, 'gy', high + [(j, i) for i, j in high])  4.74 us
    all_to_all x1, waiting for transfers between devices, shards(): rows = lax.all_to_all(packets, ('gx', 'gy'), 0, 0, axis_index_groups=groups)  4.55 us
    ppermute x1, starting transfers between devices, shards(): from_a = lax.ppermute(to_a, 'gy', low + [(j, i) for i, j in low])  2.36 us
    pallas_call x1, Pallas kernels, shards(): pl.pallas_call(packet_kernel, out_shape=f32(2 * count_y, 8, NJ), in_specs...  2.05 us
    all_to_all x1, waiting for transfers between devices, shards(): wrapped = lax.all_to_all(moved, 'gy', 0, 0)  1.75 us
  transfers between devices with their start and end apart: 6, of which 4 were waited for; matrix products, arithmetic and copies ran while one was open for 0% of the time, Pallas kernels for 13%

profile of v3, /device:TPU:1, one launch (start us, length us, event | category | flops | bytes accessed | tf_op | source)
XLA Modules:
  0.0 57.7 jit_solution(7196212973676469827)
XLA Ops:
  0.0 0.0 copy-start
  0.0 2.0 %packets.1 = f32[64,8,128]{2,1,0:T(8,128)} custom-call(f32[5,16,16,128]{3,2,1,0:T(8,128)} %fields.6, f32[16,16,128]{2,1,0:T(8,128)} %diff.6, s32[16,128]{1,0:T(8,128)} %heights.6), custom_call_target="tpu_custom_call" | custom-call | tf_op jit(solution)/shard_map/packets/pallas_call | solution.py:419
  2.1 0.0 copy-start.1
  2.1 0.0 copy-start.2
  2.1 20.0 %all-to-all-start = ((f32[64,8,128]{2,1,0:T(8,128)}), f32[64,8,128]{2,1,0:T(8,128)S(1)}, u32[]{:S(2)}, u32[]{:S(2)}) async-start(f32[64,8,128]{2,1,0:T(8,128)} %packets.1), calls=%async_computation | async-start | bytes 524288 | tf_op jit(solution)/shard_map/all_to_all | solution.py:432
  22.1 0.0 copy-done
  22.1 0.0 copy-done.1
  22.1 0.0 copy-done.2
  22.1 0.0 copy-start.3
  22.1 0.7 %pack.1 = (f32[2,1664]{1,0:T(2,128)S(1)}, f32[2,1664]{1,0:T(2,128)S(1)}) custom-call(f32[5,16,16,128]{3,2,1,0:T(8,128)S(1)} %copy-done, f32[16,16,128]{2,1,0:T(8,128)S(1)} %copy-done.1, s32[16,128]{1,0:T(8,128)S(1)} %copy-done.2), custom_call_target="tpu_custom_call" | custom-call | tf_op jit(solution)/shard_map/pack/pallas_call | solution.py:35
  22.9 2.4 %collective-permute-start = (f32[2,1664]{1,0:T(2,128)S(1)}, f32[2,1664]{1,0:T(2,128)S(1)}, u32[]{:S(2)}, u32[]{:S(2)}) collective-permute-start(f32[2,1664]{1,0:T(2,128)S(1)} %get-tuple-element.22), channel_id=1, source_target_pairs={{0,1},{2,3},{4,5},{6,7},{8,9},{10,11},{12,13},{14,15},{16,17},{18,... | collective-permute-start | bytes 39944 | tf_op jit(solution)/shard_map/ppermute | solution.py:439
  25.2 4.7 %collective-permute-start.1 = (f32[2,1664]{1,0:T(2,128)S(1)}, f32[2,1664]{1,0:T(2,128)S(1)}, u32[]{:S(2)}, u32[]{:S(2)}) collective-permute-start(f32[2,1664]{1,0:T(2,128)S(1)} %get-tuple-element.23), channel_id=1, source_target_pairs={{1,2},{3,4},{5,6},{7,8},{9,10},{11,12},{13,14},{15,16},{17,18},{19... | collective-permute-start | bytes 39944 | tf_op jit(solution)/shard_map/ppermute | solution.py:438
  30.0 0.0 copy-done.3
  30.0 0.8 %inverse.1 = s32[32,128]{1,0:T(8,128)S(1)} custom-call(s32[32,128]{1,0:T(8,128)S(1)} %bitcast.1), custom_call_target="tpu_custom_call" | custom-call | tf_op jit(solution)/shard_map/inverse/pallas_call | solution.py:35
  30.8 0.0 collective-permute-done.from_a
  30.8 1.5 %collective-permute-done.1.from_b = f32[2,1664]{1,0:T(2,128)S(1)} collective-permute-done((f32[2,1664]{1,0:T(2,128)S(1)}, f32[2,1664]{1,0:T(2,128)S(1)}, u32[]{:S(2)}, u32[]{:S(2)}) %collective-permute-start.1) | collective-permute-done | bytes 13344 | tf_op jit(solution)/shard_map/ppermute | solution.py:438
  32.3 4.5 %all-to-all-done.rows = f32[64,8,128]{2,1,0:T(8,128)S(1)} async-done(((f32[64,8,128]{2,1,0:T(8,128)}), f32[64,8,128]{2,1,0:T(8,128)S(1)}, u32[]{:S(2)}, u32[]{:S(2)}) %all-to-all-start) | async-done | bytes 262176 | tf_op jit(solution)/shard_map/all_to_all | solution.py:432
  36.8 3.0 %permute.1 = f32[32,8,128]{2,1,0:T(8,128)} custom-call(f32[64,8,128]{2,1,0:T(8,128)S(1)} %all-to-all-done.rows, s32[32,128]{1,0:T(8,128)S(1)} %bitcast.2, s32[32,128]{1,0:T(8,128)S(1)} %inverse.1), custom_call_target="tpu_custom_call" | custom-call | tf_op jit(solution)/shard_map/permute/pallas_call | solution.py:35
  39.8 5.3 %all-to-all-start.1 = ((f32[32,8,128]{2,1,0:T(8,128)}), f32[32,8,128]{2,1,0:T(8,128)S(1)}, u32[]{:S(2)}, u32[]{:S(2)}) async-start(f32[32,8,128]{2,1,0:T(8,128)} %permute.1), calls=%async_computation.1 | async-start | bytes 262144 | tf_op jit(solution)/shard_map/all_to_all | solution.py:450
  45.1 1.5 %unpack.1 = (f32[97,16,128]{2,1,0:T(8,128)S(1)}, f32[208,128]{1,0:T(8,128)S(1)}, f32[208,128]{1,0:T(8,128)S(1)}) custom-call(f32[2,1664]{1,0:T(2,128)S(1)} %collective-permute-done.from_a, f32[2,1664]{1,0:T(2,128)S(1)} %collective-permute-done.1.from_b, f32[5,16,16,128]{3,2,1,0:T(8,128)S(1)} %copy-done, f32[16,16,128]{2,1,0:T(8,128)S(1)} %copy-done.1, ...), custom_call_target="tpu_custom_call" | custom-call | tf_op jit(solution)/shard_map/unpack/pallas_call | solution.py:35
  46.6 1.3 %collective-permute-start.2 = (f32[208,128]{1,0:T(8,128)S(1)}, f32[208,128]{1,0:T(8,128)S(1)}, u32[]{:S(2)}, u32[]{:S(2)}) collective-permute-start(f32[208,128]{1,0:T(8,128)S(1)} %get-tuple-element.28), channel_id=1, source_target_pairs={{0,32},{32,64},{64,96},{96,128},{128,160},{160,192},{192,224},{256... | collective-permute-start | bytes 319496 | tf_op jit(solution)/shard_map/ppermute | solution.py:458
  47.9 1.3 %collective-permute-start.3 = (f32[208,128]{1,0:T(8,128)S(1)}, f32[208,128]{1,0:T(8,128)S(1)}, u32[]{:S(2)}, u32[]{:S(2)}) collective-permute-start(f32[208,128]{1,0:T(8,128)S(1)} %get-tuple-element.29), channel_id=1, source_target_pairs={{32,0},{64,32},{96,64},{128,96},{160,128},{192,160},{224,192},{288... | collective-permute-start | bytes 319496 | tf_op jit(solution)/shard_map/ppermute | solution.py:459
  49.2 4.4 %sections.1 = (f32[5,16,16,128]{3,2,1,0:T(8,128)S(1)}, f32[2,5,5,16,128]{4,3,2,1,0:T(8,128)S(1)}) custom-call(f32[5,16,16,128]{3,2,1,0:T(8,128)S(1)} %copy-done, f32[16,16,128]{2,1,0:T(8,128)S(1)} %copy-done.1, s32[16,128]{1,0:T(8,128)S(1)} %copy-done.2, f32[97,16,128]{2,1,0:T(8,128)S(1)} %get-tuple-element.26.halo), custom_call_target="tpu_custom_call" | custom-call | tf_op jit(solution)/shard_map/sections/pallas_call | solution.py:35
  53.5 0.0 collective-permute-done.2.west
  53.6 0.5 collective-permute-done.3.east
  54.1 1.8 %all-to-all-done.1.wrapped = f32[32,8,128]{2,1,0:T(8,128)S(1)} async-done(((f32[32,8,128]{2,1,0:T(8,128)}), f32[32,8,128]{2,1,0:T(8,128)S(1)}, u32[]{:S(2)}, u32[]{:S(2)}) %all-to-all-start.1) | async-done | bytes 131104 | tf_op jit(solution)/shard_map/all_to_all | solution.py:450
  55.9 1.8 %edges.1 = f32[5,16,16,128]{3,2,1,0:T(8,128)} custom-call(f32[5,16,16,128]{3,2,1,0:T(8,128)S(1)} %copy-done, f32[16,16,128]{2,1,0:T(8,128)S(1)} %copy-done.1, s32[16,128]{1,0:T(8,128)S(1)} %copy-done.2, f32[97,16,128]{2,1,0:T(8,128)S(1)} %get-tuple-element.26.halo, f32[2,5,5,16,128]{4,3,2,1,0:T(8,128)S(1)} %get-tuple-element.27.kept, ...), custom_call_target="tpu_custom_call" | custom-call | tf_op jit(solution)/shard_map/edges/pallas_call | solution.py:35
Async XLA Ops:
  0.0 22.1 %copy-start = (f32[5,16,16,128]{3,2,1,0:T(8,128)S(1)}, f32[5,16,16,128]{3,2,1,0:T(8,128)}, u32[]{:S(2)}) copy-start(f32[5,16,16,128]{3,2,1,0:T(8,128)} %fields.6) | copy-start | bytes 1966084
  2.1 20.0 %copy-start.1 = (f32[16,16,128]{2,1,0:T(8,128)S(1)}, f32[16,16,128]{2,1,0:T(8,128)}, u32[]{:S(2)}) copy-start(f32[16,16,128]{2,1,0:T(8,128)} %diff.6) | copy-start | bytes 393220
  2.1 20.0 %copy-start.2 = (s32[16,128]{1,0:T(8,128)S(1)}, s32[16,128]{1,0:T(8,128)}, u32[]{:S(2)}) copy-start(s32[16,128]{1,0:T(8,128)} %heights.6) | copy-start | bytes 24580
  2.1 34.7 %all-to-all-start = ((f32[64,8,128]{2,1,0:T(8,128)}), f32[64,8,128]{2,1,0:T(8,128)S(1)}, u32[]{:S(2)}, u32[]{:S(2)}) async-start(f32[64,8,128]{2,1,0:T(8,128)} %packets.1), calls=%async_computation | async-start | bytes 524288 | tf_op jit(solution)/shard_map/all_to_all | solution.py:432
  22.1 7.9 %copy-start.3 = (s32[4096]{0:T(1024)S(1)}, s32[4096]{0:T(1024)}, u32[]{:S(2)}) copy-start(s32[4096]{0:T(1024)} %param.7) | copy-start | bytes 49156
  22.9 7.9 %collective-permute-start = (f32[2,1664]{1,0:T(2,128)S(1)}, f32[2,1664]{1,0:T(2,128)S(1)}, u32[]{:S(2)}, u32[]{:S(2)}) collective-permute-start(f32[2,1664]{1,0:T(2,128)S(1)} %get-tuple-element.22), channel_id=1, source_target_pairs={{0,1},{2,3},{4,5},{6,7},{8,9},{10,11},{12,13},{14,15},{16,17},{18,... | collective-permute-start | bytes 39944 | tf_op jit(solution)/shard_map/ppermute | solution.py:439
  25.2 7.0 %collective-permute-start.1 = (f32[2,1664]{1,0:T(2,128)S(1)}, f32[2,1664]{1,0:T(2,128)S(1)}, u32[]{:S(2)}, u32[]{:S(2)}) collective-permute-start(f32[2,1664]{1,0:T(2,128)S(1)} %get-tuple-element.23), channel_id=1, source_target_pairs={{1,2},{3,4},{5,6},{7,8},{9,10},{11,12},{13,14},{15,16},{17,18},{19... | collective-permute-start | bytes 39944 | tf_op jit(solution)/shard_map/ppermute | solution.py:438
  39.8 16.1 %all-to-all-start.1 = ((f32[32,8,128]{2,1,0:T(8,128)}), f32[32,8,128]{2,1,0:T(8,128)S(1)}, u32[]{:S(2)}, u32[]{:S(2)}) async-start(f32[32,8,128]{2,1,0:T(8,128)} %permute.1), calls=%async_computation.1 | async-start | bytes 262144 | tf_op jit(solution)/shard_map/all_to_all | solution.py:450
  46.6 7.0 %collective-permute-start.2 = (f32[208,128]{1,0:T(8,128)S(1)}, f32[208,128]{1,0:T(8,128)S(1)}, u32[]{:S(2)}, u32[]{:S(2)}) collective-permute-start(f32[208,128]{1,0:T(8,128)S(1)} %get-tuple-element.28), channel_id=1, source_target_pairs={{0,32},{32,64},{64,96},{96,128},{128,160},{160,192},{192,224},{256... | collective-permute-start | bytes 319496 | tf_op jit(solution)/shard_map/ppermute | solution.py:458
  47.9 6.2 %collective-permute-start.3 = (f32[208,128]{1,0:T(8,128)S(1)}, f32[208,128]{1,0:T(8,128)S(1)}, u32[]{:S(2)}, u32[]{:S(2)}) collective-permute-start(f32[208,128]{1,0:T(8,128)S(1)} %get-tuple-element.29), channel_id=1, source_target_pairs={{32,0},{64,32},{96,64},{128,96},{160,128},{192,160},{224,192},{288... | collective-permute-start | bytes 319496 | tf_op jit(solution)/shard_map/ppermute | solution.py:459

commit v4 on v3

--- a/solution.py
+++ b/solution.py
@@ -22,6 +22,8 @@
 PACK = BLOCK + 128
 HEIGHT_AT = BLOCK
 HALO = RIM + 1
+
+LEAD = 16
 
 VMEM = pl.BlockSpec(memory_space=pltpu.VMEM)
 EXACT = lax.Precision.HIGHEST
@@ -168,24 +170,26 @@
     zero = jnp.zeros((NZ, NJ), jnp.float32)
     lower = [near[0], near[1], near[2], near[NF], rates[0], rates[1], rates[2], zero]
     upper = [near[3], near[4], near[1], near[NF], rates[3], rates[4], zero, zero]
-    at = jnp.where(late, 0, 2 * NZ)
+    at = jnp.where(late, 2 * NZ, 0)
     for row in range(8):
         out[pl.ds(at, NZ), row, :] = lower[row]
         out[pl.ds(at + NZ, NZ), row, :] = upper[row]
 
 
 def inverse_kernel(wrap, out):
-    total = jnp.zeros((64, NJ), jnp.float32)
-    lane = iota((32, NJ), 1).astype(jnp.float32)
-    for s in range(32):
-        p = wrap[s:s + 1, :]
-        hit = jnp.where(iota((32, NJ), 0) == p // NJ, 1.0, 0.0)
-        low = jnp.where(iota((NJ, NJ), 0) == lax.rem(p, NJ), 1.0, 0.0).astype(jnp.bfloat16)
-        left = jnp.concatenate([hit * lane, hit * float(s)], 0).astype(jnp.bfloat16)
-        total = total + lax.dot_general(
-            left, low, (((1,), (1,)), ((), ())), preferred_element_type=jnp.float32
-        )
-    out[...] = (total[0:32, :] + NJ * total[32:64, :]).astype(jnp.int32)
+    @pl.when(is_last())
+    def _():
+        total = jnp.zeros((64, NJ), jnp.float32)
+        lane = iota((32, NJ), 1).astype(jnp.float32)
+        for s in range(32):
+            p = wrap[s:s + 1, :]
+            hit = jnp.where(iota((32, NJ), 0) == p // NJ, 1.0, 0.0)
+            low = jnp.where(iota((NJ, NJ), 0) == lax.rem(p, NJ), 1.0, 0.0).astype(jnp.bfloat16)
+            left = jnp.concatenate([hit * lane, hit * float(s)], 0).astype(jnp.bfloat16)
+            total = total + lax.dot_general(
+                left, low, (((1,), (1,)), ((), ())), preferred_element_type=jnp.float32
+            )
+        out[...] = (total[0:32, :] + NJ * total[32:64, :]).astype(jnp.int32)
 
 
 def permute_kernel(rows, wrap, inverse, out, left_side, right_side):
@@ -193,8 +197,9 @@
     target = jnp.where(first, wrap[...], inverse[...])
     column = iota(target.shape, 0) * NJ + iota(target.shape, 1)
     target = jnp.where((gx == half) | (gx == half - 1), column, target)
-    upper = lax.axis_index("gy") >= NZ
-    x = jnp.where(first, rows[32:64], rows[0:32])
+    upper = lax.axis_index("gy") < LEAD
+    x = rows[pl.ds(jnp.where(first, 0, 32), 32)]
+    x = jnp.concatenate([x[32 - LEAD:], x[:32 - LEAD]], 0)
     lane, sub = iota(x.shape, 2), iota(x.shape, 1)
 
     def after(y):
@@ -240,7 +245,8 @@
         corner = jnp.where(lane < 64, pltpu.roll(later, r, 2), pltpu.roll(prior, (NJ - r) % NJ, 2))
         corner = pltpu.roll(corner, 7 - r, 1)
         last = jnp.where((lane == r) | (lane == NJ - 1 - r), corner, last)
-    out[...] = jnp.where(sub == 7, last, y)
+    y = jnp.where(sub == 7, last, y)
+    out[...] = y
 
 
 def beside(m, h):
@@ -346,68 +352,87 @@
             kept[1, m, 3 + r] = one_halo[m, :, NI - 1 - r, :]
 
 
-def edges_kernel(fields, diff, heights, halo, kept, west, east, wrapped, done, out):
+def redo_side(side, outer, corner, rates, fields, diff, heights, halo, kept, out):
+    sign = 1.0 if side == 0 else -1.0
+    rows = [r if side == 0 else NI - 1 - r for r in range(3)]
+
+    def block_row(i, r):
+        return (diff if i == NF else fields.at[i])[:, rows[r], :]
+
+    def halo_row(i, r):
+        return halo[i * NZ:(i + 1) * NZ, rows[r], :]
+
+    own = [block_row(i, 0) for i in range(NA)]
+    beyond = [halo_row(i, 0) for i in range(NA)]
+    ones, one_halos = [], []
+    for m in range(NF):
+        rate = rates[m] + 0.5 * (
+            (outer[NF] + own[NF]) * (own[m] - outer[m]) - sign * outer[0] * own[m]
+        )
+        one_out = outer[m] + TIME_STEP / 3.0 * rate
+        rate = (own[NF] + outer[NF] + sign * own[0]) * outer[m] - outer[NF] * own[m]
+        one_own = kept[side, m, 0] + TIME_STEP / 6.0 * rate
+        rate = (beyond[NF] + corner[NF] + sign * beyond[0]) * corner[m] - corner[NF] * beyond[m]
+        ones.append([one_out, one_own, kept[side, m, 1], kept[side, m, 2]])
+        one_halos.append([kept[side, m, 3] + TIME_STEP / 6.0 * rate, kept[side, m, 4]])
+    k_rows = [outer[NF], own[NF], block_row(NF, 1), block_row(NF, 2)]
+    k_halos = [beyond[NF], halo_row(NF, 1)]
+    for r in range(2):
+        k_cell = k_rows[r + 1]
+        k_n, k_s, _, _ = beside(k_cell, k_halos[r])
+        k_sides = (k_rows[r + 2], k_rows[r], k_n, k_s, *levels(k_cell, True))
+        cells = []
+        for m in range(NF):
+            f = ones[m][r + 1]
+            n, s, _, _ = beside(f, one_halos[m][r])
+            cells.append((f, ones[m][r + 2], ones[m][r], n, s, *levels(f, False)))
+        drag = jnp.where(iota((NZ, NJ), 0) < heights[rows[r]:rows[r] + 1, :], DRAG_COEF, 0.0)
+        rates = rates_of(cells, k_cell, k_sides, drag, sign)
+        for m in range(NF):
+            out[m, :, rows[r], :] = block_row(m, r) + TIME_STEP / 2.0 * rates[m]
+
+
+def edges_kernel(fields, diff, heights, halo, kept, west, east, done, out):
+    out[...] = done[...]
+    for side, rim, beyond_wrap, sign in ((0, west, is_first(), 1.0), (1, east, is_last(), -1.0)):
+        @pl.when(jnp.logical_not(beyond_wrap))
+        def _(side=side, rim=rim, sign=sign):
+            outer, far, height = split_rim(rim)
+            rates = row_rates(outer, far, height, sign)
+            corner = lax.dot_general(
+                rim[EDGE_ROWS:MESSAGE, :], picks(), (((0,), (0,)), ((), ())),
+                precision=EXACT, preferred_element_type=jnp.float32,
+            )
+            corner = [corner[i * NZ:(i + 1) * NZ, :] for i in range(NA)]
+            sides = [beside(outer[i], corner[i]) for i in range(NA)]
+            k_cell, k_n, k_s = outer[NF], sides[NF][0], sides[NF][1]
+            for m in range(NF):
+                f, n, s = outer[m], sides[m][0], sides[m][1]
+                rates[m] = rates[m] + 0.5 * (
+                    (k_cell + k_n) * (n - f) + (k_cell + k_s) * (s - f) - outer[1] * (n - s)
+                )
+            redo_side(side, outer, corner, rates, fields, diff, heights, halo, kept, out)
+
+
+def wrap_kernel(fields, diff, heights, halo, kept, wrapped, done, out):
     out[...] = done[...]
     lane = iota((NZ, NJ), 1)
-    place = {0: (0, 0), 1: (0, 1), 2: (0, 2), NF: (0, 3), 3: (NZ, 0), 4: (NZ, 1)}
-
-    for side, rim, mine, sign in ((0, west, is_first(), 1.0), (1, east, is_last(), -1.0)):
-        rows = [r if side == 0 else NI - 1 - r for r in range(3)]
-
-        def block_row(i, r):
-            return (diff if i == NF else fields.at[i])[:, rows[r], :]
-
-        def halo_row(i, r):
-            return halo[i * NZ:(i + 1) * NZ, rows[r], :]
-
-        outer, far, height = split_rim(rim)
-        rates = row_rates(outer, far, height, sign)
-        corner = lax.dot_general(
-            rim[EDGE_ROWS:MESSAGE, :], picks(), (((0,), (0,)), ((), ())),
-            precision=EXACT, preferred_element_type=jnp.float32,
-        )
-        corner = [corner[i * NZ:(i + 1) * NZ, :] for i in range(NA)]
-        sides = [beside(outer[i], corner[i]) for i in range(NA)]
-        k_cell, k_n, k_s = outer[NF], sides[NF][0], sides[NF][1]
-        for m in range(NF):
-            f, n, s = outer[m], sides[m][0], sides[m][1]
-            rate = rates[m] + 0.5 * ((k_cell + k_n) * (n - f) + (k_cell + k_s) * (s - f) - outer[1] * (n - s))
-            half, row = (0, 4 + m) if m < 3 else (NZ, 1 + m)
-            rates[m] = jnp.where(mine, wrapped[half:half + NZ, row, :], rate)
-        for i in range(NA):
-            half, row = place[i]
-            outer[i] = jnp.where(mine, wrapped[half:half + NZ, row, :], outer[i])
-            spare = wrapped[half:half + NZ, 7, :]
-            spare = jnp.where(lane < 64, pltpu.roll(spare, (NJ - row) % NJ, 1), pltpu.roll(spare, row, 1))
-            corner[i] = jnp.where(mine, spare, corner[i])
-        own = [block_row(i, 0) for i in range(NA)]
-        beyond = [halo_row(i, 0) for i in range(NA)]
-        ones, one_halos = [], []
-        for m in range(NF):
-            rate = rates[m] + 0.5 * (
-                (outer[NF] + own[NF]) * (own[m] - outer[m]) - sign * outer[0] * own[m]
-            )
-            one_out = outer[m] + TIME_STEP / 3.0 * rate
-            rate = (own[NF] + outer[NF] + sign * own[0]) * outer[m] - outer[NF] * own[m]
-            one_own = kept[side, m, 0] + TIME_STEP / 6.0 * rate
-            rate = (beyond[NF] + corner[NF] + sign * beyond[0]) * corner[m] - corner[NF] * beyond[m]
-            ones.append([one_out, one_own, kept[side, m, 1], kept[side, m, 2]])
-            one_halos.append([kept[side, m, 3] + TIME_STEP / 6.0 * rate, kept[side, m, 4]])
-        k_rows = [outer[NF], own[NF], block_row(NF, 1), block_row(NF, 2)]
-        k_halos = [beyond[NF], halo_row(NF, 1)]
-        for r in range(2):
-            k_cell = k_rows[r + 1]
-            k_n, k_s, _, _ = beside(k_cell, k_halos[r])
-            k_sides = (k_rows[r + 2], k_rows[r], k_n, k_s, *levels(k_cell, True))
-            cells = []
+    place = {0: (LEAD, 0), 1: (LEAD, 1), 2: (LEAD, 2), NF: (LEAD, 3), 3: (0, 0), 4: (0, 1)}
+    for side, mine in ((0, is_first()), (1, is_last())):
+        @pl.when(mine)
+        def _(side=side):
+            rates, outer, corner = [], [], []
             for m in range(NF):
-                f = ones[m][r + 1]
-                n, s, _, _ = beside(f, one_halos[m][r])
-                cells.append((f, ones[m][r + 2], ones[m][r], n, s, *levels(f, False)))
-            drag = jnp.where(iota((NZ, NJ), 0) < heights[rows[r]:rows[r] + 1, :], DRAG_COEF, 0.0)
-            rates = rates_of(cells, k_cell, k_sides, drag, sign)
-            for m in range(NF):
-                out[m, :, rows[r], :] = block_row(m, r) + TIME_STEP / 2.0 * rates[m]
+                half, row = (LEAD, 4 + m) if m < 3 else (0, 1 + m)
+                rates.append(wrapped[half:half + NZ, row, :])
+            for i in range(NA):
+                half, row = place[i]
+                outer.append(wrapped[half:half + NZ, row, :])
+                spare = wrapped[half:half + NZ, 7, :]
+                corner.append(
+                    jnp.where(lane < 64, pltpu.roll(spare, (NJ - row) % NJ, 1), pltpu.roll(spare, row, 1))
+                )
+            redo_side(side, outer, corner, rates, fields, diff, heights, halo, kept, out)
 
 
 def shards(fields, diffusivity, heights, wrap_map):
@@ -428,7 +453,10 @@
 
     half_x = count_x // 2
     row_pairs = [(0, last), (half_x, half_x - 1)] + [(i, i + half_x) for i in range(1, half_x - 1)]
-    groups = [[r * count_y + i for r in rows for i in range(count_y)] for rows in row_pairs]
+    def line(*rows):
+        return [r * count_y + (i + LEAD) % count_y for r in rows for i in range(count_y)]
+
+    groups = [line(b, a) for a, b in row_pairs]
     rows = lax.all_to_all(packets, ("gx", "gy"), 0, 0, axis_index_groups=groups)
 
     low = [(i, i + 1) for i in range(0, count_y, 2)]
@@ -442,11 +470,12 @@
     inverse = call(
         inverse_kernel, jax.ShapeDtypeStruct((count_y, NJ), jnp.int32), wrap, name="inverse"
     )
-    rows, inverse, from_a, from_b = lax.optimization_barrier((rows, inverse, from_a, from_b))
+    rows, inverse, from_a = lax.optimization_barrier((rows, inverse, from_a))
     moved = call(
         permute_kernel, f32(count_y, 8, NJ), rows, wrap, inverse, name="permute",
         scratch=[pltpu.VMEM((384, 32 * NJ), jnp.bfloat16), pltpu.VMEM((256, 32 * NJ), jnp.bfloat16)],
     )
+    moved, from_b = lax.optimization_barrier((moved, from_b))
     wrapped = lax.all_to_all(moved, "gy", 0, 0)
 
     message = f32(MESSAGE, NJ)
@@ -463,8 +492,11 @@
         sections_kernel, (f32(NF, NZ, NI, NJ), f32(2, NF, 5, NZ, NJ)),
         *block, halo, name="sections", scratch=[state, state],
     )
+    done = call(
+        edges_kernel, f32(NF, NZ, NI, NJ), *block, halo, kept, west, east, done, name="edges"
+    )
     return call(
-        edges_kernel, f32(NF, NZ, NI, NJ), *block, halo, kept, west, east, wrapped, done, name="edges"
+        wrap_kernel, f32(NF, NZ, NI, NJ), *block, halo, kept, wrapped, done, name="wrapped_rows"
     )
 
 

time: 58 us -> 54.8 us (0.945)
  waiting for transfers between devices: 8.31 us -> 3.36 us
  starting transfers between devices: 34.9 us -> 37.4 us
  Pallas kernels: 14.2 us -> 13.5 us
    all_to_all x1, waiting for transfers between devices: 4.55 us -> 1.55 us  [shards(): rows = lax.all_to_all(packets, ('gx', 'gy'), 0, 0, axis_index_groups=groups)]
    all_to_all x1, starting transfers between devices: 5.29 us -> 7.77 us  [shards(): wrapped = lax.all_to_all(moved, 'gy', 0, 0)]
    ppermute x1, waiting for transfers between devices: 1.45 us -> 0.01 us  [shards(): from_b = lax.ppermute(to_b, 'gy', high + [(j, i) for i, j in high])]
    all_to_all x1, starting transfers between devices: 20 us -> 21 us  [shards(): rows = lax.all_to_all(packets, ('gx', 'gy'), 0, 0, axis_index_groups=groups)]
    ppermute x1, starting transfers between devices: 4.74 us -> 3.74 us  [shards(): from_b = lax.ppermute(to_b, 'gy', high + [(j, i) for i, j in high])]
    pallas_call x6 -> x7, Pallas kernels: 12.2 us -> 11.4 us  [call(): pl.pallas_call(kernel, out_shape=outs, in_specs=[VMEM] * len(args), out_s...]
  transfers between devices with their start and end apart: 6 -> 6, of which waited for: 4 -> 3; matrix products, arithmetic and copies ran while one was open for 0% -> 0% of each run, Pallas kernels for 13% -> 19%
where the time goes in v4:
time: 54.8 us; the launch traced here: 54.4 us
  starting transfers between devices  37.4 us (68%)
  Pallas kernels  13.5 us (25%)
  waiting for transfers between devices  3.36 us (6%)
    all_to_all x1, starting transfers between devices, shards(): rows = lax.all_to_all(packets, ('gx', 'gy'), 0, 0, axis_index_groups=groups)  21 us
    pallas_call x7, Pallas kernels, call(): pl.pallas_call(kernel, out_shape=outs, in_specs=[VMEM] * len(args), out_s...  11.4 us
    all_to_all x1, starting transfers between devices, shards(): wrapped = lax.all_to_all(moved, 'gy', 0, 0)  7.77 us
    ppermute x1, starting transfers between devices, shards(): from_b = lax.ppermute(to_b, 'gy', high + [(j, i) for i, j in high])  3.74 us
    ppermute x1, starting transfers between devices, shards(): from_a = lax.ppermute(to_a, 'gy', low + [(j, i) for i, j in low])  2.27 us
    pallas_call x1, Pallas kernels, shards(): pl.pallas_call(packet_kernel, out_shape=f32(2 * count_y, 8, NJ), in_specs...  2.05 us
    all_to_all x1, waiting for transfers between devices, shards(): rows = lax.all_to_all(packets, ('gx', 'gy'), 0, 0, axis_index_groups=groups)  1.55 us
    ppermute x1, starting transfers between devices, shards(): west = lax.ppermute(to_east, 'gx', east_pairs)  1.29 us
  transfers between devices with their start and end apart: 6, of which 3 were waited for; matrix products, arithmetic and copies ran while one was open for 0% of the time, Pallas kernels for 19%

profile of v4, /device:TPU:1, one launch (start us, length us, event | category | flops | bytes accessed | tf_op | source)
XLA Modules:
  0.0 54.4 jit_solution(13849902675849483144)
XLA Ops:
  0.0 0.0 copy-start
  0.0 2.0 %packets.1 = f32[64,8,128]{2,1,0:T(8,128)} custom-call(f32[5,16,16,128]{3,2,1,0:T(8,128)} %fields.8, f32[16,16,128]{2,1,0:T(8,128)} %diff.8, s32[16,128]{1,0:T(8,128)} %heights.8), custom_call_target="tpu_custom_call" | custom-call | tf_op jit(solution)/shard_map/packets/pallas_call | solution.py:444
  2.1 0.0 copy-start.1
  2.1 0.0 copy-start.2
  2.1 21.0 %all-to-all-start = ((f32[64,8,128]{2,1,0:T(8,128)}), f32[64,8,128]{2,1,0:T(8,128)S(1)}, u32[]{:S(2)}, u32[]{:S(2)}) async-start(f32[64,8,128]{2,1,0:T(8,128)} %packets.1), calls=%async_computation | async-start | bytes 524288 | tf_op jit(solution)/shard_map/all_to_all | solution.py:460
  23.1 0.0 copy-done
  23.1 0.0 copy-done.1
  23.1 0.0 copy-done.2
  23.1 0.0 copy-start.3
  23.2 0.7 %pack.1 = (f32[2,1664]{1,0:T(2,128)S(1)}, f32[2,1664]{1,0:T(2,128)S(1)}) custom-call(f32[5,16,16,128]{3,2,1,0:T(8,128)S(1)} %copy-done, f32[16,16,128]{2,1,0:T(8,128)S(1)} %copy-done.1, s32[16,128]{1,0:T(8,128)S(1)} %copy-done.2), custom_call_target="tpu_custom_call" | custom-call | tf_op jit(solution)/shard_map/pack/pallas_call | solution.py:37
  23.9 2.3 %collective-permute-start = (f32[2,1664]{1,0:T(2,128)S(1)}, f32[2,1664]{1,0:T(2,128)S(1)}, u32[]{:S(2)}, u32[]{:S(2)}) collective-permute-start(f32[2,1664]{1,0:T(2,128)S(1)} %get-tuple-element.23), channel_id=1, source_target_pairs={{0,1},{2,3},{4,5},{6,7},{8,9},{10,11},{12,13},{14,15},{16,17},{18,... | collective-permute-start | bytes 39944 | tf_op jit(solution)/shard_map/ppermute | solution.py:467
  26.2 3.7 %collective-permute-start.1 = (f32[2,1664]{1,0:T(2,128)S(1)}, f32[2,1664]{1,0:T(2,128)S(1)}, u32[]{:S(2)}, u32[]{:S(2)}) collective-permute-start(f32[2,1664]{1,0:T(2,128)S(1)} %get-tuple-element.27), channel_id=1, source_target_pairs={{1,2},{3,4},{5,6},{7,8},{9,10},{11,12},{13,14},{15,16},{17,18},{19... | collective-permute-start | bytes 39944 | tf_op jit(solution)/shard_map/ppermute | solution.py:466
  29.9 0.0 copy-done.3
  30.0 0.0 collective-permute-done.from_a
  30.0 1.5 %all-to-all-done.rows = f32[64,8,128]{2,1,0:T(8,128)S(1)} async-done(((f32[64,8,128]{2,1,0:T(8,128)}), f32[64,8,128]{2,1,0:T(8,128)S(1)}, u32[]{:S(2)}, u32[]{:S(2)}) %all-to-all-start) | async-done | bytes 262176 | tf_op jit(solution)/shard_map/all_to_all | solution.py:460
  31.5 3.0 %permute.1 = f32[32,8,128]{2,1,0:T(8,128)} custom-call(f32[64,8,128]{2,1,0:T(8,128)S(1)} %all-to-all-done.rows, s32[32,128]{1,0:T(8,128)S(1)} %bitcast.2, s32[32,128]{1,0:T(8,128)S(1)} %inverse.1), custom_call_target="tpu_custom_call" | custom-call | tf_op jit(solution)/shard_map/permute/pallas_call | solution.py:37
  34.5 0.0 collective-permute-done.1.from_b
  34.5 7.8 %all-to-all-start.1 = ((f32[32,8,128]{2,1,0:T(8,128)}), f32[32,8,128]{2,1,0:T(8,128)S(1)}, u32[]{:S(2)}, u32[]{:S(2)}) async-start(f32[32,8,128]{2,1,0:T(8,128)} %permute.1), calls=%async_computation.1 | async-start | bytes 262144 | tf_op jit(solution)/shard_map/all_to_all | solution.py:479
  42.3 1.5 %unpack.1 = (f32[97,16,128]{2,1,0:T(8,128)S(1)}, f32[208,128]{1,0:T(8,128)S(1)}, f32[208,128]{1,0:T(8,128)S(1)}) custom-call(f32[2,1664]{1,0:T(2,128)S(1)} %collective-permute-done.from_a, f32[2,1664]{1,0:T(2,128)S(1)} %collective-permute-done.1.from_b, f32[5,16,16,128]{3,2,1,0:T(8,128)S(1)} %copy-done, f32[16,16,128]{2,1,0:T(8,128)S(1)} %copy-done.1, ...), custom_call_target="tpu_custom_call" | custom-call | tf_op jit(solution)/shard_map/unpack/pallas_call | solution.py:37
  43.8 1.3 %collective-permute-start.2 = (f32[208,128]{1,0:T(8,128)S(1)}, f32[208,128]{1,0:T(8,128)S(1)}, u32[]{:S(2)}, u32[]{:S(2)}) collective-permute-start(f32[208,128]{1,0:T(8,128)S(1)} %get-tuple-element.32), channel_id=1, source_target_pairs={{0,32},{32,64},{64,96},{96,128},{128,160},{160,192},{192,224},{256... | collective-permute-start | bytes 319496 | tf_op jit(solution)/shard_map/ppermute | solution.py:487
  45.1 1.3 %collective-permute-start.3 = (f32[208,128]{1,0:T(8,128)S(1)}, f32[208,128]{1,0:T(8,128)S(1)}, u32[]{:S(2)}, u32[]{:S(2)}) collective-permute-start(f32[208,128]{1,0:T(8,128)S(1)} %get-tuple-element.33), channel_id=1, source_target_pairs={{32,0},{64,32},{96,64},{128,96},{160,128},{192,160},{224,192},{288... | collective-permute-start | bytes 319496 | tf_op jit(solution)/shard_map/ppermute | solution.py:488
  46.4 4.4 %sections.1 = (f32[5,16,16,128]{3,2,1,0:T(8,128)S(1)}, f32[2,5,5,16,128]{4,3,2,1,0:T(8,128)S(1)}) custom-call(f32[5,16,16,128]{3,2,1,0:T(8,128)S(1)} %copy-done, f32[16,16,128]{2,1,0:T(8,128)S(1)} %copy-done.1, s32[16,128]{1,0:T(8,128)S(1)} %copy-done.2, f32[97,16,128]{2,1,0:T(8,128)S(1)} %get-tuple-element.29.halo), custom_call_target="tpu_custom_call" | custom-call | tf_op jit(solution)/shard_map/sections/pallas_call | solution.py:37
  50.8 0.0 collective-permute-done.2.west
  50.8 0.5 %collective-permute-done.3.east = f32[208,128]{1,0:T(8,128)S(1)} collective-permute-done((f32[208,128]{1,0:T(8,128)S(1)}, f32[208,128]{1,0:T(8,128)S(1)}, u32[]{:S(2)}, u32[]{:S(2)}) %collective-permute-start.3) | collective-permute-done | bytes 106528 | tf_op jit(solution)/shard_map/ppermute | solution.py:488
  51.3 0.5 edges.1.done
  51.8 1.3 %all-to-all-done.1.wrapped = f32[32,8,128]{2,1,0:T(8,128)S(1)} async-done(((f32[32,8,128]{2,1,0:T(8,128)}), f32[32,8,128]{2,1,0:T(8,128)S(1)}, u32[]{:S(2)}, u32[]{:S(2)}) %all-to-all-start.1) | async-done | bytes 131104 | tf_op jit(solution)/shard_map/all_to_all | solution.py:479
  53.1 1.3 %wrapped_rows.1 = f32[5,16,16,128]{3,2,1,0:T(8,128)} custom-call(f32[5,16,16,128]{3,2,1,0:T(8,128)S(1)} %copy-done, f32[16,16,128]{2,1,0:T(8,128)S(1)} %copy-done.1, s32[16,128]{1,0:T(8,128)S(1)} %copy-done.2, f32[97,16,128]{2,1,0:T(8,128)S(1)} %get-tuple-element.29.halo, f32[2,5,5,16,128]{4,3,2,1,0:T(8,128)S(1)} %get-tuple-element.30.kept, ...), custom_call_target="tpu_custom_call" | custom-call | tf_op jit(solution)/shard_map/wrapped_rows/pallas_call | solution.py:37
  (1 shorter events, 0.0 us)
Async XLA Ops:
  0.0 23.1 %copy-start = (f32[5,16,16,128]{3,2,1,0:T(8,128)S(1)}, f32[5,16,16,128]{3,2,1,0:T(8,128)}, u32[]{:S(2)}) copy-start(f32[5,16,16,128]{3,2,1,0:T(8,128)} %fields.8) | copy-start | bytes 1966084
  2.1 21.1 %copy-start.1 = (f32[16,16,128]{2,1,0:T(8,128)S(1)}, f32[16,16,128]{2,1,0:T(8,128)}, u32[]{:S(2)}) copy-start(f32[16,16,128]{2,1,0:T(8,128)} %diff.8) | copy-start | bytes 393220
  2.1 21.1 %copy-start.2 = (s32[16,128]{1,0:T(8,128)S(1)}, s32[16,128]{1,0:T(8,128)}, u32[]{:S(2)}) copy-start(s32[16,128]{1,0:T(8,128)} %heights.8) | copy-start | bytes 24580
  2.1 29.4 %all-to-all-start = ((f32[64,8,128]{2,1,0:T(8,128)}), f32[64,8,128]{2,1,0:T(8,128)S(1)}, u32[]{:S(2)}, u32[]{:S(2)}) async-start(f32[64,8,128]{2,1,0:T(8,128)} %packets.1), calls=%async_computation | async-start | bytes 524288 | tf_op jit(solution)/shard_map/all_to_all | solution.py:460
  23.1 6.8 %copy-start.3 = (s32[4096]{0:T(1024)S(1)}, s32[4096]{0:T(1024)}, u32[]{:S(2)}) copy-start(s32[4096]{0:T(1024)} %param.7) | copy-start | bytes 49156
  23.9 6.1 %collective-permute-start = (f32[2,1664]{1,0:T(2,128)S(1)}, f32[2,1664]{1,0:T(2,128)S(1)}, u32[]{:S(2)}, u32[]{:S(2)}) collective-permute-start(f32[2,1664]{1,0:T(2,128)S(1)} %get-tuple-element.23), channel_id=1, source_target_pairs={{0,1},{2,3},{4,5},{6,7},{8,9},{10,11},{12,13},{14,15},{16,17},{18,... | collective-permute-start | bytes 39944 | tf_op jit(solution)/shard_map/ppermute | solution.py:467
  26.2 8.3 %collective-permute-start.1 = (f32[2,1664]{1,0:T(2,128)S(1)}, f32[2,1664]{1,0:T(2,128)S(1)}, u32[]{:S(2)}, u32[]{:S(2)}) collective-permute-start(f32[2,1664]{1,0:T(2,128)S(1)} %get-tuple-element.27), channel_id=1, source_target_pairs={{1,2},{3,4},{5,6},{7,8},{9,10},{11,12},{13,14},{15,16},{17,18},{19... | collective-permute-start | bytes 39944 | tf_op jit(solution)/shard_map/ppermute | solution.py:466
  34.5 18.5 %all-to-all-start.1 = ((f32[32,8,128]{2,1,0:T(8,128)}), f32[32,8,128]{2,1,0:T(8,128)S(1)}, u32[]{:S(2)}, u32[]{:S(2)}) async-start(f32[32,8,128]{2,1,0:T(8,128)} %permute.1), calls=%async_computation.1 | async-start | bytes 262144 | tf_op jit(solution)/shard_map/all_to_all | solution.py:479
  43.8 7.0 %collective-permute-start.2 = (f32[208,128]{1,0:T(8,128)S(1)}, f32[208,128]{1,0:T(8,128)S(1)}, u32[]{:S(2)}, u32[]{:S(2)}) collective-permute-start(f32[208,128]{1,0:T(8,128)S(1)} %get-tuple-element.32), channel_id=1, source_target_pairs={{0,32},{32,64},{64,96},{96,128},{128,160},{160,192},{192,224},{256... | collective-permute-start | bytes 319496 | tf_op jit(solution)/shard_map/ppermute | solution.py:487
  45.1 6.2 %collective-permute-start.3 = (f32[208,128]{1,0:T(8,128)S(1)}, f32[208,128]{1,0:T(8,128)S(1)}, u32[]{:S(2)}, u32[]{:S(2)}) collective-permute-start(f32[208,128]{1,0:T(8,128)S(1)} %get-tuple-element.33), channel_id=1, source_target_pairs={{32,0},{64,32},{96,64},{128,96},{160,128},{192,160},{224,192},{288... | collective-permute-start | bytes 319496 | tf_op jit(solution)/shard_map/ppermute | solution.py:488

commit v5 on v4

--- a/solution.py
+++ b/solution.py
@@ -23,7 +23,7 @@
 HEIGHT_AT = BLOCK
 HALO = RIM + 1
 
-LEAD = 16
+LEAD = 20
 
 VMEM = pl.BlockSpec(memory_space=pltpu.VMEM)
 EXACT = lax.Precision.HIGHEST
@@ -64,6 +64,18 @@
     return lax.rem(lax.axis_index("gx"), half) == half - 1
 
 
+def spread_out(cols):
+    part_a = cols.astype(jnp.bfloat16).astype(jnp.float32)
+    rest = cols - part_a
+    part_b = rest.astype(jnp.bfloat16).astype(jnp.float32)
+    parts = jnp.concatenate([part_a, part_b, rest - part_b, jnp.zeros_like(cols)], 0)
+    hot = jnp.concatenate([picks()] * 4, 0)
+    return lax.dot_general(
+        parts.astype(jnp.bfloat16), hot.astype(jnp.bfloat16), (((0,), (0,)), ((), ())),
+        preferred_element_type=jnp.float32,
+    )
+
+
 def pack_kernel(fields, diff, heights, to_a, to_b):
     even = lax.rem(lax.axis_index("gy"), 2) == 0
     rows = jnp.concatenate(
@@ -88,9 +100,7 @@
     a, b = from_a[...], from_b[...]
     north, south = jnp.where(even, a, b), jnp.where(even, b, a)
     cols = jnp.concatenate([north, south, jnp.zeros((4, PACK), jnp.float32)], 0)
-    spread = lax.dot_general(
-        cols, picks(), (((0,), (0,)), ((), ())), precision=EXACT, preferred_element_type=jnp.float32
-    )
+    spread = spread_out(cols)
     halo[...] = spread[0:HALO * NI, :].reshape(HALO, NI, NJ)
     spare = jnp.zeros((NJ - RIM, NJ), jnp.float32)
     for to, near, far in ((to_east, NI - 1, NI - 2), (to_west, 0, 1)):
@@ -197,7 +207,7 @@
     target = jnp.where(first, wrap[...], inverse[...])
     column = iota(target.shape, 0) * NJ + iota(target.shape, 1)
     target = jnp.where((gx == half) | (gx == half - 1), column, target)
-    upper = lax.axis_index("gy") < LEAD
+    upper = lax.rem(lax.axis_index("gy") + 32 - LEAD, 32) >= NZ
     x = rows[pl.ds(jnp.where(first, 0, 32), 32)]
     x = jnp.concatenate([x[32 - LEAD:], x[:32 - LEAD]], 0)
     lane, sub = iota(x.shape, 2), iota(x.shape, 1)
@@ -246,7 +256,7 @@
         corner = pltpu.roll(corner, 7 - r, 1)
         last = jnp.where((lane == r) | (lane == NJ - 1 - r), corner, last)
     y = jnp.where(sub == 7, last, y)
-    out[...] = y
+    out[...] = jnp.concatenate([y[LEAD:], y[:LEAD]], 0)
 
 
 def beside(m, h):
@@ -322,7 +332,7 @@
             one_halo[m, k] = halos[m][0] + TIME_STEP / 3.0 * rates_h[m]
         return 0
 
-    lax.fori_loop(0, NZ, section_one, 0)
+    lax.fori_loop(0, NZ, section_one, 0, unroll=4)
 
     def section_two(k, _):
         up, dn = jnp.minimum(k + 1, NZ - 1), jnp.maximum(k - 1, 0)
@@ -342,7 +352,7 @@
             out[m, k] = fields[m, k] + TIME_STEP / 2.0 * rates[m]
         return 0
 
-    lax.fori_loop(0, NZ, section_two, 0)
+    lax.fori_loop(0, NZ, section_two, 0, unroll=4)
     for m in range(NF):
         for r in range(3):
             kept[0, m, r] = one[m, :, r, :]
@@ -399,10 +409,7 @@
         def _(side=side, rim=rim, sign=sign):
             outer, far, height = split_rim(rim)
             rates = row_rates(outer, far, height, sign)
-            corner = lax.dot_general(
-                rim[EDGE_ROWS:MESSAGE, :], picks(), (((0,), (0,)), ((), ())),
-                precision=EXACT, preferred_element_type=jnp.float32,
-            )
+            corner = spread_out(rim[EDGE_ROWS:MESSAGE, :])
             corner = [corner[i * NZ:(i + 1) * NZ, :] for i in range(NA)]
             sides = [beside(outer[i], corner[i]) for i in range(NA)]
             k_cell, k_n, k_s = outer[NF], sides[NF][0], sides[NF][1]
@@ -417,13 +424,13 @@
 def wrap_kernel(fields, diff, heights, halo, kept, wrapped, done, out):
     out[...] = done[...]
     lane = iota((NZ, NJ), 1)
-    place = {0: (LEAD, 0), 1: (LEAD, 1), 2: (LEAD, 2), NF: (LEAD, 3), 3: (0, 0), 4: (0, 1)}
+    place = {0: (0, 0), 1: (0, 1), 2: (0, 2), NF: (0, 3), 3: (NZ, 0), 4: (NZ, 1)}
     for side, mine in ((0, is_first()), (1, is_last())):
         @pl.when(mine)
         def _(side=side):
             rates, outer, corner = [], [], []
             for m in range(NF):
-                half, row = (LEAD, 4 + m) if m < 3 else (0, 1 + m)
+                half, row = (0, 4 + m) if m < 3 else (NZ, 1 + m)
                 rates.append(wrapped[half:half + NZ, row, :])
             for i in range(NA):
                 half, row = place[i]
@@ -453,10 +460,10 @@
 
     half_x = count_x // 2
     row_pairs = [(0, last), (half_x, half_x - 1)] + [(i, i + half_x) for i in range(1, half_x - 1)]
-    def line(*rows):
-        return [r * count_y + (i + LEAD) % count_y for r in rows for i in range(count_y)]
-
-    groups = [line(b, a) for a, b in row_pairs]
+    def line(lead, *rows):
+        return [r * count_y + (i + lead) % count_y for r in rows for i in range(count_y)]
+
+    groups = [line(LEAD, b, a) for a, b in row_pairs]
     rows = lax.all_to_all(packets, ("gx", "gy"), 0, 0, axis_index_groups=groups)
 
     low = [(i, i + 1) for i in range(0, count_y, 2)]
@@ -476,7 +483,8 @@
         scratch=[pltpu.VMEM((384, 32 * NJ), jnp.bfloat16), pltpu.VMEM((256, 32 * NJ), jnp.bfloat16)],
     )
     moved, from_b = lax.optimization_barrier((moved, from_b))
-    wrapped = lax.all_to_all(moved, "gy", 0, 0)
+    groups = [line(LEAD, r) for r in range(count_x)]
+    wrapped = lax.all_to_all(moved, ("gx", "gy"), 0, 0, axis_index_groups=groups)
 
     message = f32(MESSAGE, NJ)
     halo, to_east, to_west = call(

time: 54.8 us -> 53.3 us (0.973)
  Pallas kernels: 13.5 us -> 11.3 us
  waiting for transfers between devices: 3.36 us -> 4.41 us
    pallas_call x7, Pallas kernels: 11.4 us -> 9.29 us  [call(): pl.pallas_call(kernel, out_shape=outs, in_specs=[VMEM] * len(args), out_s...]
    all_to_all x1, waiting for transfers between devices: 1.26 us -> 0.01 us  [shards(): lax.all_to_all(moved, ('gx', 'gy'), 0, 0, axis_index_groups=groups)]
    ppermute x1, waiting for transfers between devices: 0.55 us -> 1.8 us  [shards(): east = lax.ppermute(to_west, 'gx', [(j, i) for i, j in east_pairs])]
    all_to_all x1, waiting for transfers between devices: 1.55 us -> 2.6 us  [shards(): rows = lax.all_to_all(packets, ('gx', 'gy'), 0, 0, axis_index_groups=groups)]
  transfers between devices with their start and end apart: 6 -> 6, of which waited for: 3 -> 2; matrix products, arithmetic and copies ran while one was open for 0% -> 0% of each run, Pallas kernels for 19% -> 15%
where the time goes in v5:
time: 53.3 us; the launch traced here: 53 us
  starting transfers between devices  37 us (69%)
  Pallas kernels  11.3 us (21%)
  waiting for transfers between devices  4.41 us (8%)
    all_to_all x1, starting transfers between devices, shards(): rows = lax.all_to_all(packets, ('gx', 'gy'), 0, 0, axis_index_groups=groups)  20.7 us
    pallas_call x7, Pallas kernels, call(): pl.pallas_call(kernel, out_shape=outs, in_specs=[VMEM] * len(args), out_s...  9.29 us
    all_to_all x1, starting transfers between devices, shards(): lax.all_to_all(moved, ('gx', 'gy'), 0, 0, axis_index_groups=groups)  7.77 us
    ppermute x1, starting transfers between devices, shards(): from_b = lax.ppermute(to_b, 'gy', high + [(j, i) for i, j in high])  3.74 us
    all_to_all x1, waiting for transfers between devices, shards(): rows = lax.all_to_all(packets, ('gx', 'gy'), 0, 0, axis_index_groups=groups)  2.6 us
    ppermute x1, starting transfers between devices, shards(): from_a = lax.ppermute(to_a, 'gy', low + [(j, i) for i, j in low])  2.27 us
    pallas_call x1, Pallas kernels, shards(): pl.pallas_call(packet_kernel, out_shape=f32(2 * count_y, 8, NJ), in_specs...  2.05 us
    ppermute x1, waiting for transfers between devices, shards(): east = lax.ppermute(to_west, 'gx', [(j, i) for i, j in east_pairs])  1.8 us
  transfers between devices with their start and end apart: 6, of which 2 were waited for; matrix products, arithmetic and copies ran while one was open for 0% of the time, Pallas kernels for 15%

profile of v5, /device:TPU:1, one launch (start us, length us, event | category | flops | bytes accessed | tf_op | source)
XLA Modules:
  0.0 53.0 jit_solution(7393238995213108466)
XLA Ops:
  0.0 0.0 copy-start
  0.0 2.0 %packets.1 = f32[64,8,128]{2,1,0:T(8,128)} custom-call(f32[5,16,16,128]{3,2,1,0:T(8,128)} %fields.8, f32[16,16,128]{2,1,0:T(8,128)} %diff.8, s32[16,128]{1,0:T(8,128)} %heights.8), custom_call_target="tpu_custom_call" | custom-call | tf_op jit(solution)/shard_map/packets/pallas_call | solution.py:451
  2.1 0.0 copy-start.1
  2.1 0.0 copy-start.2
  2.1 20.7 %all-to-all-start = ((f32[64,8,128]{2,1,0:T(8,128)}), f32[64,8,128]{2,1,0:T(8,128)S(1)}, u32[]{:S(2)}, u32[]{:S(2)}) async-start(f32[64,8,128]{2,1,0:T(8,128)} %packets.1), calls=%async_computation | async-start | bytes 524288 | tf_op jit(solution)/shard_map/all_to_all | solution.py:467
  22.7 0.0 copy-done
  22.8 0.0 copy-done.1
  22.8 0.0 copy-done.2
  22.8 0.0 copy-start.3
  22.8 0.7 %pack.1 = (f32[2,1664]{1,0:T(2,128)S(1)}, f32[2,1664]{1,0:T(2,128)S(1)}) custom-call(f32[5,16,16,128]{3,2,1,0:T(8,128)S(1)} %copy-done, f32[16,16,128]{2,1,0:T(8,128)S(1)} %copy-done.1, s32[16,128]{1,0:T(8,128)S(1)} %copy-done.2), custom_call_target="tpu_custom_call" | custom-call | tf_op jit(solution)/shard_map/pack/pallas_call | solution.py:37
  23.5 2.3 %collective-permute-start = (f32[2,1664]{1,0:T(2,128)S(1)}, f32[2,1664]{1,0:T(2,128)S(1)}, u32[]{:S(2)}, u32[]{:S(2)}) collective-permute-start(f32[2,1664]{1,0:T(2,128)S(1)} %get-tuple-element.23), channel_id=1, source_target_pairs={{0,1},{2,3},{4,5},{6,7},{8,9},{10,11},{12,13},{14,15},{16,17},{18,... | collective-permute-start | bytes 39944 | tf_op jit(solution)/shard_map/ppermute | solution.py:474
  25.8 3.7 %collective-permute-start.1 = (f32[2,1664]{1,0:T(2,128)S(1)}, f32[2,1664]{1,0:T(2,128)S(1)}, u32[]{:S(2)}, u32[]{:S(2)}) collective-permute-start(f32[2,1664]{1,0:T(2,128)S(1)} %get-tuple-element.27), channel_id=1, source_target_pairs={{1,2},{3,4},{5,6},{7,8},{9,10},{11,12},{13,14},{15,16},{17,18},{19... | collective-permute-start | bytes 39944 | tf_op jit(solution)/shard_map/ppermute | solution.py:473
  29.6 0.0 copy-done.3
  29.6 0.0 collective-permute-done.from_a
  29.6 2.6 %all-to-all-done.rows = f32[64,8,128]{2,1,0:T(8,128)S(1)} async-done(((f32[64,8,128]{2,1,0:T(8,128)}), f32[64,8,128]{2,1,0:T(8,128)S(1)}, u32[]{:S(2)}, u32[]{:S(2)}) %all-to-all-start) | async-done | bytes 262176 | tf_op jit(solution)/shard_map/all_to_all | solution.py:467
  32.2 3.0 %permute.1 = f32[32,8,128]{2,1,0:T(8,128)} custom-call(f32[64,8,128]{2,1,0:T(8,128)S(1)} %all-to-all-done.rows, s32[32,128]{1,0:T(8,128)S(1)} %bitcast.2, s32[32,128]{1,0:T(8,128)S(1)} %inverse.1), custom_call_target="tpu_custom_call" | custom-call | tf_op jit(solution)/shard_map/permute/pallas_call | solution.py:37
  35.2 0.0 collective-permute-done.1.from_b
  35.2 7.8 %all-to-all-start.1 = ((f32[32,8,128]{2,1,0:T(8,128)}), f32[32,8,128]{2,1,0:T(8,128)S(1)}, u32[]{:S(2)}, u32[]{:S(2)}) async-start(f32[32,8,128]{2,1,0:T(8,128)} %permute.1), calls=%async_computation.1 | async-start | bytes 262144 | tf_op jit(solution)/shard_map/all_to_all | solution.py:487
  43.0 0.8 %unpack.1 = (f32[97,16,128]{2,1,0:T(8,128)S(1)}, f32[208,128]{1,0:T(8,128)S(1)}, f32[208,128]{1,0:T(8,128)S(1)}) custom-call(f32[2,1664]{1,0:T(2,128)S(1)} %collective-permute-done.from_a, f32[2,1664]{1,0:T(2,128)S(1)} %collective-permute-done.1.from_b, f32[5,16,16,128]{3,2,1,0:T(8,128)S(1)} %copy-done, f32[16,16,128]{2,1,0:T(8,128)S(1)} %copy-done.1, ...), custom_call_target="tpu_custom_call" | custom-call | tf_op jit(solution)/shard_map/unpack/pallas_call | solution.py:37
  43.8 1.3 %collective-permute-start.2 = (f32[208,128]{1,0:T(8,128)S(1)}, f32[208,128]{1,0:T(8,128)S(1)}, u32[]{:S(2)}, u32[]{:S(2)}) collective-permute-start(f32[208,128]{1,0:T(8,128)S(1)} %get-tuple-element.32), channel_id=1, source_target_pairs={{0,32},{32,64},{64,96},{96,128},{128,160},{160,192},{192,224},{256... | collective-permute-start | bytes 319496 | tf_op jit(solution)/shard_map/ppermute | solution.py:495
  45.1 1.3 %collective-permute-start.3 = (f32[208,128]{1,0:T(8,128)S(1)}, f32[208,128]{1,0:T(8,128)S(1)}, u32[]{:S(2)}, u32[]{:S(2)}) collective-permute-start(f32[208,128]{1,0:T(8,128)S(1)} %get-tuple-element.33), channel_id=1, source_target_pairs={{32,0},{64,32},{96,64},{128,96},{160,128},{192,160},{224,192},{288... | collective-permute-start | bytes 319496 | tf_op jit(solution)/shard_map/ppermute | solution.py:496
  46.4 3.0 %sections.1 = (f32[5,16,16,128]{3,2,1,0:T(8,128)S(1)}, f32[2,5,5,16,128]{4,3,2,1,0:T(8,128)S(1)}) custom-call(f32[5,16,16,128]{3,2,1,0:T(8,128)S(1)} %copy-done, f32[16,16,128]{2,1,0:T(8,128)S(1)} %copy-done.1, s32[16,128]{1,0:T(8,128)S(1)} %copy-done.2, f32[97,16,128]{2,1,0:T(8,128)S(1)} %get-tuple-element.29.halo), custom_call_target="tpu_custom_call" | custom-call | tf_op jit(solution)/shard_map/sections/pallas_call | solution.py:37
  49.4 0.0 collective-permute-done.2.west
  49.4 1.8 %collective-permute-done.3.east = f32[208,128]{1,0:T(8,128)S(1)} collective-permute-done((f32[208,128]{1,0:T(8,128)S(1)}, f32[208,128]{1,0:T(8,128)S(1)}, u32[]{:S(2)}, u32[]{:S(2)}) %collective-permute-start.3) | collective-permute-done | bytes 106528 | tf_op jit(solution)/shard_map/ppermute | solution.py:496
  51.2 0.4 edges.1.done
  51.6 0.0 all-to-all-done.1.wrapped
  51.6 1.3 %wrapped_rows.1 = f32[5,16,16,128]{3,2,1,0:T(8,128)} custom-call(f32[5,16,16,128]{3,2,1,0:T(8,128)S(1)} %copy-done, f32[16,16,128]{2,1,0:T(8,128)S(1)} %copy-done.1, s32[16,128]{1,0:T(8,128)S(1)} %copy-done.2, f32[97,16,128]{2,1,0:T(8,128)S(1)} %get-tuple-element.29.halo, f32[2,5,5,16,128]{4,3,2,1,0:T(8,128)S(1)} %get-tuple-element.30.kept, ...), custom_call_target="tpu_custom_call" | custom-call | tf_op jit(solution)/shard_map/wrapped_rows/pallas_call | solution.py:37
  (1 shorter events, 0.0 us)
Async XLA Ops:
  0.0 22.7 %copy-start = (f32[5,16,16,128]{3,2,1,0:T(8,128)S(1)}, f32[5,16,16,128]{3,2,1,0:T(8,128)}, u32[]{:S(2)}) copy-start(f32[5,16,16,128]{3,2,1,0:T(8,128)} %fields.8) | copy-start | bytes 1966084
  2.1 20.7 %copy-start.1 = (f32[16,16,128]{2,1,0:T(8,128)S(1)}, f32[16,16,128]{2,1,0:T(8,128)}, u32[]{:S(2)}) copy-start(f32[16,16,128]{2,1,0:T(8,128)} %diff.8) | copy-start | bytes 393220
  2.1 20.7 %copy-start.2 = (s32[16,128]{1,0:T(8,128)S(1)}, s32[16,128]{1,0:T(8,128)}, u32[]{:S(2)}) copy-start(s32[16,128]{1,0:T(8,128)} %heights.8) | copy-start | bytes 24580
  2.1 30.1 %all-to-all-start = ((f32[64,8,128]{2,1,0:T(8,128)}), f32[64,8,128]{2,1,0:T(8,128)S(1)}, u32[]{:S(2)}, u32[]{:S(2)}) async-start(f32[64,8,128]{2,1,0:T(8,128)} %packets.1), calls=%async_computation | async-start | bytes 524288 | tf_op jit(solution)/shard_map/all_to_all | solution.py:467
  22.8 6.8 %copy-start.3 = (s32[4096]{0:T(1024)S(1)}, s32[4096]{0:T(1024)}, u32[]{:S(2)}) copy-start(s32[4096]{0:T(1024)} %param.7) | copy-start | bytes 49156
  23.5 6.1 %collective-permute-start = (f32[2,1664]{1,0:T(2,128)S(1)}, f32[2,1664]{1,0:T(2,128)S(1)}, u32[]{:S(2)}, u32[]{:S(2)}) collective-permute-start(f32[2,1664]{1,0:T(2,128)S(1)} %get-tuple-element.23), channel_id=1, source_target_pairs={{0,1},{2,3},{4,5},{6,7},{8,9},{10,11},{12,13},{14,15},{16,17},{18,... | collective-permute-start | bytes 39944 | tf_op jit(solution)/shard_map/ppermute | solution.py:474
  25.8 9.4 %collective-permute-start.1 = (f32[2,1664]{1,0:T(2,128)S(1)}, f32[2,1664]{1,0:T(2,128)S(1)}, u32[]{:S(2)}, u32[]{:S(2)}) collective-permute-start(f32[2,1664]{1,0:T(2,128)S(1)} %get-tuple-element.27), channel_id=1, source_target_pairs={{1,2},{3,4},{5,6},{7,8},{9,10},{11,12},{13,14},{15,16},{17,18},{19... | collective-permute-start | bytes 39944 | tf_op jit(solution)/shard_map/ppermute | solution.py:473
  35.2 16.4 %all-to-all-start.1 = ((f32[32,8,128]{2,1,0:T(8,128)}), f32[32,8,128]{2,1,0:T(8,128)S(1)}, u32[]{:S(2)}, u32[]{:S(2)}) async-start(f32[32,8,128]{2,1,0:T(8,128)} %permute.1), calls=%async_computation.1 | async-start | bytes 262144 | tf_op jit(solution)/shard_map/all_to_all | solution.py:487
  43.8 5.6 %collective-permute-start.2 = (f32[208,128]{1,0:T(8,128)S(1)}, f32[208,128]{1,0:T(8,128)S(1)}, u32[]{:S(2)}, u32[]{:S(2)}) collective-permute-start(f32[208,128]{1,0:T(8,128)S(1)} %get-tuple-element.32), channel_id=1, source_target_pairs={{0,32},{32,64},{64,96},{96,128},{128,160},{160,192},{192,224},{256... | collective-permute-start | bytes 319496 | tf_op jit(solution)/shard_map/ppermute | solution.py:495
  45.1 6.1 %collective-permute-start.3 = (f32[208,128]{1,0:T(8,128)S(1)}, f32[208,128]{1,0:T(8,128)S(1)}, u32[]{:S(2)}, u32[]{:S(2)}) collective-permute-start(f32[208,128]{1,0:T(8,128)S(1)} %get-tuple-element.33), channel_id=1, source_target_pairs={{32,0},{64,32},{96,64},{128,96},{160,128},{192,160},{224,192},{288... | collective-permute-start | bytes 319496 | tf_op jit(solution)/shard_map/ppermute | solution.py:496

commit v6 on v5

--- a/solution.py
+++ b/solution.py
@@ -501,10 +501,10 @@
         *block, halo, name="sections", scratch=[state, state],
     )
     done = call(
+        wrap_kernel, f32(NF, NZ, NI, NJ), *block, halo, kept, wrapped, done, name="wrapped_rows"
+    )
+    return call(
         edges_kernel, f32(NF, NZ, NI, NJ), *block, halo, kept, west, east, done, name="edges"
-    )
-    return call(
-        wrap_kernel, f32(NF, NZ, NI, NJ), *block, halo, kept, wrapped, done, name="wrapped_rows"
     )
 
 

time: 53.3 us -> 52.8 us (level)
    ppermute x1, waiting for transfers between devices: 1.8 us -> 0.41 us  [shards(): east = lax.ppermute(to_west, 'gx', [(j, i) for i, j in east_pairs])]
    all_to_all x1, waiting for transfers between devices: 0.01 us -> 0.89 us  [shards(): lax.all_to_all(moved, ('gx', 'gy'), 0, 0, axis_index_groups=groups)]
  transfers between devices with their start and end apart: 6 -> 6, of which waited for: 2 -> 3; matrix products, arithmetic and copies ran while one was open for 0% -> 0% of each run, Pallas kernels for 15% -> 15%
where the time goes in v6:
time: 52.8 us; the launch traced here: 52.5 us
  starting transfers between devices  37 us (70%)
  Pallas kernels  11.3 us (21%)
  waiting for transfers between devices  3.91 us (7%)
    all_to_all x1, starting transfers between devices, shards(): rows = lax.all_to_all(packets, ('gx', 'gy'), 0, 0, axis_index_groups=groups)  20.7 us
    pallas_call x7, Pallas kernels, call(): pl.pallas_call(kernel, out_shape=outs, in_specs=[VMEM] * len(args), out_s...  9.29 us
    all_to_all x1, starting transfers between devices, shards(): lax.all_to_all(moved, ('gx', 'gy'), 0, 0, axis_index_groups=groups)  7.77 us
    ppermute x1, starting transfers between devices, shards(): from_b = lax.ppermute(to_b, 'gy', high + [(j, i) for i, j in high])  3.74 us
    all_to_all x1, waiting for transfers between devices, shards(): rows = lax.all_to_all(packets, ('gx', 'gy'), 0, 0, axis_index_groups=groups)  2.6 us
    ppermute x1, starting transfers between devices, shards(): from_a = lax.ppermute(to_a, 'gy', low + [(j, i) for i, j in low])  2.27 us
    pallas_call x1, Pallas kernels, shards(): pl.pallas_call(packet_kernel, out_shape=f32(2 * count_y, 8, NJ), in_specs...  2.05 us
    ppermute x1, starting transfers between devices, shards(): west = lax.ppermute(to_east, 'gx', east_pairs)  1.29 us
  transfers between devices with their start and end apart: 6, of which 3 were waited for; matrix products, arithmetic and copies ran while one was open for 0% of the time, Pallas kernels for 15%

profile of v6, /device:TPU:1, one launch (start us, length us, event | category | flops | bytes accessed | tf_op | source)
XLA Modules:
  0.0 52.5 jit_solution(4284862533182793666)
XLA Ops:
  0.0 0.0 copy-start
  0.0 2.0 %packets.1 = f32[64,8,128]{2,1,0:T(8,128)} custom-call(f32[5,16,16,128]{3,2,1,0:T(8,128)} %fields.8, f32[16,16,128]{2,1,0:T(8,128)} %diff.8, s32[16,128]{1,0:T(8,128)} %heights.8), custom_call_target="tpu_custom_call" | custom-call | tf_op jit(solution)/shard_map/packets/pallas_call | solution.py:451
  2.1 0.0 copy-start.1
  2.1 0.0 copy-start.2
  2.1 20.7 %all-to-all-start = ((f32[64,8,128]{2,1,0:T(8,128)}), f32[64,8,128]{2,1,0:T(8,128)S(1)}, u32[]{:S(2)}, u32[]{:S(2)}) async-start(f32[64,8,128]{2,1,0:T(8,128)} %packets.1), calls=%async_computation | async-start | bytes 524288 | tf_op jit(solution)/shard_map/all_to_all | solution.py:467
  22.7 0.0 copy-done
  22.8 0.0 copy-done.1
  22.8 0.0 copy-done.2
  22.8 0.0 copy-start.3
  22.8 0.7 %pack.1 = (f32[2,1664]{1,0:T(2,128)S(1)}, f32[2,1664]{1,0:T(2,128)S(1)}) custom-call(f32[5,16,16,128]{3,2,1,0:T(8,128)S(1)} %copy-done, f32[16,16,128]{2,1,0:T(8,128)S(1)} %copy-done.1, s32[16,128]{1,0:T(8,128)S(1)} %copy-done.2), custom_call_target="tpu_custom_call" | custom-call | tf_op jit(solution)/shard_map/pack/pallas_call | solution.py:37
  23.5 2.3 %collective-permute-start = (f32[2,1664]{1,0:T(2,128)S(1)}, f32[2,1664]{1,0:T(2,128)S(1)}, u32[]{:S(2)}, u32[]{:S(2)}) collective-permute-start(f32[2,1664]{1,0:T(2,128)S(1)} %get-tuple-element.23), channel_id=1, source_target_pairs={{0,1},{2,3},{4,5},{6,7},{8,9},{10,11},{12,13},{14,15},{16,17},{18,... | collective-permute-start | bytes 39944 | tf_op jit(solution)/shard_map/ppermute | solution.py:474
  25.8 3.7 %collective-permute-start.1 = (f32[2,1664]{1,0:T(2,128)S(1)}, f32[2,1664]{1,0:T(2,128)S(1)}, u32[]{:S(2)}, u32[]{:S(2)}) collective-permute-start(f32[2,1664]{1,0:T(2,128)S(1)} %get-tuple-element.27), channel_id=1, source_target_pairs={{1,2},{3,4},{5,6},{7,8},{9,10},{11,12},{13,14},{15,16},{17,18},{19... | collective-permute-start | bytes 39944 | tf_op jit(solution)/shard_map/ppermute | solution.py:473
  29.6 0.0 copy-done.3
  29.6 0.0 collective-permute-done.from_a
  29.6 2.6 %all-to-all-done.rows = f32[64,8,128]{2,1,0:T(8,128)S(1)} async-done(((f32[64,8,128]{2,1,0:T(8,128)}), f32[64,8,128]{2,1,0:T(8,128)S(1)}, u32[]{:S(2)}, u32[]{:S(2)}) %all-to-all-start) | async-done | bytes 262176 | tf_op jit(solution)/shard_map/all_to_all | solution.py:467
  32.2 3.0 %permute.1 = f32[32,8,128]{2,1,0:T(8,128)} custom-call(f32[64,8,128]{2,1,0:T(8,128)S(1)} %all-to-all-done.rows, s32[32,128]{1,0:T(8,128)S(1)} %bitcast.2, s32[32,128]{1,0:T(8,128)S(1)} %inverse.1), custom_call_target="tpu_custom_call" | custom-call | tf_op jit(solution)/shard_map/permute/pallas_call | solution.py:37
  35.2 0.0 collective-permute-done.1.from_b
  35.2 7.8 %all-to-all-start.1 = ((f32[32,8,128]{2,1,0:T(8,128)}), f32[32,8,128]{2,1,0:T(8,128)S(1)}, u32[]{:S(2)}, u32[]{:S(2)}) async-start(f32[32,8,128]{2,1,0:T(8,128)} %permute.1), calls=%async_computation.1 | async-start | bytes 262144 | tf_op jit(solution)/shard_map/all_to_all | solution.py:487
  43.0 0.8 %unpack.1 = (f32[97,16,128]{2,1,0:T(8,128)S(1)}, f32[208,128]{1,0:T(8,128)S(1)}, f32[208,128]{1,0:T(8,128)S(1)}) custom-call(f32[2,1664]{1,0:T(2,128)S(1)} %collective-permute-done.from_a, f32[2,1664]{1,0:T(2,128)S(1)} %collective-permute-done.1.from_b, f32[5,16,16,128]{3,2,1,0:T(8,128)S(1)} %copy-done, f32[16,16,128]{2,1,0:T(8,128)S(1)} %copy-done.1, ...), custom_call_target="tpu_custom_call" | custom-call | tf_op jit(solution)/shard_map/unpack/pallas_call | solution.py:37
  43.8 1.3 %collective-permute-start.2 = (f32[208,128]{1,0:T(8,128)S(1)}, f32[208,128]{1,0:T(8,128)S(1)}, u32[]{:S(2)}, u32[]{:S(2)}) collective-permute-start(f32[208,128]{1,0:T(8,128)S(1)} %get-tuple-element.31), channel_id=1, source_target_pairs={{0,32},{32,64},{64,96},{96,128},{128,160},{160,192},{192,224},{256... | collective-permute-start | bytes 319496 | tf_op jit(solution)/shard_map/ppermute | solution.py:495
  45.1 1.3 %collective-permute-start.3 = (f32[208,128]{1,0:T(8,128)S(1)}, f32[208,128]{1,0:T(8,128)S(1)}, u32[]{:S(2)}, u32[]{:S(2)}) collective-permute-start(f32[208,128]{1,0:T(8,128)S(1)} %get-tuple-element.32), channel_id=1, source_target_pairs={{32,0},{64,32},{96,64},{128,96},{160,128},{192,160},{224,192},{288... | collective-permute-start | bytes 319496 | tf_op jit(solution)/shard_map/ppermute | solution.py:496
  46.4 3.0 %sections.1 = (f32[5,16,16,128]{3,2,1,0:T(8,128)S(1)}, f32[2,5,5,16,128]{4,3,2,1,0:T(8,128)S(1)}) custom-call(f32[5,16,16,128]{3,2,1,0:T(8,128)S(1)} %copy-done, f32[16,16,128]{2,1,0:T(8,128)S(1)} %copy-done.1, s32[16,128]{1,0:T(8,128)S(1)} %copy-done.2, f32[97,16,128]{2,1,0:T(8,128)S(1)} %get-tuple-element.29.halo), custom_call_target="tpu_custom_call" | custom-call | tf_op jit(solution)/shard_map/sections/pallas_call | solution.py:37
  49.4 0.9 %all-to-all-done.1.wrapped = f32[32,8,128]{2,1,0:T(8,128)S(1)} async-done(((f32[32,8,128]{2,1,0:T(8,128)}), f32[32,8,128]{2,1,0:T(8,128)S(1)}, u32[]{:S(2)}, u32[]{:S(2)}) %all-to-all-start.1) | async-done | bytes 131104 | tf_op jit(solution)/shard_map/all_to_all | solution.py:487
  50.3 0.5 wrapped_rows.1.done
  50.8 0.0 collective-permute-done.2.west
  50.8 0.4 collective-permute-done.3.east
  51.2 1.3 %edges.1 = f32[5,16,16,128]{3,2,1,0:T(8,128)} custom-call(f32[5,16,16,128]{3,2,1,0:T(8,128)S(1)} %copy-done, f32[16,16,128]{2,1,0:T(8,128)S(1)} %copy-done.1, s32[16,128]{1,0:T(8,128)S(1)} %copy-done.2, f32[97,16,128]{2,1,0:T(8,128)S(1)} %get-tuple-element.29.halo, f32[2,5,5,16,128]{4,3,2,1,0:T(8,128)S(1)} %get-tuple-element.30.kept, ...), custom_call_target="tpu_custom_call" | custom-call | tf_op jit(solution)/shard_map/edges/pallas_call | solution.py:37
  (1 shorter events, 0.0 us)
Async XLA Ops:
  0.0 22.7 %copy-start = (f32[5,16,16,128]{3,2,1,0:T(8,128)S(1)}, f32[5,16,16,128]{3,2,1,0:T(8,128)}, u32[]{:S(2)}) copy-start(f32[5,16,16,128]{3,2,1,0:T(8,128)} %fields.8) | copy-start | bytes 1966084
  2.1 20.7 %copy-start.1 = (f32[16,16,128]{2,1,0:T(8,128)S(1)}, f32[16,16,128]{2,1,0:T(8,128)}, u32[]{:S(2)}) copy-start(f32[16,16,128]{2,1,0:T(8,128)} %diff.8) | copy-start | bytes 393220
  2.1 20.7 %copy-start.2 = (s32[16,128]{1,0:T(8,128)S(1)}, s32[16,128]{1,0:T(8,128)}, u32[]{:S(2)}) copy-start(s32[16,128]{1,0:T(8,128)} %heights.8) | copy-start | bytes 24580
  2.1 30.1 %all-to-all-start = ((f32[64,8,128]{2,1,0:T(8,128)}), f32[64,8,128]{2,1,0:T(8,128)S(1)}, u32[]{:S(2)}, u32[]{:S(2)}) async-start(f32[64,8,128]{2,1,0:T(8,128)} %packets.1), calls=%async_computation | async-start | bytes 524288 | tf_op jit(solution)/shard_map/all_to_all | solution.py:467
  22.8 6.8 %copy-start.3 = (s32[4096]{0:T(1024)S(1)}, s32[4096]{0:T(1024)}, u32[]{:S(2)}) copy-start(s32[4096]{0:T(1024)} %param.7) | copy-start | bytes 49156
  23.5 6.1 %collective-permute-start = (f32[2,1664]{1,0:T(2,128)S(1)}, f32[2,1664]{1,0:T(2,128)S(1)}, u32[]{:S(2)}, u32[]{:S(2)}) collective-permute-start(f32[2,1664]{1,0:T(2,128)S(1)} %get-tuple-element.23), channel_id=1, source_target_pairs={{0,1},{2,3},{4,5},{6,7},{8,9},{10,11},{12,13},{14,15},{16,17},{18,... | collective-permute-start | bytes 39944 | tf_op jit(solution)/shard_map/ppermute | solution.py:474
  25.8 9.4 %collective-permute-start.1 = (f32[2,1664]{1,0:T(2,128)S(1)}, f32[2,1664]{1,0:T(2,128)S(1)}, u32[]{:S(2)}, u32[]{:S(2)}) collective-permute-start(f32[2,1664]{1,0:T(2,128)S(1)} %get-tuple-element.27), channel_id=1, source_target_pairs={{1,2},{3,4},{5,6},{7,8},{9,10},{11,12},{13,14},{15,16},{17,18},{19... | collective-permute-start | bytes 39944 | tf_op jit(solution)/shard_map/ppermute | solution.py:473
  35.2 15.1 %all-to-all-start.1 = ((f32[32,8,128]{2,1,0:T(8,128)}), f32[32,8,128]{2,1,0:T(8,128)S(1)}, u32[]{:S(2)}, u32[]{:S(2)}) async-start(f32[32,8,128]{2,1,0:T(8,128)} %permute.1), calls=%async_computation.1 | async-start | bytes 262144 | tf_op jit(solution)/shard_map/all_to_all | solution.py:487
  43.8 7.0 %collective-permute-start.2 = (f32[208,128]{1,0:T(8,128)S(1)}, f32[208,128]{1,0:T(8,128)S(1)}, u32[]{:S(2)}, u32[]{:S(2)}) collective-permute-start(f32[208,128]{1,0:T(8,128)S(1)} %get-tuple-element.31), channel_id=1, source_target_pairs={{0,32},{32,64},{64,96},{96,128},{128,160},{160,192},{192,224},{256... | collective-permute-start | bytes 319496 | tf_op jit(solution)/shard_map/ppermute | solution.py:495
  45.1 6.1 %collective-permute-start.3 = (f32[208,128]{1,0:T(8,128)S(1)}, f32[208,128]{1,0:T(8,128)S(1)}, u32[]{:S(2)}, u32[]{:S(2)}) collective-permute-start(f32[208,128]{1,0:T(8,128)S(1)} %get-tuple-element.32), channel_id=1, source_target_pairs={{32,0},{64,32},{96,64},{128,96},{160,128},{192,160},{224,192},{288... | collective-permute-start | bytes 319496 | tf_op jit(solution)/shard_map/ppermute | solution.py:496
